TPU v7x, 32 devices: a whole 2x2x4 slice. The times are simulated.
32 devices in a mesh: ckpt: 2 (over x), tok: 16 (over z, y, core).
Axes of the slice: x: 2, y: 2, z: 4, core: 2. Of those that a mesh axis runs over, the one named last changes fastest.
Arguments:
- features: bfloat16 [2, 2048, 1792], P('ckpt', 'tok'), may hold values from -22 to 22
- pairing: int32 [2, 16, 128], P('ckpt', 'tok'), may hold values from 0 to 127, each once within a row
- rotation: bfloat16 [2, 1792, 1792], P('ckpt', 'tok'), may hold values from -1 to 2
Outputs:
- consensus: bfloat16 [2048, 1792], P('tok')
- rotation_next: bfloat16 [2, 1792, 1792], P('ckpt', 'tok')
Inputs may be any that keep to these rules, and one draw needn't show every extreme that they name: Each row of a shard of 128 rows appears once in that shard's pairing.
All inputs are finite; a program needn't handle non-finite values.
Results may differ from a plain program's by a relative error of at most 0.011.
Values may be sent and summed in bfloat16 or wider, within the bound.
No kernel may reach another device: no remote copies, remote signals or barrier semaphores. Data moves between devices by JAX's collectives and lax.ppermute only.
A program may use at most 64 MiB of HBM per device.

v0:
```python
import math

import jax
import jax.numpy as jnp
from jax import lax
from jax.sharding import PartitionSpec as P


def apply_once(vector, whole):
    inner = lax.dot_general(
        vector.astype(jnp.bfloat16),
        whole,
        (((1,), (1,)), ((), ())),
        preferred_element_type=jnp.float32,
    ).astype(jnp.bfloat16)
    return jnp.dot(inner, whole, preferred_element_type=jnp.float32)


def normalize(own_cov, feature_width):
    squares = lax.psum(jnp.sum(own_cov * own_cov), "tok")
    return (own_cov / (2.0 * jnp.sqrt(squares / feature_width + 1e-06))).astype(jnp.bfloat16)


def block_form(aligned, consensus, devices, column_groups, send_fn, collect_fn):
    row_count, feature_width = aligned.shape
    row_groups = devices // column_groups
    row_width = feature_width // row_groups
    col_width = feature_width // column_groups
    aligned_cols = jnp.repeat(
        aligned.reshape(row_count, row_groups, row_width).transpose(1, 0, 2), column_groups, axis=0
    ).reshape(devices * row_count, row_width)
    consensus_cols = jnp.tile(
        consensus.reshape(row_count, column_groups, col_width).transpose(1, 0, 2),
        (row_groups, 1, 1),
    ).reshape(devices * row_count, col_width)
    aligned_all, consensus_all = send_fn(aligned_cols, consensus_cols)
    own_cov = lax.dot_general(
        aligned_all, consensus_all, (((0,), (0,)), ((), ())), preferred_element_type=jnp.float32
    )
    start_block = normalize(own_cov, feature_width)
    pieces = collect_fn(start_block)
    return (
        pieces.reshape(row_groups, column_groups, row_width, col_width)
        .transpose(0, 2, 1, 3)
        .reshape(feature_width, feature_width)
    )


def shards(features, pairing, rotation):
    own_rows = features[0]
    own_order = pairing[0, 0]
    rot_rows = rotation[0]
    feature_width = own_rows.shape[1]
    aligned = jnp.take(own_rows, own_order, axis=0)
    rotated = jnp.dot(
        aligned,
        lax.all_gather(rot_rows, "tok", axis=0, tiled=True),
        preferred_element_type=jnp.float32,
    ).astype(jnp.bfloat16)
    summed = lax.psum(rotated.astype(jnp.float32).astype(jnp.bfloat16), "ckpt").astype(jnp.float32)
    consensus = (summed / lax.axis_size("ckpt")).astype(jnp.bfloat16)
    devices = lax.axis_size("tok")
    slab_rows = feature_width // devices

    def send_narrow(left, right):
        return (
            lax.all_to_all(left, "tok", split_axis=0, concat_axis=0, tiled=True),
            lax.all_to_all(right, "tok", split_axis=0, concat_axis=0, tiled=True),
        )

    def collect_narrow(block):
        return lax.all_gather(block, "tok", axis=0, tiled=True)

    whole = block_form(aligned, consensus, devices, min(devices, 8), send_narrow, collect_narrow)
    start_rows = lax.dynamic_slice_in_dim(whole, lax.axis_index("tok") * slab_rows, slab_rows, 0)
    first = 1.5 * start_rows.astype(jnp.float32) - 0.5 * apply_once(start_rows, whole)
    upper = 1.5 * first - 0.5 * apply_once(first, whole)
    middle = apply_once(upper, whole)
    cubic = 1.5 * middle - 0.5 * apply_once(middle, whole)
    rotation_next = (math.sqrt(feature_width) * (1.5 * first - 0.5 * cubic)).astype(jnp.bfloat16)
    return (consensus, rotation_next[None])


def solution(mesh):
    placed = (P("ckpt", "tok", None), P("ckpt", "tok", None), P("ckpt", "tok", None))
    return jax.shard_map(
        shards,
        mesh=mesh,
        in_specs=placed,
        out_specs=(P("tok", None), P("ckpt", "tok", None)),
        check_vma=False,
    )
```

profile of v0, /device:TPU:0, one launch (start us, length us, event | category | flops | bytes accessed | tf_op | source)
XLA Modules:
  0.0 366.0 jit_solution(12044244964260322321)
XLA Ops:
  7.2 0.0 copy-start
  7.2 0.0 all-gather.6.cloned.1.call-start
  7.2 0.7 all-gather.6.cloned.1.call-update
  7.9 0.7 fusion.23
  8.6 0.0 copy-done
  8.6 0.9 gather_fusion
  9.5 0.1 gather.7
  9.6 0.7 compare_and_fusion
  10.3 0.5 fusion.16
  10.8 0.1 copy.8
  10.9 2.5 broadcast_in_dim.24
  13.3 7.4 %all-to-all-start = ((bf16[16,128,896]{2,1,0:T(8,128)(2,1)}), bf16[16,128,896]{2,1,0:T(8,128)(2,1)}, u32[]{:S(2)}, u32[]{:S(2)}) async-start(bf16[16,128,896]{2,1,0:T(8,128)(2,1)} %bitcast.54), calls=%async_computation | async-start | bytes 7340032 | tf_op jit(solution)/shard_map/all_to_all | solution.py:67
  20.8 0.0 all-reduce.2.cloned.1.call-start
  20.8 108.3 %all-gather.6.cloned.1.call-done = bf16[1,1792,1792]{2,1,0:T(8,128)(2,1)} async-done(((bf16[1,112,1792]{2,1,0:T(8,128)(2,1)}), bf16[1,1792,1792]{2,1,0:T(8,128)(2,1)}) %all-gather.6.cloned.1.call-update) | async-done | bytes 6422544 | tf_op jit(solution)/shard_map/all_gather | solution.py:57
  129.2 4.7 %fusion.6 = bf16[128,1792]{1,0:T(8,128)(2,1)} fusion(bf16[1,1792,1792]{2,1,0:T(8,128)(2,1)} %all-gather.6.cloned.1.call-done, bf16[128,1792]{1,0:T(8,128)(2,1)S(1)} %gather_fusion, pred[128]{0:T(512)(128)(4,1)S(1)} %compare_and_fusion), kind=kOutput, calls=%fused_computation.10 | convolution fusion | flops 822542336 | bytes 7340160 | tf_op jit(solution)/shard_map/dot_general | solution.py:55
  133.8 0.0 all-reduce.2.cloned.1.call-update
  133.8 0.0 all-gather.4.cloned.1.call-start
  133.9 29.6 %all-reduce.2.cloned.1.call-done = bf16[128,1792]{1,0:T(8,128)(2,1)} async-done(((bf16[128,1792]{1,0:T(8,128)(2,1)}), bf16[128,1792]{1,0:T(8,128)(2,1)}) %all-reduce.2.cloned.1.call-update) | async-done | bytes 458768 | tf_op jit(solution)/shard_map/psum | solution.py:60
  163.5 1.1 multiply_convert_fusion
  164.6 0.0 copy-start.2
  164.6 0.3 copy.9
  164.8 0.0 all-to-all-done
  164.8 0.1 tile.8
  165.0 28.0 %all_to_all.15 = bf16[16,128,224]{1,2,0:T(8,128)(2,1)S(1)} all-to-all(bf16[16,128,224]{1,2,0:T(8,128)(2,1)S(1)} %bitcast.56), channel_id=1, replica_groups=mesh['ckpt'=2,'tok'=16] {'tok'}, dimensions={0} | all-to-all | bytes 1835008 | tf_op jit(solution)/shard_map/all_to_all | solution.py:68
  192.9 3.8 %multiply_reduce_fusion = (f32[]{:T(128)}, f32[896,224]{0,1:T(8,128)S(1)}) fusion(bf16[16,128,224]{1,2,0:T(8,128)(2,1)S(1)} %all_to_all.15, bf16[16,128,896]{2,1,0:T(8,128)(2,1)} %all-to-all-done), kind=kOutput, calls=%fused_computation.24 | convolution fusion | flops 822484992 | bytes 5390340 | tf_op jit(solution)/shard_map/dot_general | solution.py:37
  196.8 33.3 %psum.15 = f32[]{:T(128)} all-reduce(f32[]{:T(128)} %get-tuple-element.2), channel_id=1, replica_groups=mesh['ckpt'=2,'tok'=16] {'tok'}, use_global_device_ids=true, to_apply=%region_2.3 | all-reduce | flops 1 | bytes 8 | tf_op jit(solution)/shard_map/psum | solution.py:20
  230.7 0.8 divide_convert_fusion
  231.5 0.0 all-gather.4.cloned.1.call-update
  231.6 59.0 %all-gather.4.cloned.1.call-done = bf16[14336,224]{0,1:T(8,128)(2,1)} async-done(((bf16[896,224]{0,1:T(8,128)(2,1)}), bf16[14336,224]{0,1:T(8,128)(2,1)}) %all-gather.4.cloned.1.call-update) | async-done | bytes 6422544 | tf_op jit(solution)/shard_map/all_gather | solution.py:72
  290.6 4.0 %copy.13 = bf16[28,8,16,896]{3,2,1,0:T(8,128)(2,1)S(1)} copy(bf16[28,8,16,896]{3,1,2,0:T(8,128)(2,1)} %bitcast.55) | data formatting | bytes 12845056
  294.6 0.0 copy-done.2
  294.6 29.7 %copy.10 = bf16[2,8,896,224]{2,0,3,1:T(2,128)(2,1)S(1)} copy(bf16[2,8,896,224]{2,1,0,3:T(8,128)(2,1)S(1)} %bitcast.52) | data formatting | bytes 12845056 | tf_op jit(solution)/shard_map/reshape | solution.py:43
  324.4 1.2 copy.14
  325.6 0.0 copy-start.1
  325.6 2.7 copy-done.1
  328.3 0.2 constant_dynamic-slice_fusion
  328.5 0.2 copy.12
  328.7 7.7 %fusion.2 = f32[112,1792]{1,0:T(8,128)S(1)} fusion(bf16[1792,1792]{0,1:T(8,128)(2,1)} %bitcast.48, bf16[112,1792]{1,0:T(8,128)(2,1)S(1)} %copy.12, bf16[112,1792]{0,1:T(8,128)(2,1)S(1)} %constant_dynamic-slice_fusion), kind=kOutput, calls=%fused_computation.6 | convolution fusion | flops 1439649792 | bytes 8028160 | tf_op jit(solution)/shard_map/dot_general | solution.py:16
  336.4 7.4 %fusion.12 = bf16[112,1792]{1,0:T(8,128)(2,1)S(1)} fusion(bf16[1792,1792]{0,1:T(8,128)(2,1)} %bitcast.49, f32[112,1792]{1,0:T(8,128)S(1)} %fusion.2), kind=kOutput, calls=%fused_computation.14 | convolution fusion | flops 1439850496 | bytes 7626752 | tf_op jit(solution)/shard_map/dot_general | solution.py:16
  343.8 7.5 %fusion.14 = f32[112,1792]{1,0:T(8,128)S(1)} fusion(bf16[1792,1792]{0,1:T(8,128)(2,1)} %bitcast.50, bf16[112,1792]{1,0:T(8,128)(2,1)S(1)} %fusion.12), kind=kOutput, calls=%fused_computation.25 | convolution fusion | flops 1438846976 | bytes 7626752 | tf_op jit(solution)/shard_map/dot_general | solution.py:16
  351.3 8.2 %fusion.13 = bf16[1,112,1792]{2,1,0:T(8,128)(2,1)} fusion(bf16[1792,1792]{0,1:T(8,128)(2,1)} %bitcast.51, f32[112,1792]{1,0:T(8,128)S(1)} %fusion.14, f32[112,1792]{1,0:T(8,128)S(1)} %fusion.2), kind=kOutput, calls=%fused_computation.19 | convolution fusion | flops 1440653312 | bytes 8429568 | tf_op jit(solution)/shard_map/dot_general | solution.py:16
  (1 shorter events, 0.0 us)
Async XLA Ops:
  7.2 1.4 copy-start
  7.2 122.0 %all-gather.6.cloned.1.call-start = ((), (), s32[]{:S(2)}) async-start(), calls=%async_computation.4 | async-start | bytes 6823936 | tf_op jit(solution)/shard_map/all_gather | solution.py:57
  13.3 151.5 %all-to-all-start = ((bf16[16,128,896]{2,1,0:T(8,128)(2,1)}), bf16[16,128,896]{2,1,0:T(8,128)(2,1)}, u32[]{:S(2)}, u32[]{:S(2)}) async-start(bf16[16,128,896]{2,1,0:T(8,128)(2,1)} %bitcast.54), calls=%async_computation | async-start | bytes 7340032 | tf_op jit(solution)/shard_map/all_to_all | solution.py:67
  20.8 142.7 %all-reduce.2.cloned.1.call-start = ((), (), s32[]{:S(2)}) async-start(), calls=%async_computation.2 | async-start | bytes 917504 | tf_op jit(solution)/shard_map/psum | solution.py:60
  133.8 156.7 %all-gather.4.cloned.1.call-start = ((), (), s32[]{:S(2)}) async-start(), calls=%async_computation.3 | async-start | bytes 6823936 | tf_op jit(solution)/shard_map/all_gather | solution.py:72
  164.6 130.0 %copy-start.2 = (bf16[128,1792]{1,0:T(8,128)(2,1)}, bf16[128,1792]{1,0:T(8,128)(2,1)S(1)}, u32[]{:S(2)}) copy-start(bf16[128,1792]{1,0:T(8,128)(2,1)S(1)} %multiply_convert_fusion) | copy-start | bytes 1376260
  325.6 2.7 copy-start.1
Sparse Core Ops, SparseCore 0:
  10.3 118.8 all-gather.5
  134.0 29.4 all-reduce.1
  231.7 58.8 all-gather.3
where the time goes:
time: 366 us
  waiting for transfers between devices  198 us (54%)
  blocking collectives  61.2 us (17%)
  local copies, waits for them, and re-layouts  42 us (11%)
  matrix products  39.2 us (11%)
  between operations  14.6 us (4%)
  starting transfers between devices  7.55 us (2%)
  other arithmetic  3.74 us (1%)
    all_gather x1, waiting for transfers between devices, shards(): lax.all_gather(rot_rows, 'tok', axis=0, tiled=True)  108 us
    all_gather x1, waiting for transfers between devices, collect_narrow(): return lax.all_gather(block, 'tok', axis=0, tiled=True)  59 us
    psum x1, blocking collectives, normalize(): squares = lax.psum(jnp.sum(own_cov * own_cov), 'tok')  33.3 us
    dot_general x4, matrix products, apply_once(): return jnp.dot(inner, whole, preferred_element_type=jnp.float32)  30.8 us
    reshape x1, local copies, waits for them, and re-layouts, block_form(): pieces.reshape(row_groups, column_groups, row_width, col_width)  29.7 us
    psum x1, waiting for transfers between devices, shards(): lax.psum(rotated.astype(jnp.float32).astype(jnp.bfloat16), 'ckpt')  29.6 us
    all_to_all x1, blocking collectives, send_narrow(): lax.all_to_all(right, 'tok', split_axis=0, concat_axis=0, tiled=True)  28 us
    unnamed x10, local copies, waits for them, and re-layouts  8.38 us
  transfers between devices with their start and end apart: 4, of which 3 were waited for; matrix products, arithmetic and copies ran while one was open for 3% of the time, Pallas kernels for 0%

commit v1 on v0

v1 whole, which is shorter than its diff:
```python
import functools
import math

import jax
import jax.numpy as jnp
from jax import lax
from jax.experimental import pallas as pl
from jax.experimental.pallas import tpu as pltpu
from jax.sharding import PartitionSpec as P

BF16 = jnp.bfloat16
F32 = jnp.float32
VMEM = pl.BlockSpec(memory_space=pltpu.VMEM)
SMEM = pl.BlockSpec(memory_space=pltpu.SMEM)
PARAMS = pltpu.CompilerParams(vmem_limit_bytes=56 * 2**20)


def shape(dims, dtype):
    return jax.ShapeDtypeStruct(dims, dtype)


def contract(left, right, left_dim, right_dim):
    return lax.dot_general(
        left, right, (((left_dim,), (right_dim,)), ((), ())), preferred_element_type=F32
    )


def call(kernel, outs, smem, vmem, scratch=(), flops=0, nbytes=0):
    return pl.pallas_call(
        kernel,
        out_shape=outs,
        in_specs=[SMEM] * len(smem) + [VMEM] * len(vmem),
        out_specs=jax.tree.map(lambda _: VMEM, outs),
        scratch_shapes=list(scratch),
        compiler_params=PARAMS,
        cost_estimate=pl.CostEstimate(flops=flops, bytes_accessed=nbytes, transcendentals=0),
    )(*smem, *vmem)


def chip_at(position, chips):
    half = chips // 2
    return jnp.where(position < half, 2 * position, 2 * (chips - 1 - position) + 1)


def ring_pairs(chips):
    order = list(range(0, chips, 2)) + list(range(chips - 1, 0, -2))
    steps = [(order[i], order[(i + 1) % chips]) for i in range(chips)]
    up = [(a * 2 + core, b * 2 + core) for a, b in steps for core in (0, 1)]
    down = [(b, a) for a, b in up]
    last = [(a * 2, b * 2) for a, b in steps] + [(b * 2 + 1, a * 2 + 1) for a, b in steps]
    return up, down, last


def ring_gather(block, core, chips):
    up, down, last = ring_pairs(chips)
    blocks, ahead, behind = [block], block, block
    for _ in range(chips // 2 - 1):
        ahead = lax.ppermute(ahead, "tok", up)
        behind = lax.ppermute(behind, "tok", down)
        blocks += [ahead, behind]
    blocks.append(lax.ppermute(jnp.where(core == 0, ahead, behind), "tok", last))
    return blocks


def ring_offsets(chips):
    near = [sign * step for step in range(1, chips // 2) for sign in (-1, 1)]
    return [0] + near + [chips // 2]


def align_kernel(order_ref, rows_ref, out_ref):
    count = rows_ref.shape[0]
    picks = lax.broadcasted_iota(jnp.int32, (count, count), 0) == order_ref[...]
    out_ref[...] = contract(picks.astype(BF16), rows_ref[...], 0, 0).astype(BF16)


def rotate_kernel(count, *refs):
    blocks, cols_ref, out_ref = refs[:count], refs[count], refs[count + 1]
    for i, block in enumerate(blocks):
        out_ref[i] = jnp.dot(block[...], cols_ref[...], preferred_element_type=F32).astype(BF16)


def cov_kernel(count, members, *refs):
    blocks, parts = refs[:count], refs[count : count + members]
    cons_ref, cov_ref, rows_ref, all_ref = refs[count + members :]
    size = blocks[0].shape[0]
    for i, block in enumerate(blocks):
        total = parts[0][i].astype(F32)
        for part in parts[1:]:
            total = total + part[i].astype(F32)
        consensus = (total / members).astype(BF16)
        cons_ref[i] = consensus
        rows_ref[i * size : (i + 1) * size, :] = block[...]
        all_ref[i * size : (i + 1) * size, :] = consensus
    cov_ref[...] = contract(all_ref[...], rows_ref[...], 0, 0)


def chain_kernel(count, slab, *refs):
    where_ref, blocks = refs[0], refs[1 : count + 1]
    out_ref, whole, turned = refs[count + 1 :]
    width = whole.shape[0]
    size = width // count
    squares = jnp.zeros((1, width), F32)
    for i, block in enumerate(blocks):
        values = block[...]
        whole[i * size : (i + 1) * size, :] = values
        values = values.astype(F32)
        squares = squares + jnp.sum(values * values, axis=0, keepdims=True)
    inverse = 1.0 / (2.0 * jnp.sqrt(jnp.sum(squares, axis=1, keepdims=True) / width + 1e-06))

    rows = turned.shape[1]
    span = min(rows + 128, width)
    first_row = where_ref[count] * slab
    window = jnp.minimum(first_row // 128, (width - span) // 128) * 128
    window = pl.multiple_of(window, 128)
    columns = whole[:, pl.ds(window, span)]
    picks = lax.broadcasted_iota(jnp.int32, (rows, span), 1) == (
        lax.broadcasted_iota(jnp.int32, (rows, span), 0) + (first_row - window)
    )
    own = contract(picks.astype(BF16), columns, 1, 1)
    start = (own * inverse).astype(BF16)

    def apply_once(vector):
        inner = jnp.dot(vector.astype(BF16), whole[...], preferred_element_type=F32) * inverse
        return contract(inner.astype(BF16), whole[...], 1, 1) * inverse

    first = 1.5 * start.astype(F32) - 0.5 * apply_once(start)
    upper = 1.5 * first - 0.5 * apply_once(first)
    middle = apply_once(upper)
    cubic = 1.5 * middle - 0.5 * apply_once(middle)
    result = math.sqrt(width) * (1.5 * first - 0.5 * cubic)
    if count == 1:
        out_ref[...] = result[:slab].astype(BF16)
        return
    result = result.T
    for i in range(count):
        row = pl.multiple_of(where_ref[i] * size, 16)
        turned[pl.ds(row, size), :] = result[i * size : (i + 1) * size, :]
    out_ref[...] = turned[...].T[:slab].astype(BF16)


def shards(features, pairing, rotation):
    own_rows, own_order, rot_rows = features[0], pairing[0], rotation[0]
    count, width = own_rows.shape
    devices, members = lax.axis_size("tok"), lax.axis_size("ckpt")
    chips = devices // 2
    slab, cols = width // devices, width // chips
    index = lax.axis_index("tok")
    chip, core = index // 2, index % 2
    position = jnp.where(chip % 2 == 0, chip // 2, chips - 1 - chip // 2)
    siblings = [(i, i ^ 1) for i in range(devices)]
    parity = [[2 * i + c for i in range(chips)] for c in (0, 1)]
    pairs = [[2 * i, 2 * i + 1] for i in range(chips)]

    aligned = call(
        align_kernel, shape((count, width), BF16), [], [own_order, own_rows]
    )
    blocks = ring_gather(aligned, core, chips)

    rot_pieces = rot_rows.reshape(slab, chips, cols).transpose(1, 0, 2)
    rot_pieces = lax.all_to_all(
        rot_pieces, "tok", split_axis=0, concat_axis=0, tiled=True, axis_index_groups=parity
    )
    rot_cols = lax.all_gather(rot_pieces, "tok", axis=1, axis_index_groups=pairs).reshape(width, cols)

    rotated = call(
        functools.partial(rotate_kernel, chips),
        shape((chips, count, cols), BF16),
        [],
        blocks + [rot_cols],
        flops=2 * chips * count * cols * width,
        nbytes=2 * chips * count * width,
    )
    if members == 2:
        parts = [rotated, lax.ppermute(rotated, "ckpt", [(0, 1), (1, 0)])]
    else:
        gathered = lax.all_gather(rotated, "ckpt", axis=0)
        parts = [gathered[i] for i in range(members)]
    cons_blocks, cov = call(
        functools.partial(cov_kernel, chips, members),
        (shape((chips, count, cols), BF16), shape((cols, width), F32)),
        [],
        blocks + parts,
        [pltpu.VMEM((chips * count, width), BF16), pltpu.VMEM((chips * count, cols), BF16)],
        flops=2 * chips * count * cols * width,
        nbytes=2 * chips * count * width,
    )
    halves = cov.reshape(2, slab, width)
    keep = jnp.where(core == 0, halves[0], halves[1])
    give = jnp.where(core == 0, halves[1], halves[0]).astype(BF16)
    own = (keep + lax.ppermute(give, "tok", siblings).astype(F32)).astype(BF16)

    offsets = ring_offsets(chips)
    if slab % 16 == 0:
        same = ring_gather(own, core, chips)
        other = [lax.ppermute(block, "tok", siblings) for block in same]
        at = [chip_at((position + offset) % chips, chips) * 2 for offset in offsets]
        places = [a + core for a in at] + [a + 1 - core for a in at]
        gathered = same + other
    else:
        places = [jnp.zeros_like(index)]
        gathered = [lax.all_gather(own, "tok", axis=0, tiled=True)]
    rows = -(-slab // 128) * 128
    rotation_next = call(
        functools.partial(chain_kernel, len(gathered), slab),
        shape((slab, width), BF16),
        [jnp.stack(places + [index]).astype(jnp.int32)],
        gathered,
        [pltpu.VMEM((width, width), BF16), pltpu.VMEM((width, rows), F32)],
        flops=16 * rows * width * width,
        nbytes=2 * width * width,
    )

    natural = jnp.stack([chip_at((position + offset) % chips, chips) for offset in offsets])
    ordered = jnp.zeros_like(cons_blocks).at[natural].set(cons_blocks, unique_indices=True)
    consensus = lax.all_to_all(
        ordered, "tok", split_axis=0, concat_axis=0, tiled=True, axis_index_groups=parity
    )
    consensus = consensus.transpose(1, 0, 2).reshape(count, width)
    return (consensus, rotation_next[None])


def solution(mesh):
    placed = (P("ckpt", "tok", None), P("ckpt", "tok", None), P("ckpt", "tok", None))
    return jax.shard_map(
        shards,
        mesh=mesh,
        in_specs=placed,
        out_specs=(P("tok", None), P("ckpt", "tok", None)),
        check_vma=False,
    )
```

time: 366 us -> 151 us (0.41)
  waiting for transfers between devices: 198 us -> 71 us
  blocking collectives: 61.2 us -> 4.17 us
  matrix products: 39.2 us -> 0 us
  local copies, waits for them, and re-layouts: 42 us -> 11.1 us
  Pallas kernels: 0 us -> 27.6 us
  starting transfers between devices: 7.55 us -> 31.2 us
  between operations: 14.6 us -> 0.82 us
    all_gather x2 -> x0, waiting for transfers between devices: 167 us -> none  [the longest x1 108 us: shards(): lax.all_gather(rot_rows, 'tok', axis=0, tiled=True)]
    ppermute x0 -> x24, waiting for transfers between devices: none -> 62.8 us  [the longest x6 39.2 us: ring_gather(): behind = lax.ppermute(behind, 'tok', down)]
    dot_general x6 -> x0, matrix products: 39.2 us -> none  [the longest x4 30.8 us: apply_once(): return jnp.dot(inner, whole, preferred_element_type=jnp.float32)]
    psum x1 -> x0, blocking collectives: 33.3 us -> none  [normalize(): squares = lax.psum(jnp.sum(own_cov * own_cov), 'tok')]
    reshape x1 -> x0, local copies, waits for them, and re-layouts: 29.7 us -> none  [block_form(): pieces.reshape(row_groups, column_groups, row_width, col_width)]
    psum x1 -> x0, waiting for transfers between devices: 29.6 us -> none  [shards(): lax.psum(rotated.astype(jnp.float32).astype(jnp.bfloat16), 'ckpt')]
    all_to_all x1 -> x0, blocking collectives: 28 us -> none  [send_narrow(): lax.all_to_all(right, 'tok', split_axis=0, concat_axis=0, tiled=True)]
    pallas_call x0 -> x4, Pallas kernels: none -> 27.6 us  [call(): pl.pallas_call(kernel, out_shape=outs, in_specs=[SMEM] * len(smem) + [VME...]
  transfers between devices with their start and end apart: 4 -> 26, of which waited for: 3 -> 11; matrix products, arithmetic and copies ran while one was open for 3% -> 6% of each run, Pallas kernels for 0% -> 0%
where the time goes in v1:
time: 151 us; the launch traced here: 150 us
  waiting for transfers between devices  71 us (47%)
  starting transfers between devices  31.2 us (21%)
  Pallas kernels  27.6 us (18%)
  local copies, waits for them, and re-layouts  11.1 us (7%)
  blocking collectives  4.17 us (3%)
  other arithmetic  3.92 us (3%)
    ppermute x6, waiting for transfers between devices, ring_gather(): behind = lax.ppermute(behind, 'tok', down)  39.2 us
    pallas_call x4, Pallas kernels, call(): pl.pallas_call(kernel, out_shape=outs, in_specs=[SMEM] * len(smem) + [VME...  27.6 us
    ppermute x1, waiting for transfers between devices, shards(): parts = [rotated, lax.ppermute(rotated, 'ckpt', [(0, 1), (1, 0)])]  12.9 us
    all_to_all x1, waiting for transfers between devices, shards(): lax.all_to_all(rot_pieces, 'tok', split_axis=0, concat_axis=0, tiled=True...  8.2 us
    ppermute x6, starting transfers between devices, ring_gather(): behind = lax.ppermute(behind, 'tok', down)  7.68 us
    ppermute x2, waiting for transfers between devices, ring_gather(): lax.ppermute(jnp.where(core == 0, ahead, behind), 'tok', last)  7.01 us
    all_to_all x1, starting transfers between devices, shards(): lax.all_to_all(rot_pieces, 'tok', split_axis=0, concat_axis=0, tiled=True...  5.68 us
    ppermute x6, starting transfers between devices, ring_gather(): ahead = lax.ppermute(ahead, 'tok', up)  5.53 us
  transfers between devices with their start and end apart: 26, of which 11 were waited for; matrix products, arithmetic and copies ran while one was open for 6% of the time, Pallas kernels for 0%

profile of v1, /device:TPU:0, one launch (start us, length us, event | category | flops | bytes accessed | tf_op | source)
XLA Modules:
  0.0 149.8 jit_solution(15217699435702981163)
XLA Ops:
  0.6 2.1 %shard_map.50.refs_0_ = bf16[128,1792]{1,0:T(8,128)(2,1)} custom-call(s32[1,128]{1,0:T(1,128)} %bitcast.41, bf16[128,1792]{1,0:T(8,128)(2,1)} %bitcast.40), custom_call_target="tpu_custom_call" | custom-call | tf_op jit(solution)/shard_map/pallas_call | solution.py:29
  2.8 3.0 %collective-permute-start.1 = (bf16[128,1792]{1,0:T(8,128)(2,1)}, bf16[128,1792]{1,0:T(8,128)(2,1)S(1)}, u32[]{:S(2)}, u32[]{:S(2)}) collective-permute-start(bf16[128,1792]{1,0:T(8,128)(2,1)} %shard_map.50.refs_0_), channel_id=1, source_target_pairs={{4,0},{5,1},{8,4},{9,5},{12,8},{13,9},{14,12},{15,13},{10,14},{11,... | collective-permute-start | bytes 1376264 | tf_op jit(solution)/shard_map/ppermute | solution.py:59
  5.8 10.7 %collective-permute-done.1.refs_2_ = bf16[128,1792]{1,0:T(8,128)(2,1)S(1)} collective-permute-done((bf16[128,1792]{1,0:T(8,128)(2,1)}, bf16[128,1792]{1,0:T(8,128)(2,1)S(1)}, u32[]{:S(2)}, u32[]{:S(2)}) %collective-permute-start.1) | collective-permute-done | bytes 458784 | tf_op jit(solution)/shard_map/ppermute | solution.py:59
  16.5 1.7 %collective-permute-start.3 = (bf16[128,1792]{1,0:T(8,128)(2,1)S(1)}, bf16[128,1792]{1,0:T(8,128)(2,1)S(1)}, u32[]{:S(2)}, u32[]{:S(2)}) collective-permute-start(bf16[128,1792]{1,0:T(8,128)(2,1)S(1)} %collective-permute-done.1.refs_2_), channel_id=1, source_target_pairs={{4,0},{5,1},{8,4},{9,5},{12,8},{13,9},{14,12},{15,13},{10,14},{11,... | collective-permute-start | bytes 1376264 | tf_op jit(solution)/shard_map/ppermute | solution.py:59
  18.5 9.7 %collective-permute-done.3.refs_4_ = bf16[128,1792]{1,0:T(8,128)(2,1)S(1)} collective-permute-done((bf16[128,1792]{1,0:T(8,128)(2,1)S(1)}, bf16[128,1792]{1,0:T(8,128)(2,1)S(1)}, u32[]{:S(2)}, u32[]{:S(2)}) %collective-permute-start.3) | collective-permute-done | bytes 458784 | tf_op jit(solution)/shard_map/ppermute | solution.py:59
  28.2 1.4 collective-permute-start.5
  29.6 0.7 collective-permute-start.4
  30.2 1.7 %reshape_squeeze.3 = bf16[112,8,224]{2,1,0:T(8,128)(2,1)S(1)} reshape(bf16[1,112,1792]{2,1,0:T(8,128)(2,1)} %param.5) | data formatting | bytes 802816 | tf_op jit(solution)/shard_map/reshape;squeeze | solution.py:159
  31.9 0.9 copy.9
  32.8 5.7 %all-to-all-start = ((bf16[8,112,224]{2,1,0:T(8,128)(2,1)}), bf16[8,112,224]{2,1,0:T(8,128)(2,1)}, u32[]{:S(2)}, u32[]{:S(2)}) async-start(bf16[8,112,224]{2,1,0:T(8,128)(2,1)} %bitcast.36), calls=%async_computation | async-start | bytes 917504 | tf_op jit(solution)/shard_map/all_to_all | solution.py:160
  38.5 1.0 collective-permute-done.5.refs_6_
  39.5 1.0 collective-permute-done.4.refs_5_
  40.5 0.9 broadcast_select_fusion
  41.4 2.3 %collective-permute-start.6 = (bf16[128,1792]{1,0:T(8,128)(2,1)}, bf16[128,1792]{1,0:T(8,128)(2,1)S(1)}, u32[]{:S(2)}, u32[]{:S(2)}) collective-permute-start(bf16[128,1792]{1,0:T(8,128)(2,1)} %broadcast_select_fusion), channel_id=1, source_target_pairs={{0,4},{4,8},{8,12},{12,14},{14,10},{10,6},{6,2},{2,0},{5,1},{9,5},... | collective-permute-start | bytes 1376264 | tf_op jit(solution)/shard_map/ppermute | solution.py:61
  43.7 8.2 %all-to-all-done = bf16[8,112,224]{2,1,0:T(8,128)(2,1)} async-done(((bf16[8,112,224]{2,1,0:T(8,128)(2,1)}), bf16[8,112,224]{2,1,0:T(8,128)(2,1)}, u32[]{:S(2)}, u32[]{:S(2)}) %all-to-all-start) | async-done | bytes 401440 | tf_op jit(solution)/shard_map/all_to_all | solution.py:160
  51.9 4.2 %all-gather = bf16[8,224,224]{2,1,0:T(8,128)(2,1)} all-gather(bf16[8,112,224]{2,1,0:T(8,128)(2,1)} %all-to-all-done), channel_id=2, replica_groups={{0,1},{2,3},{4,5},{6,7},{8,9},{10,11},{12,13},{14,15},{16,17},{18,19},{..., dimensions={1}, use_global_device_ids=true | all-gather | bytes 1204224 | tf_op jit(solution)/shard_map/all_gather | solution.py:163
  56.1 0.8 copy-done.6
  56.9 4.2 %shard_map.51.refs_8_ = bf16[8,128,224]{2,1,0:T(8,128)(2,1)} custom-call(bf16[128,1792]{1,0:T(8,128)(2,1)} %shard_map.50.refs_0_, bf16[128,1792]{1,0:T(8,128)(2,1)} %copy-done.3, bf16[128,1792]{1,0:T(8,128)(2,1)} %copy-done.2, bf16[128,1792]{1,0:T(8,128)(2,1)} %copy-done.5, bf16[128,1792]{1,0:T(8,128)(2,1)} %copy-done.4, bf16[128,1792]{1,0:T(8,128)(2,1)} %copy-done.1, ...), custom_call_target="tpu_custom_call" | custom-call | flops 822083584 | bytes 3670016 | tf_op jit(solution)/shard_map/pallas_call | solution.py:29
  61.1 1.5 %collective-permute-start.7 = (bf16[8,128,224]{2,1,0:T(8,128)(2,1)}, bf16[8,128,224]{2,1,0:T(8,128)(2,1)S(1)}, u32[]{:S(2)}, u32[]{:S(2)}) collective-permute-start(bf16[8,128,224]{2,1,0:T(8,128)(2,1)} %shard_map.51.refs_8_), channel_id=1, source_target_pairs={{0,16},{16,0},{1,17},{17,1},{2,18},{18,2},{3,19},{19,3},{4,20},{20... | collective-permute-start | bytes 1376264 | tf_op jit(solution)/shard_map/ppermute | solution.py:174
  62.6 12.9 %collective-permute-done.7.refs_9_ = bf16[8,128,224]{2,1,0:T(8,128)(2,1)S(1)} collective-permute-done((bf16[8,128,224]{2,1,0:T(8,128)(2,1)}, bf16[8,128,224]{2,1,0:T(8,128)(2,1)S(1)}, u32[]{:S(2)}, u32[]{:S(2)}) %collective-permute-start.7) | collective-permute-done | bytes 458784 | tf_op jit(solution)/shard_map/ppermute | solution.py:174
  75.5 0.8 copy-done.7
  76.3 4.7 %shard_map.52 = (bf16[8,128,224]{2,1,0:T(8,128)(2,1)}, f32[224,1792]{1,0:T(8,128)}) custom-call(bf16[128,1792]{1,0:T(8,128)(2,1)} %shard_map.50.refs_0_, bf16[128,1792]{1,0:T(8,128)(2,1)} %copy-done.3, bf16[128,1792]{1,0:T(8,128)(2,1)} %copy-done.2, bf16[128,1792]{1,0:T(8,128)(2,1)} %copy-done.5, bf16[128,1792]{1,0:T(8,128)(2,1)} %copy-done.4, ...), custom_call_target="tpu_custom_call" | custom-call | flops 822083584 | bytes 3670016 | tf_op jit(solution)/shard_map/pallas_call | solution.py:29
  81.0 1.5 select_convert_fusion
  82.5 1.7 %collective-permute-done.8 = bf16[112,1792]{1,0:T(8,128)(2,1)S(1)} collective-permute-done((bf16[112,1792]{1,0:T(8,128)(2,1)S(1)}, bf16[112,1792]{1,0:T(8,128)(2,1)S(1)}, u32[]{:S(2)}, u32[]{:S(2)}) %collective-permute-start.8) | collective-permute-done | bytes 401440 | tf_op jit(solution)/shard_map/ppermute | solution.py:190
  84.3 1.5 add_convert_fusion.refs_1_
  85.8 0.6 collective-permute-start.10
  86.3 1.5 collective-permute-start.9
  87.8 9.3 %collective-permute-done.10.refs_3_ = bf16[112,1792]{1,0:T(8,128)(2,1)S(1)} collective-permute-done((bf16[112,1792]{1,0:T(8,128)(2,1)S(1)}, bf16[112,1792]{1,0:T(8,128)(2,1)S(1)}, u32[]{:S(2)}, u32[]{:S(2)}) %collective-permute-start.10) | collective-permute-done | bytes 401440 | tf_op jit(solution)/shard_map/ppermute | solution.py:59
  97.1 0.5 collective-permute-start.12
  97.7 1.5 collective-permute-start.11
  99.2 8.5 %collective-permute-done.12.refs_5_ = bf16[112,1792]{1,0:T(8,128)(2,1)S(1)} collective-permute-done((bf16[112,1792]{1,0:T(8,128)(2,1)S(1)}, bf16[112,1792]{1,0:T(8,128)(2,1)S(1)}, u32[]{:S(2)}, u32[]{:S(2)}) %collective-permute-start.12) | collective-permute-done | bytes 401440 | tf_op jit(solution)/shard_map/ppermute | solution.py:59
  107.7 0.5 collective-permute-start.14
  108.2 1.5 collective-permute-start.13
  110.1 0.8 broadcast_in_dim.7
  110.9 2.4 %scatter_fusion = bf16[8,128,224]{1,2,0:T(8,128)(2,1)} fusion(bf16[8,128,224]{1,2,0:T(8,128)(2,1)} %broadcast_in_dim.7, s32[8]{0:T(128)S(1)} %fusion, bf16[8,128,224]{1,2,0:T(8,128)(2,1)S(1)} %copy.6), kind=kCustom, calls=%fused_computation | custom fusion | bytes 1376288 | tf_op jit(solution)/shard_map/scatter | solution.py:214
  113.3 3.5 %all-to-all-start.1 = ((bf16[8,128,224]{1,2,0:T(8,128)(2,1)}), bf16[8,128,224]{1,2,0:T(8,128)(2,1)S(1)}, u32[]{:S(2)}, u32[]{:S(2)}) async-start(bf16[8,128,224]{1,2,0:T(8,128)(2,1)} %scatter_fusion), calls=%async_computation.1 | async-start | bytes 917504 | tf_op jit(solution)/shard_map/all_to_all | solution.py:215
  116.9 0.5 collective-permute-start.18
  117.4 1.0 collective-permute-done.13.refs_6_
  118.5 2.6 %collective-permute-start.15 = (bf16[112,1792]{1,0:T(8,128)(2,1)S(1)}, bf16[112,1792]{1,0:T(8,128)(2,1)}, u32[]{:S(2)}, u32[]{:S(2)}) collective-permute-start(bf16[112,1792]{1,0:T(8,128)(2,1)S(1)} %broadcast_select_fusion.1), channel_id=1, source_target_pairs={{0,4},{4,8},{8,12},{12,14},{14,10},{10,6},{6,2},{2,0},{5,1},{9,5},... | collective-permute-start | bytes 1204232 | tf_op jit(solution)/shard_map/ppermute | solution.py:61
  121.1 0.5 collective-permute-start.19
  121.7 0.4 collective-permute-start.21
  122.2 7.0 %collective-permute-done.15.refs_8_ = bf16[112,1792]{1,0:T(8,128)(2,1)} collective-permute-done((bf16[112,1792]{1,0:T(8,128)(2,1)S(1)}, bf16[112,1792]{1,0:T(8,128)(2,1)}, u32[]{:S(2)}, u32[]{:S(2)}) %collective-permute-start.15) | collective-permute-done | bytes 401440 | tf_op jit(solution)/shard_map/ppermute | solution.py:61
  129.2 0.7 collective-permute-start.23
  129.8 0.6 stack.107.refs_0_
  130.5 1.0 copy.7
  131.5 0.7 copy-done.18
  132.5 0.8 copy-done.21
  133.3 16.5 %shard_map.53 = bf16[112,1792]{1,0:T(8,128)(2,1)} custom-call(s32[17]{0:T(128)} %stack.107.refs_0_, bf16[112,1792]{1,0:T(8,128)(2,1)} %copy-done.11, bf16[112,1792]{1,0:T(8,128)(2,1)} %copy-done.13, bf16[112,1792]{1,0:T(8,128)(2,1)} %copy-done.12, bf16[112,1792]{1,0:T(8,128)(2,1)} %collective-permute-done.11.refs_4_, bf16[112,1792]{1,0:T(8,128)(2,1)} %copy-done.14, ...), custom_call_target="tpu_custom_call" | custom-call | flops 6576668672 | bytes 6422528 | tf_op jit(solution)/shard_map/pallas_call | solution.py:29
  (66 shorter events, 1.5 us)
Async XLA Ops:
  2.8 13.7 %collective-permute-start.1 = (bf16[128,1792]{1,0:T(8,128)(2,1)}, bf16[128,1792]{1,0:T(8,128)(2,1)S(1)}, u32[]{:S(2)}, u32[]{:S(2)}) collective-permute-start(bf16[128,1792]{1,0:T(8,128)(2,1)} %shard_map.50.refs_0_), channel_id=1, source_target_pairs={{4,0},{5,1},{8,4},{9,5},{12,8},{13,9},{14,12},{15,13},{10,14},{11,... | collective-permute-start | bytes 1376264 | tf_op jit(solution)/shard_map/ppermute | solution.py:59
  5.7 12.5 %collective-permute-start = (bf16[128,1792]{1,0:T(8,128)(2,1)}, bf16[128,1792]{1,0:T(8,128)(2,1)S(1)}, u32[]{:S(2)}, u32[]{:S(2)}) collective-permute-start(bf16[128,1792]{1,0:T(8,128)(2,1)} %shard_map.50.refs_0_), channel_id=1, source_target_pairs={{0,4},{1,5},{4,8},{5,9},{8,12},{9,13},{12,14},{13,15},{14,10},{15,... | collective-permute-start | bytes 1376264 | tf_op jit(solution)/shard_map/ppermute | solution.py:58
  16.5 24.9 %copy-start.2 = (bf16[128,1792]{1,0:T(8,128)(2,1)}, bf16[128,1792]{1,0:T(8,128)(2,1)S(1)}, u32[]{:S(2)}) copy-start(bf16[128,1792]{1,0:T(8,128)(2,1)S(1)} %collective-permute-done.1.refs_2_) | copy-start | bytes 1376260
  16.5 11.7 %collective-permute-start.3 = (bf16[128,1792]{1,0:T(8,128)(2,1)S(1)}, bf16[128,1792]{1,0:T(8,128)(2,1)S(1)}, u32[]{:S(2)}, u32[]{:S(2)}) collective-permute-start(bf16[128,1792]{1,0:T(8,128)(2,1)S(1)} %collective-permute-done.1.refs_2_), channel_id=1, source_target_pairs={{4,0},{5,1},{8,4},{9,5},{12,8},{13,9},{14,12},{15,13},{10,14},{11,... | collective-permute-start | bytes 1376264 | tf_op jit(solution)/shard_map/ppermute | solution.py:59
  18.2 23.2 %copy-start.3 = (bf16[128,1792]{1,0:T(8,128)(2,1)}, bf16[128,1792]{1,0:T(8,128)(2,1)S(1)}, u32[]{:S(2)}) copy-start(bf16[128,1792]{1,0:T(8,128)(2,1)S(1)} %collective-permute-done.refs_1_) | copy-start | bytes 1376260
  18.2 11.4 %collective-permute-start.2 = (bf16[128,1792]{1,0:T(8,128)(2,1)S(1)}, bf16[128,1792]{1,0:T(8,128)(2,1)S(1)}, u32[]{:S(2)}, u32[]{:S(2)}) collective-permute-start(bf16[128,1792]{1,0:T(8,128)(2,1)S(1)} %collective-permute-done.refs_1_), channel_id=1, source_target_pairs={{0,4},{1,5},{4,8},{5,9},{8,12},{9,13},{12,14},{13,15},{14,10},{15,... | collective-permute-start | bytes 1376264 | tf_op jit(solution)/shard_map/ppermute | solution.py:58
  28.2 13.2 %copy-start.4 = (bf16[128,1792]{1,0:T(8,128)(2,1)}, bf16[128,1792]{1,0:T(8,128)(2,1)S(1)}, u32[]{:S(2)}) copy-start(bf16[128,1792]{1,0:T(8,128)(2,1)S(1)} %collective-permute-done.3.refs_4_) | copy-start | bytes 1376260
  28.2 11.2 %collective-permute-start.5 = (bf16[128,1792]{1,0:T(8,128)(2,1)S(1)}, bf16[128,1792]{1,0:T(8,128)(2,1)S(1)}, u32[]{:S(2)}, u32[]{:S(2)}) collective-permute-start(bf16[128,1792]{1,0:T(8,128)(2,1)S(1)} %collective-permute-done.3.refs_4_), channel_id=1, source_target_pairs={{4,0},{5,1},{8,4},{9,5},{12,8},{13,9},{14,12},{15,13},{10,14},{11,... | collective-permute-start | bytes 1376264 | tf_op jit(solution)/shard_map/ppermute | solution.py:59
  29.6 11.8 %copy-start.5 = (bf16[128,1792]{1,0:T(8,128)(2,1)}, bf16[128,1792]{1,0:T(8,128)(2,1)S(1)}, u32[]{:S(2)}) copy-start(bf16[128,1792]{1,0:T(8,128)(2,1)S(1)} %collective-permute-done.2.refs_3_) | copy-start | bytes 1376260
  29.6 10.9 %collective-permute-start.4 = (bf16[128,1792]{1,0:T(8,128)(2,1)S(1)}, bf16[128,1792]{1,0:T(8,128)(2,1)S(1)}, u32[]{:S(2)}, u32[]{:S(2)}) collective-permute-start(bf16[128,1792]{1,0:T(8,128)(2,1)S(1)} %collective-permute-done.2.refs_3_), channel_id=1, source_target_pairs={{0,4},{1,5},{4,8},{5,9},{8,12},{9,13},{12,14},{13,15},{14,10},{15,... | collective-permute-start | bytes 1376264 | tf_op jit(solution)/shard_map/ppermute | solution.py:58
  32.8 19.1 %all-to-all-start = ((bf16[8,112,224]{2,1,0:T(8,128)(2,1)}), bf16[8,112,224]{2,1,0:T(8,128)(2,1)}, u32[]{:S(2)}, u32[]{:S(2)}) async-start(bf16[8,112,224]{2,1,0:T(8,128)(2,1)} %bitcast.36), calls=%async_computation | async-start | bytes 917504 | tf_op jit(solution)/shard_map/all_to_all | solution.py:160
  39.5 16.6 %copy-start = (bf16[128,1792]{1,0:T(8,128)(2,1)}, bf16[128,1792]{1,0:T(8,128)(2,1)S(1)}, u32[]{:S(2)}) copy-start(bf16[128,1792]{1,0:T(8,128)(2,1)S(1)} %collective-permute-done.5.refs_6_) | copy-start | bytes 1376260
  40.5 15.6 %copy-start.1 = (bf16[128,1792]{1,0:T(8,128)(2,1)}, bf16[128,1792]{1,0:T(8,128)(2,1)S(1)}, u32[]{:S(2)}) copy-start(bf16[128,1792]{1,0:T(8,128)(2,1)S(1)} %collective-permute-done.4.refs_5_) | copy-start | bytes 1376260
  41.4 14.6 %collective-permute-start.6 = (bf16[128,1792]{1,0:T(8,128)(2,1)}, bf16[128,1792]{1,0:T(8,128)(2,1)S(1)}, u32[]{:S(2)}, u32[]{:S(2)}) collective-permute-start(bf16[128,1792]{1,0:T(8,128)(2,1)} %broadcast_select_fusion), channel_id=1, source_target_pairs={{0,4},{4,8},{8,12},{12,14},{14,10},{10,6},{6,2},{2,0},{5,1},{9,5},... | collective-permute-start | bytes 1376264 | tf_op jit(solution)/shard_map/ppermute | solution.py:61
  56.0 0.8 copy-start.6
  61.1 14.4 %collective-permute-start.7 = (bf16[8,128,224]{2,1,0:T(8,128)(2,1)}, bf16[8,128,224]{2,1,0:T(8,128)(2,1)S(1)}, u32[]{:S(2)}, u32[]{:S(2)}) collective-permute-start(bf16[8,128,224]{2,1,0:T(8,128)(2,1)} %shard_map.51.refs_8_), channel_id=1, source_target_pairs={{0,16},{16,0},{1,17},{17,1},{2,18},{18,2},{3,19},{19,3},{4,20},{20... | collective-permute-start | bytes 1376264 | tf_op jit(solution)/shard_map/ppermute | solution.py:174
  75.5 0.8 copy-start.7
  82.5 27.3 %copy-start.8 = (bf16[8,128,224]{2,1,0:T(8,128)(2,1)S(1)}, bf16[8,128,224]{2,1,0:T(8,128)(2,1)}, u32[]{:S(2)}) copy-start(bf16[8,128,224]{2,1,0:T(8,128)(2,1)} %get-tuple-element.4) | copy-start | bytes 1376260
  82.5 1.8 %collective-permute-start.8 = (bf16[112,1792]{1,0:T(8,128)(2,1)S(1)}, bf16[112,1792]{1,0:T(8,128)(2,1)S(1)}, u32[]{:S(2)}, u32[]{:S(2)}) collective-permute-start(bf16[112,1792]{1,0:T(8,128)(2,1)S(1)} %select_convert_fusion), channel_id=1, source_target_pairs={{0,1},{1,0},{2,3},{3,2},{4,5},{5,4},{6,7},{7,6},{8,9},{9,8},{10,11... | collective-permute-start | bytes 1204232 | tf_op jit(solution)/shard_map/ppermute | solution.py:190
  85.8 31.0 %copy-start.11 = (bf16[112,1792]{1,0:T(8,128)(2,1)}, bf16[112,1792]{1,0:T(8,128)(2,1)S(1)}, u32[]{:S(2)}) copy-start(bf16[112,1792]{1,0:T(8,128)(2,1)S(1)} %add_convert_fusion.refs_1_) | copy-start | bytes 1204228
  85.8 11.4 %collective-permute-start.10 = (bf16[112,1792]{1,0:T(8,128)(2,1)S(1)}, bf16[112,1792]{1,0:T(8,128)(2,1)S(1)}, u32[]{:S(2)}, u32[]{:S(2)}) collective-permute-start(bf16[112,1792]{1,0:T(8,128)(2,1)S(1)} %add_convert_fusion.refs_1_), channel_id=1, source_target_pairs={{4,0},{5,1},{8,4},{9,5},{12,8},{13,9},{14,12},{15,13},{10,14},{11,... | collective-permute-start | bytes 1204232 | tf_op jit(solution)/shard_map/ppermute | solution.py:59
  86.3 11.3 %collective-permute-start.9 = (bf16[112,1792]{1,0:T(8,128)(2,1)S(1)}, bf16[112,1792]{1,0:T(8,128)(2,1)S(1)}, u32[]{:S(2)}, u32[]{:S(2)}) collective-permute-start(bf16[112,1792]{1,0:T(8,128)(2,1)S(1)} %add_convert_fusion.refs_1_), channel_id=1, source_target_pairs={{0,4},{1,5},{4,8},{5,9},{8,12},{9,13},{12,14},{13,15},{14,10},{15,... | collective-permute-start | bytes 1204232 | tf_op jit(solution)/shard_map/ppermute | solution.py:58
  97.1 19.7 %copy-start.12 = (bf16[112,1792]{1,0:T(8,128)(2,1)}, bf16[112,1792]{1,0:T(8,128)(2,1)S(1)}, u32[]{:S(2)}) copy-start(bf16[112,1792]{1,0:T(8,128)(2,1)S(1)} %collective-permute-done.10.refs_3_) | copy-start | bytes 1204228
  97.1 10.5 %collective-permute-start.12 = (bf16[112,1792]{1,0:T(8,128)(2,1)S(1)}, bf16[112,1792]{1,0:T(8,128)(2,1)S(1)}, u32[]{:S(2)}, u32[]{:S(2)}) collective-permute-start(bf16[112,1792]{1,0:T(8,128)(2,1)S(1)} %collective-permute-done.10.refs_3_), channel_id=1, source_target_pairs={{4,0},{5,1},{8,4},{9,5},{12,8},{13,9},{14,12},{15,13},{10,14},{11,... | collective-permute-start | bytes 1204232 | tf_op jit(solution)/shard_map/ppermute | solution.py:59
  97.7 19.7 %copy-start.13 = (bf16[112,1792]{1,0:T(8,128)(2,1)}, bf16[112,1792]{1,0:T(8,128)(2,1)S(1)}, u32[]{:S(2)}) copy-start(bf16[112,1792]{1,0:T(8,128)(2,1)S(1)} %collective-permute-done.9.refs_2_) | copy-start | bytes 1204228
  97.7 10.5 %collective-permute-start.11 = (bf16[112,1792]{1,0:T(8,128)(2,1)S(1)}, bf16[112,1792]{1,0:T(8,128)(2,1)}, u32[]{:S(2)}, u32[]{:S(2)}) collective-permute-start(bf16[112,1792]{1,0:T(8,128)(2,1)S(1)} %collective-permute-done.9.refs_2_), channel_id=1, source_target_pairs={{0,4},{1,5},{4,8},{5,9},{8,12},{9,13},{12,14},{13,15},{14,10},{15,... | collective-permute-start | bytes 1204232 | tf_op jit(solution)/shard_map/ppermute | solution.py:58
  107.7 13.5 %copy-start.14 = (bf16[112,1792]{1,0:T(8,128)(2,1)}, bf16[112,1792]{1,0:T(8,128)(2,1)S(1)}, u32[]{:S(2)}) copy-start(bf16[112,1792]{1,0:T(8,128)(2,1)S(1)} %collective-permute-done.12.refs_5_) | copy-start | bytes 1204228
  107.7 9.8 %collective-permute-start.14 = (bf16[112,1792]{1,0:T(8,128)(2,1)S(1)}, bf16[112,1792]{1,0:T(8,128)(2,1)S(1)}, u32[]{:S(2)}, u32[]{:S(2)}) collective-permute-start(bf16[112,1792]{1,0:T(8,128)(2,1)S(1)} %collective-permute-done.12.refs_5_), channel_id=1, source_target_pairs={{4,0},{5,1},{8,4},{9,5},{12,8},{13,9},{14,12},{15,13},{10,14},{11,... | collective-permute-start | bytes 1204232 | tf_op jit(solution)/shard_map/ppermute | solution.py:59
  108.2 10.3 %collective-permute-start.13 = (bf16[112,1792]{1,0:T(8,128)(2,1)}, bf16[112,1792]{1,0:T(8,128)(2,1)S(1)}, u32[]{:S(2)}, u32[]{:S(2)}) collective-permute-start(bf16[112,1792]{1,0:T(8,128)(2,1)} %collective-permute-done.11.refs_4_), channel_id=1, source_target_pairs={{0,4},{1,5},{4,8},{5,9},{8,12},{9,13},{12,14},{13,15},{14,10},{15,... | collective-permute-start | bytes 1204232 | tf_op jit(solution)/shard_map/ppermute | solution.py:58
  113.3 17.2 %all-to-all-start.1 = ((bf16[8,128,224]{1,2,0:T(8,128)(2,1)}), bf16[8,128,224]{1,2,0:T(8,128)(2,1)S(1)}, u32[]{:S(2)}, u32[]{:S(2)}) async-start(bf16[8,128,224]{1,2,0:T(8,128)(2,1)} %scatter_fusion), calls=%async_computation.1 | async-start | bytes 917504 | tf_op jit(solution)/shard_map/all_to_all | solution.py:215
  116.8 4.3 %collective-permute-start.16 = (bf16[112,1792]{1,0:T(8,128)(2,1)S(1)}, bf16[112,1792]{1,0:T(8,128)(2,1)S(1)}, u32[]{:S(2)}, u32[]{:S(2)}) collective-permute-start(bf16[112,1792]{1,0:T(8,128)(2,1)S(1)} %add_convert_fusion.refs_1_), channel_id=1, source_target_pairs={{0,1},{1,0},{2,3},{3,2},{4,5},{5,4},{6,7},{7,6},{8,9},{9,8},{10,11... | collective-permute-start | bytes 1204232 | tf_op jit(solution)/shard_map/ppermute | solution.py:195
  116.9 4.8 %collective-permute-start.18 = (bf16[112,1792]{1,0:T(8,128)(2,1)S(1)}, bf16[112,1792]{1,0:T(8,128)(2,1)S(1)}, u32[]{:S(2)}, u32[]{:S(2)}) collective-permute-start(bf16[112,1792]{1,0:T(8,128)(2,1)S(1)} %collective-permute-done.10.refs_3_), channel_id=1, source_target_pairs={{0,1},{1,0},{2,3},{3,2},{4,5},{5,4},{6,7},{7,6},{8,9},{9,8},{10,11... | collective-permute-start | bytes 1204232 | tf_op jit(solution)/shard_map/ppermute | solution.py:195
  117.4 4.4 %collective-permute-start.17 = (bf16[112,1792]{1,0:T(8,128)(2,1)S(1)}, bf16[112,1792]{1,0:T(8,128)(2,1)S(1)}, u32[]{:S(2)}, u32[]{:S(2)}) collective-permute-start(bf16[112,1792]{1,0:T(8,128)(2,1)S(1)} %collective-permute-done.9.refs_2_), channel_id=1, source_target_pairs={{0,1},{1,0},{2,3},{3,2},{4,5},{5,4},{6,7},{7,6},{8,9},{9,8},{10,11... | collective-permute-start | bytes 1204232 | tf_op jit(solution)/shard_map/ppermute | solution.py:195
  117.4 14.1 %copy-start.9 = (bf16[112,1792]{1,0:T(8,128)(2,1)}, bf16[112,1792]{1,0:T(8,128)(2,1)S(1)}, u32[]{:S(2)}) copy-start(bf16[112,1792]{1,0:T(8,128)(2,1)S(1)} %collective-permute-done.14.refs_7_) | copy-start | bytes 1204228
  118.4 13.1 %copy-start.10 = (bf16[112,1792]{1,0:T(8,128)(2,1)}, bf16[112,1792]{1,0:T(8,128)(2,1)S(1)}, u32[]{:S(2)}) copy-start(bf16[112,1792]{1,0:T(8,128)(2,1)S(1)} %collective-permute-done.13.refs_6_) | copy-start | bytes 1204228
  118.5 10.7 %collective-permute-start.15 = (bf16[112,1792]{1,0:T(8,128)(2,1)S(1)}, bf16[112,1792]{1,0:T(8,128)(2,1)}, u32[]{:S(2)}, u32[]{:S(2)}) collective-permute-start(bf16[112,1792]{1,0:T(8,128)(2,1)S(1)} %broadcast_select_fusion.1), channel_id=1, source_target_pairs={{0,4},{4,8},{8,12},{12,14},{14,10},{10,6},{6,2},{2,0},{5,1},{9,5},... | collective-permute-start | bytes 1204232 | tf_op jit(solution)/shard_map/ppermute | solution.py:61
  121.1 10.3 %collective-permute-start.20 = (bf16[112,1792]{1,0:T(8,128)(2,1)S(1)}, bf16[112,1792]{1,0:T(8,128)(2,1)}, u32[]{:S(2)}, u32[]{:S(2)}) collective-permute-start(bf16[112,1792]{1,0:T(8,128)(2,1)S(1)} %collective-permute-done.12.refs_5_), channel_id=1, source_target_pairs={{0,1},{1,0},{2,3},{3,2},{4,5},{5,4},{6,7},{7,6},{8,9},{9,8},{10,11... | collective-permute-start | bytes 1204232 | tf_op jit(solution)/shard_map/ppermute | solution.py:195
  121.1 8.0 %copy-start.15 = (bf16[112,1792]{1,0:T(8,128)(2,1)}, bf16[112,1792]{1,0:T(8,128)(2,1)S(1)}, u32[]{:S(2)}) copy-start(bf16[112,1792]{1,0:T(8,128)(2,1)S(1)} %collective-permute-done.16.refs_9_) | copy-start | bytes 1204228
  121.1 10.3 %collective-permute-start.19 = (bf16[112,1792]{1,0:T(8,128)(2,1)}, bf16[112,1792]{1,0:T(8,128)(2,1)S(1)}, u32[]{:S(2)}, u32[]{:S(2)}) collective-permute-start(bf16[112,1792]{1,0:T(8,128)(2,1)} %collective-permute-done.11.refs_4_), channel_id=1, source_target_pairs={{0,1},{1,0},{2,3},{3,2},{4,5},{5,4},{6,7},{7,6},{8,9},{9,8},{10,11... | collective-permute-start | bytes 1204232 | tf_op jit(solution)/shard_map/ppermute | solution.py:195
  121.6 7.5 %copy-start.16 = (bf16[112,1792]{1,0:T(8,128)(2,1)}, bf16[112,1792]{1,0:T(8,128)(2,1)S(1)}, u32[]{:S(2)}) copy-start(bf16[112,1792]{1,0:T(8,128)(2,1)S(1)} %collective-permute-done.18.refs_11_) | copy-start | bytes 1204228
  121.6 9.8 %collective-permute-start.22 = (bf16[112,1792]{1,0:T(8,128)(2,1)S(1)}, bf16[112,1792]{1,0:T(8,128)(2,1)S(1)}, u32[]{:S(2)}, u32[]{:S(2)}) collective-permute-start(bf16[112,1792]{1,0:T(8,128)(2,1)S(1)} %collective-permute-done.14.refs_7_), channel_id=1, source_target_pairs={{0,1},{1,0},{2,3},{3,2},{4,5},{5,4},{6,7},{7,6},{8,9},{9,8},{10,11... | collective-permute-start | bytes 1204232 | tf_op jit(solution)/shard_map/ppermute | solution.py:195
  121.7 7.4 %copy-start.17 = (bf16[112,1792]{1,0:T(8,128)(2,1)}, bf16[112,1792]{1,0:T(8,128)(2,1)S(1)}, u32[]{:S(2)}) copy-start(bf16[112,1792]{1,0:T(8,128)(2,1)S(1)} %collective-permute-done.17.refs_10_) | copy-start | bytes 1204228
  121.7 9.7 %collective-permute-start.21 = (bf16[112,1792]{1,0:T(8,128)(2,1)S(1)}, bf16[112,1792]{1,0:T(8,128)(2,1)S(1)}, u32[]{:S(2)}, u32[]{:S(2)}) collective-permute-start(bf16[112,1792]{1,0:T(8,128)(2,1)S(1)} %collective-permute-done.13.refs_6_), channel_id=1, source_target_pairs={{0,1},{1,0},{2,3},{3,2},{4,5},{5,4},{6,7},{7,6},{8,9},{9,8},{10,11... | collective-permute-start | bytes 1204232 | tf_op jit(solution)/shard_map/ppermute | solution.py:195
  129.2 2.3 %collective-permute-start.23 = (bf16[112,1792]{1,0:T(8,128)(2,1)}, bf16[112,1792]{1,0:T(8,128)(2,1)S(1)}, u32[]{:S(2)}, u32[]{:S(2)}) collective-permute-start(bf16[112,1792]{1,0:T(8,128)(2,1)} %collective-permute-done.15.refs_8_), channel_id=1, source_target_pairs={{0,1},{1,0},{2,3},{3,2},{4,5},{5,4},{6,7},{7,6},{8,9},{9,8},{10,11... | collective-permute-start | bytes 1204232 | tf_op jit(solution)/shard_map/ppermute | solution.py:195
  131.4 0.8 copy-start.18
  131.5 0.9 copy-start.19
  131.5 1.0 copy-start.20
  132.5 0.8 copy-start.21

commit v2 on v1

v2 whole, which is shorter than its diff:
```python
import functools
import math

import jax
import jax.numpy as jnp
from jax import lax
from jax.experimental import pallas as pl
from jax.experimental.pallas import tpu as pltpu
from jax.sharding import PartitionSpec as P

BF16 = jnp.bfloat16
F32 = jnp.float32
VMEM = pl.BlockSpec(memory_space=pltpu.VMEM)
SMEM = pl.BlockSpec(memory_space=pltpu.SMEM)


def shape(dims, dtype):
    return jax.ShapeDtypeStruct(dims, dtype)


def contract(left, right, left_dim, right_dim):
    return lax.dot_general(
        left, right, (((left_dim,), (right_dim,)), ((), ())), preferred_element_type=F32
    )


def nbytes(array):
    return math.prod(array.shape) * jnp.dtype(array.dtype).itemsize


def call(kernel, outs, smem, vmem, scratch=(), flops=0, room=4):
    held = sum(map(nbytes, [*vmem, *jax.tree.leaves(outs), *scratch]))
    return pl.pallas_call(
        kernel,
        out_shape=outs,
        in_specs=[SMEM] * len(smem) + [VMEM] * len(vmem),
        out_specs=jax.tree.map(lambda _: VMEM, outs),
        scratch_shapes=[pltpu.VMEM(s.shape, s.dtype) for s in scratch],
        compiler_params=pltpu.CompilerParams(vmem_limit_bytes=held + room * 2**20),
        cost_estimate=pl.CostEstimate(flops=flops, bytes_accessed=held, transcendentals=0),
    )(*smem, *vmem)


def position_of(chip, chips):
    return jnp.where(chip % 2 == 0, chip // 2, chips - 1 - chip // 2)


def chip_at(position, chips):
    return jnp.where(position < chips // 2, 2 * position, 2 * (chips - 1 - position) + 1)


def me(chips):
    index = lax.axis_index("tok")
    return index, index % 2, position_of(index // 2, chips)


def ring_order(chips):
    return list(range(0, chips, 2)) + list(range(chips - 1, 0, -2))


def shift(block, by, chips):
    order = ring_order(chips)
    pairs = [(order[i], order[(i + by) % chips]) for i in range(chips)]
    return lax.ppermute(block, "tok", [(2 * a + c, 2 * b + c) for a, b in pairs for c in (0, 1)])


def ring_gather(halves, chips):
    blocks, ahead, behind = [list(halves)], list(halves), list(halves)
    for _ in range(chips // 2 - 1):
        for i in range(2):
            ahead[i] = shift(ahead[i], 1, chips)
            behind[i] = shift(behind[i], -1, chips)
        blocks += [list(ahead), list(behind)]
    blocks.append([shift(ahead[0], 1, chips), shift(behind[1], -1, chips)])
    return blocks


def ring_offsets(chips):
    near = [sign * step for step in range(1, chips // 2) for sign in (-1, 1)]
    return [0] + near + [chips // 2]


def align_kernel(order_ref, rows_ref, out_ref):
    count = rows_ref.shape[0]
    picks = lax.broadcasted_iota(jnp.int32, (count, count), 0) == order_ref[...]
    out_ref[...] = contract(picks.astype(BF16), rows_ref[...], 0, 0).astype(BF16)


def pieces_kernel(chips, rows_ref, *refs):
    outs, held = refs[:chips], refs[chips]
    _, _, position = me(chips)
    cols = held.shape[2]
    for chip in range(chips):
        held[chip] = rows_ref[:, chip * cols : (chip + 1) * cols]
    for out, offset in zip(outs, ring_offsets(chips), strict=True):
        out[...] = held[chip_at((position + offset + chips) % chips, chips)]


def stack_kernel(chips, *refs):
    pieces, out_ref = refs[:chips], refs[chips]
    _, _, position = me(chips)
    slab = pieces[0].shape[0]
    for piece, offset in zip(pieces, ring_offsets(chips), strict=True):
        chip = chip_at((position - offset + chips) % chips, chips)
        out_ref[pl.ds(pl.multiple_of(chip * slab, 16), slab), :] = piece[...]


def join_kernel(chips, *refs):
    pieces, out_ref, held = refs[:chips], refs[chips], refs[chips + 1]
    _, _, position = me(chips)
    cols = held.shape[2]
    for piece, offset in zip(pieces, ring_offsets(chips), strict=True):
        held[chip_at((position - offset + chips) % chips, chips)] = piece[...]
    for chip in range(chips):
        out_ref[:, chip * cols : (chip + 1) * cols] = held[chip]


def rotate_kernel(count, chips, *refs):
    halves = refs[:count]
    size = halves[0].shape[0]
    if len(refs) == count + 2:
        cols_ref, out_ref = refs[count:]
    else:
        own_ref, sibling_ref, out_ref, cols_ref = refs[count:]
        _, core, _ = me(chips)
        slab = own_ref.shape[0] // chips
        for chip in range(chips):
            for ref, parity in ((own_ref, core), (sibling_ref, 1 - core)):
                row = pl.multiple_of((2 * chip + parity) * slab, 16)
                cols_ref[pl.ds(row, slab), :] = ref[chip * slab : (chip + 1) * slab, :]
    for i, half in enumerate(halves):
        out_ref[i * size : (i + 1) * size, :] = jnp.dot(
            half[...], cols_ref[...], preferred_element_type=F32
        ).astype(BF16)


def cov_sum(halves, groups, cons_ref, rows_ref):
    size = halves[0].shape[0]
    for i, half in enumerate(halves):
        rows_ref[i * size : (i + 1) * size, :] = half[...]
    at = 0
    for parts in groups:
        total = parts[0][...].astype(F32)
        for part in parts[1:]:
            total = total + part[...].astype(F32)
        cons_ref[at : at + total.shape[0], :] = (total / len(parts)).astype(BF16)
        at += total.shape[0]
    return contract(cons_ref[...], rows_ref[...], 0, 0)


def early_kernel(count, members, *refs):
    halves, parts = refs[:count], refs[count : count + members]
    cons_ref, cov_ref, rows_ref = refs[count + members :]
    cov_ref[...] = cov_sum(halves, [parts], cons_ref, rows_ref)


def late_kernel(count, members, *refs):
    core = lax.axis_index("tok") % 2
    halves, middle = refs[:count], refs[count : count + members]
    far = refs[count + members : count + 2 * members]
    early_ref, cons_ref, keep_ref, give_ref, rows_ref = refs[count + 2 * members :]
    cov = early_ref[...] + cov_sum(halves, [middle, far], cons_ref, rows_ref)
    slab = cov.shape[0] // 2
    low, high = cov[:slab], cov[slab:]
    keep_ref[...] = jnp.where(core == 0, low, high)
    give_ref[...] = jnp.where(core == 0, high, low).astype(BF16)


def chain_kernel(count, slab, *refs):
    blocks = refs[: 2 * count]
    out_ref, whole, turned = refs[2 * count :]
    width = whole.shape[0]
    chips = width // slab // 2
    index, core, position = me(chips)
    size, half = width // count, width // 2
    squares = jnp.zeros((1, width), F32)
    for i in range(count):
        for side in range(2):
            whole[i * size : (i + 1) * size, side * half : (side + 1) * half] = blocks[2 * i + side][...]
        values = whole[i * size : (i + 1) * size, :].astype(F32)
        squares = squares + jnp.sum(values * values, axis=0, keepdims=True)
    inverse = 1.0 / (2.0 * jnp.sqrt(jnp.sum(squares, axis=1, keepdims=True) / width + 1e-06))

    rows = turned.shape[1]
    span = min(rows + 128, width)
    first_row = index * slab
    window = jnp.minimum(first_row // 128, (width - span) // 128) * 128
    window = pl.multiple_of(window, 128)
    columns = whole[:, pl.ds(window, span)]
    picks = lax.broadcasted_iota(jnp.int32, (rows, span), 1) == (
        lax.broadcasted_iota(jnp.int32, (rows, span), 0) + (first_row - window)
    )
    own = contract(picks.astype(BF16), columns, 1, 1)
    start = (own * inverse).astype(BF16)

    def apply_once(vector):
        inner = jnp.dot(vector.astype(BF16), whole[...], preferred_element_type=F32) * inverse
        return contract(inner.astype(BF16), whole[...], 1, 1) * inverse

    first = 1.5 * start.astype(F32) - 0.5 * apply_once(start)
    upper = 1.5 * first - 0.5 * apply_once(first)
    middle = apply_once(upper)
    cubic = 1.5 * middle - 0.5 * apply_once(middle)
    result = math.sqrt(width) * (1.5 * first - 0.5 * cubic)
    if count == 1:
        out_ref[...] = result[:slab].astype(BF16)
        return
    result = result.T
    for i in range(count):
        chip = chip_at((position + ring_offsets(chips)[i % chips] + chips) % chips, chips)
        parity = core if i < chips else 1 - core
        row = pl.multiple_of((2 * chip + parity) * size, 16)
        turned[pl.ds(row, size), :] = result[i * size : (i + 1) * size, :]
    out_ref[...] = turned[...].T[:slab].astype(BF16)


def shards(features, pairing, rotation):
    own_rows, own_order, rot_rows = features[0], pairing[0], rotation[0]
    count, width = own_rows.shape
    devices, members = lax.axis_size("tok"), lax.axis_size("ckpt")
    chips = devices // 2
    slab, cols = width // devices, width // chips
    siblings = [(i, i ^ 1) for i in range(devices)]
    parity = [[2 * i + c for i in range(chips)] for c in (0, 1)]
    pairs = [[2 * i, 2 * i + 1] for i in range(chips)]
    offsets = ring_offsets(chips)
    tiled = slab % 16 == 0

    aligned = call(align_kernel, shape((count, width), BF16), [], [own_order, own_rows])
    blocks = ring_gather(jnp.split(aligned, 2, axis=0), chips)

    if tiled:
        pieces = call(
            functools.partial(pieces_kernel, chips),
            [shape((slab, cols), BF16)] * chips,
            [],
            [rot_rows],
            [shape((chips, slab, cols), BF16)],
        )
        pieces = [pieces[0]] + [
            shift(piece, offset, chips) for piece, offset in zip(pieces[1:], offsets[1:], strict=True)
        ]
        stacked = call(
            functools.partial(stack_kernel, chips), shape((chips * slab, cols), BF16), [], pieces
        )
        rot_cols = [stacked, lax.ppermute(stacked, "tok", siblings)]
        rot_scratch = [shape((width, cols), BF16)]
    else:
        pieces = rot_rows.reshape(slab, chips, cols).transpose(1, 0, 2)
        pieces = lax.all_to_all(
            pieces, "tok", split_axis=0, concat_axis=0, tiled=True, axis_index_groups=parity
        )
        pieces = lax.all_gather(pieces, "tok", axis=1, axis_index_groups=pairs)
        rot_cols, rot_scratch = [pieces.reshape(width, cols)], []

    def rotate(group):
        halves = sum(group, [])
        rotated = call(
            functools.partial(rotate_kernel, len(halves), chips),
            shape((len(group) * count, cols), BF16),
            [],
            halves + rot_cols,
            rot_scratch,
            flops=2 * len(group) * count * cols * width,
        )
        if members == 2:
            return halves, [rotated, lax.ppermute(rotated, "ckpt", [(0, 1), (1, 0)])]
        gathered = lax.all_gather(rotated, "ckpt", axis=0)
        return halves, [gathered[i] for i in range(members)]

    early_rows, early_parts = rotate(blocks[:-3])
    middle_rows, middle_parts = rotate(blocks[-3:-1])
    far_rows, far_parts = rotate(blocks[-1:])
    near = (chips - 3) * count
    early_cons, early_cov = call(
        functools.partial(early_kernel, len(early_rows), members),
        (shape((near, cols), BF16), shape((cols, width), F32)),
        [],
        early_rows + early_parts,
        [shape((near, width), BF16)],
        flops=2 * near * cols * width,
    )
    late_rows = middle_rows + far_rows
    late_cons, keep, give = call(
        functools.partial(late_kernel, len(late_rows), members),
        (shape((3 * count, cols), BF16), shape((slab, width), F32), shape((slab, width), BF16)),
        [],
        late_rows + middle_parts + far_parts + [early_cov],
        [shape((3 * count, width), BF16)],
        flops=2 * 3 * count * cols * width,
    )
    own = (keep + lax.ppermute(give, "tok", siblings).astype(F32)).astype(BF16)

    if tiled:
        same = ring_gather(jnp.split(own, 2, axis=1), chips)
        other = [[lax.ppermute(half, "tok", siblings) for half in block] for block in same]
        gathered = sum(same + other, [])
    else:
        gathered = jnp.split(lax.all_gather(own, "tok", axis=0, tiled=True), 2, axis=1)
    rows = -(-slab // 128) * 128
    rotation_next = call(
        functools.partial(chain_kernel, len(gathered) // 2, slab),
        shape((slab, width), BF16),
        [],
        gathered,
        [shape((width, width), BF16), shape((width, rows), F32)],
        flops=16 * rows * width * width,
        room=10,
    )

    cons = [early_cons[i : i + count] for i in range(0, near, count)]
    cons += [late_cons[i : i + count] for i in range(0, 3 * count, count)]
    if tiled:
        cons = cons[:1] + [
            shift(block, offset, chips) for block, offset in zip(cons[1:], offsets[1:], strict=True)
        ]
        consensus = call(
            functools.partial(join_kernel, chips),
            shape((count, width), BF16),
            [],
            cons,
            [shape((chips, count, cols), BF16)],
        )
    else:
        _, _, position = me(chips)
        natural = jnp.stack([chip_at((position + offset + chips) % chips, chips) for offset in offsets])
        ordered = jnp.zeros((chips, count, cols), BF16).at[natural].set(jnp.stack(cons), unique_indices=True)
        consensus = lax.all_to_all(
            ordered, "tok", split_axis=0, concat_axis=0, tiled=True, axis_index_groups=parity
        )
        consensus = consensus.transpose(1, 0, 2).reshape(count, width)
    return (consensus, rotation_next[None])


def solution(mesh):
    placed = (P("ckpt", "tok", None), P("ckpt", "tok", None), P("ckpt", "tok", None))
    return jax.shard_map(
        shards,
        mesh=mesh,
        in_specs=placed,
        out_specs=(P("tok", None), P("ckpt", "tok", None)),
        check_vma=False,
    )
```

time: 151 us -> 134 us (0.89)
  starting transfers between devices: 31.2 us -> 59.1 us
  waiting for transfers between devices: 71 us -> 51.7 us
  local copies, waits for them, and re-layouts: 11.1 us -> 1.77 us
  Pallas kernels: 27.6 us -> 20.1 us
  blocking collectives: 4.17 us -> 0 us
  other arithmetic: 3.92 us -> 0.08 us
    ppermute x23 -> x62, starting transfers between devices: 21.9 us -> 59.1 us  [the longest x42 53.6 us: shift(): lax.ppermute(block, 'tok', [(2 * a + c, 2 * b + c) for a, b in pairs for...]
    ppermute x23 -> x62, waiting for transfers between devices: 61.1 us -> 51.7 us  [the longest x42 49.4 us: shift(): lax.ppermute(block, 'tok', [(2 * a + c, 2 * b + c) for a, b in pairs for...]
    all_to_all x2 -> x0, starting transfers between devices: 9.18 us -> none  [the longest x1 5.68 us: shards(): lax.all_to_all(rot_pieces, 'tok', split_axis=0, concat_axis=0, tiled=True...]
    all_to_all x2 -> x0, waiting for transfers between devices: 8.2 us -> none  [the longest x1 8.2 us: shards(): lax.all_to_all(rot_pieces, 'tok', split_axis=0, concat_axis=0, tiled=True...]
    pallas_call x4 -> x10, Pallas kernels: 27.6 us -> 20.1 us  [call(): pl.pallas_call(kernel, out_shape=outs, in_specs=[SMEM] * len(smem) + [VME...]
    all_gather x1 -> x0, blocking collectives: 4.17 us -> none  [shards(): lax.all_gather(rot_pieces, 'tok', axis=1, axis_index_groups=pairs)]
    another operation x4 -> x0, local copies, waits for them, and re-layouts: 3.25 us -> none  [the longest x2 2.53 us: shards(): rot_pieces = rot_rows.reshape(slab, chips, cols).transpose(1, 0, 2)]
    unnamed x45 -> x6, local copies, waits for them, and re-layouts: 4.39 us -> 1.67 us
  transfers between devices with their start and end apart: 26 -> 63, of which waited for: 11 -> 26; matrix products, arithmetic and copies ran while one was open for 6% -> 0% of each run, Pallas kernels for 0% -> 4%
where the time goes in v2:
time: 134 us
  starting transfers between devices  59.1 us (44%)
  waiting for transfers between devices  51.7 us (39%)
  Pallas kernels  20.1 us (15%)
  local copies, waits for them, and re-layouts  1.77 us (1%)
    ppermute x42, starting transfers between devices, shift(): lax.ppermute(block, 'tok', [(2 * a + c, 2 * b + c) for a, b in pairs for...  53.6 us
    ppermute x42, waiting for transfers between devices, shift(): lax.ppermute(block, 'tok', [(2 * a + c, 2 * b + c) for a, b in pairs for...  49.4 us
    pallas_call x10, Pallas kernels, call(): pl.pallas_call(kernel, out_shape=outs, in_specs=[SMEM] * len(smem) + [VME...  20.1 us
    ppermute x3, starting transfers between devices, rotate(): return (halves, [rotated, lax.ppermute(rotated, 'ckpt', [(0, 1), (1, 0)])])  4.68 us
  transfers between devices with their start and end apart: 63, of which 26 were waited for; matrix products, arithmetic and copies ran while one was open for 0% of the time, Pallas kernels for 4%

profile of v2, /device:TPU:0, one launch (start us, length us, event | category | flops | bytes accessed | tf_op | source)
XLA Modules:
  0.0 133.7 jit_solution(8345086865981336619)
XLA Ops:
  2.7 3.0 %collective-permute-start.3 = (bf16[64,1792]{1,0:T(8,128)(2,1)S(1)}, bf16[64,1792]{1,0:T(8,128)(2,1)S(1)}, u32[]{:S(2)}, u32[]{:S(2)}) collective-permute-start(bf16[64,1792]{1,0:T(8,128)(2,1)S(1)} %get-tuple-element.28.refs_1_), channel_id=1, source_target_pairs={{0,2},{1,3},{4,0},{5,1},{8,4},{9,5},{12,8},{13,9},{14,12},{15,13},... | collective-permute-start | bytes 688136 | tf_op jit(solution)/shard_map/ppermute | solution.py:64
  6.1 2.0 %collective-permute-start.8 = (bf16[112,224]{1,0:T(8,128)(2,1)S(1)}, bf16[112,224]{1,0:T(8,128)(2,1)S(1)}, u32[]{:S(2)}, u32[]{:S(2)}) collective-permute-start(bf16[112,224]{1,0:T(8,128)(2,1)S(1)} %get-tuple-element.16), channel_id=1, source_target_pairs={{0,2},{1,3},{4,0},{5,1},{8,4},{9,5},{12,8},{13,9},{14,12},{15,13},... | collective-permute-start | bytes 150536 | tf_op jit(solution)/shard_map/ppermute | solution.py:64
  8.1 2.9 %collective-permute-start.10 = (bf16[112,224]{1,0:T(8,128)(2,1)S(1)}, bf16[112,224]{1,0:T(8,128)(2,1)S(1)}, u32[]{:S(2)}, u32[]{:S(2)}) collective-permute-start(bf16[112,224]{1,0:T(8,128)(2,1)S(1)} %get-tuple-element.18), channel_id=1, source_target_pairs={{0,6},{1,7},{4,2},{5,3},{8,0},{9,1},{12,4},{13,5},{14,8},{15,9},{1... | collective-permute-start | bytes 150536 | tf_op jit(solution)/shard_map/ppermute | solution.py:64
  11.1 2.7 %collective-permute-done.8.refs_1_ = bf16[112,224]{1,0:T(8,128)(2,1)S(1)} collective-permute-done((bf16[112,224]{1,0:T(8,128)(2,1)S(1)}, bf16[112,224]{1,0:T(8,128)(2,1)S(1)}, u32[]{:S(2)}, u32[]{:S(2)}) %collective-permute-start.8) | collective-permute-done | bytes 50208 | tf_op jit(solution)/shard_map/ppermute | solution.py:64
  13.7 2.2 %collective-permute-start.11 = (bf16[112,224]{1,0:T(8,128)(2,1)S(1)}, bf16[112,224]{1,0:T(8,128)(2,1)S(1)}, u32[]{:S(2)}, u32[]{:S(2)}) collective-permute-start(bf16[112,224]{1,0:T(8,128)(2,1)S(1)} %get-tuple-element.19), channel_id=1, source_target_pairs={{0,8},{1,9},{4,12},{5,13},{8,14},{9,15},{12,10},{13,11},{14,6},{15... | collective-permute-start | bytes 150536 | tf_op jit(solution)/shard_map/ppermute | solution.py:64
  16.0 2.6 %collective-permute-start.12 = (bf16[112,224]{1,0:T(8,128)(2,1)S(1)}, bf16[112,224]{1,0:T(8,128)(2,1)S(1)}, u32[]{:S(2)}, u32[]{:S(2)}) collective-permute-start(bf16[112,224]{1,0:T(8,128)(2,1)S(1)} %get-tuple-element.20), channel_id=1, source_target_pairs={{0,10},{1,11},{4,6},{5,7},{8,2},{9,3},{12,0},{13,1},{14,4},{15,5},... | collective-permute-start | bytes 150536 | tf_op jit(solution)/shard_map/ppermute | solution.py:64
  19.8 1.4 %collective-permute-start.1 = (bf16[64,1792]{1,0:T(8,128)(2,1)S(1)}, bf16[64,1792]{1,0:T(8,128)(2,1)S(1)}, u32[]{:S(2)}, u32[]{:S(2)}) collective-permute-start(bf16[64,1792]{1,0:T(8,128)(2,1)S(1)} %get-tuple-element.28.refs_1_), channel_id=1, source_target_pairs={{0,4},{1,5},{4,8},{5,9},{8,12},{9,13},{12,14},{13,15},{14,10},{15,... | collective-permute-start | bytes 688136 | tf_op jit(solution)/shard_map/ppermute | solution.py:64
  21.2 1.3 %collective-permute-done.12.refs_5_ = bf16[112,224]{1,0:T(8,128)(2,1)S(1)} collective-permute-done((bf16[112,224]{1,0:T(8,128)(2,1)S(1)}, bf16[112,224]{1,0:T(8,128)(2,1)S(1)}, u32[]{:S(2)}, u32[]{:S(2)}) %collective-permute-start.12) | collective-permute-done | bytes 50208 | tf_op jit(solution)/shard_map/ppermute | solution.py:64
  23.5 2.4 %collective-permute-done.13.refs_6_ = bf16[112,224]{1,0:T(8,128)(2,1)S(1)} collective-permute-done((bf16[112,224]{1,0:T(8,128)(2,1)S(1)}, bf16[112,224]{1,0:T(8,128)(2,1)S(1)}, u32[]{:S(2)}, u32[]{:S(2)}) %collective-permute-start.13) | collective-permute-done | bytes 50208 | tf_op jit(solution)/shard_map/ppermute | solution.py:64
  25.9 2.4 %collective-permute-start.14 = (bf16[112,224]{1,0:T(8,128)(2,1)S(1)}, bf16[112,224]{1,0:T(8,128)(2,1)S(1)}, u32[]{:S(2)}, u32[]{:S(2)}) collective-permute-start(bf16[112,224]{1,0:T(8,128)(2,1)S(1)} %get-tuple-element.22), channel_id=1, source_target_pairs={{0,14},{1,15},{4,10},{5,11},{8,6},{9,7},{12,2},{13,3},{14,0},{15,1... | collective-permute-start | bytes 150536 | tf_op jit(solution)/shard_map/ppermute | solution.py:64
  28.3 4.5 %collective-permute-done.14.refs_7_ = bf16[112,224]{1,0:T(8,128)(2,1)S(1)} collective-permute-done((bf16[112,224]{1,0:T(8,128)(2,1)S(1)}, bf16[112,224]{1,0:T(8,128)(2,1)S(1)}, u32[]{:S(2)}, u32[]{:S(2)}) %collective-permute-start.14) | collective-permute-done | bytes 50208 | tf_op jit(solution)/shard_map/ppermute | solution.py:64
  33.2 1.8 %collective-permute-start.4 = (bf16[64,1792]{1,0:T(8,128)(2,1)S(1)}, bf16[64,1792]{1,0:T(8,128)(2,1)S(1)}, u32[]{:S(2)}, u32[]{:S(2)}) collective-permute-start(bf16[64,1792]{1,0:T(8,128)(2,1)S(1)} %collective-permute-done.refs_2_), channel_id=1, source_target_pairs={{0,4},{1,5},{4,8},{5,9},{8,12},{9,13},{12,14},{13,15},{14,10},{15,... | collective-permute-start | bytes 688136 | tf_op jit(solution)/shard_map/ppermute | solution.py:64
  35.1 2.0 %collective-permute-start.6 = (bf16[64,1792]{1,0:T(8,128)(2,1)S(1)}, bf16[64,1792]{1,0:T(8,128)(2,1)S(1)}, u32[]{:S(2)}, u32[]{:S(2)}) collective-permute-start(bf16[64,1792]{1,0:T(8,128)(2,1)S(1)} %collective-permute-done.2.refs_4_), channel_id=1, source_target_pairs={{0,2},{1,3},{4,0},{5,1},{8,4},{9,5},{12,8},{13,9},{14,12},{15,13},... | collective-permute-start | bytes 688136 | tf_op jit(solution)/shard_map/ppermute | solution.py:64
  37.1 4.3 %collective-permute-done.7.refs_9_ = bf16[64,1792]{1,0:T(8,128)(2,1)S(1)} collective-permute-done((bf16[64,1792]{1,0:T(8,128)(2,1)S(1)}, bf16[64,1792]{1,0:T(8,128)(2,1)S(1)}, u32[]{:S(2)}, u32[]{:S(2)}) %collective-permute-start.7) | collective-permute-done | bytes 229408 | tf_op jit(solution)/shard_map/ppermute | solution.py:64
  41.6 1.9 %collective-permute-start.21 = (bf16[64,1792]{1,0:T(8,128)(2,1)S(1)}, bf16[64,1792]{1,0:T(8,128)(2,1)S(1)}, u32[]{:S(2)}, u32[]{:S(2)}) collective-permute-start(bf16[64,1792]{1,0:T(8,128)(2,1)S(1)} %collective-permute-done.4.refs_6_), channel_id=1, source_target_pairs={{0,4},{1,5},{4,8},{5,9},{8,12},{9,13},{12,14},{13,15},{14,10},{15,... | collective-permute-start | bytes 688136 | tf_op jit(solution)/shard_map/ppermute | solution.py:64
  43.5 3.0 %collective-permute-done.5.refs_7_ = bf16[64,1792]{1,0:T(8,128)(2,1)S(1)} collective-permute-done((bf16[64,1792]{1,0:T(8,128)(2,1)S(1)}, bf16[64,1792]{1,0:T(8,128)(2,1)S(1)}, u32[]{:S(2)}, u32[]{:S(2)}) %collective-permute-start.5) | collective-permute-done | bytes 229408 | tf_op jit(solution)/shard_map/ppermute | solution.py:64
  46.6 1.9 %collective-permute-start.22 = (bf16[64,1792]{1,0:T(8,128)(2,1)S(1)}, bf16[64,1792]{1,0:T(8,128)(2,1)S(1)}, u32[]{:S(2)}, u32[]{:S(2)}) collective-permute-start(bf16[64,1792]{1,0:T(8,128)(2,1)S(1)} %collective-permute-done.5.refs_7_), channel_id=1, source_target_pairs={{0,4},{1,5},{4,8},{5,9},{8,12},{9,13},{12,14},{13,15},{14,10},{15,... | collective-permute-start | bytes 688136 | tf_op jit(solution)/shard_map/ppermute | solution.py:64
  48.6 1.8 %shard_map.53.refs_10_ = bf16[640,224]{1,0:T(8,128)(2,1)S(1)} custom-call(bf16[64,1792]{1,0:T(8,128)(2,1)S(1)} %get-tuple-element.29.refs_0_, bf16[64,1792]{1,0:T(8,128)(2,1)S(1)} %get-tuple-element.28.refs_1_, bf16[64,1792]{1,0:T(8,128)(2,1)S(1)} %collective-permute-done.refs_2_, bf16[64,1792]{1,0:T(8,128)(2,1)S(1)} %collective-permute-done.1.refs_3_, ...), custom_call_target="tpu_custom_call" | custom-call | flops 513802240 | bytes 4186112 | tf_op jit(solution)/shard_map/pallas_call | solution.py:33
  50.4 1.6 %collective-permute-start.16 = (bf16[640,224]{1,0:T(8,128)(2,1)S(1)}, bf16[640,224]{1,0:T(8,128)(2,1)S(1)}, u32[]{:S(2)}, u32[]{:S(2)}) collective-permute-start(bf16[640,224]{1,0:T(8,128)(2,1)S(1)} %shard_map.53.refs_10_), channel_id=1, source_target_pairs={{0,16},{16,0},{1,17},{17,1},{2,18},{18,2},{3,19},{19,3},{4,20},{20... | collective-permute-start | bytes 860168 | tf_op jit(solution)/shard_map/ppermute | solution.py:267
  52.5 1.4 %collective-permute-start.25 = (bf16[64,1792]{1,0:T(8,128)(2,1)S(1)}, bf16[64,1792]{1,0:T(8,128)(2,1)S(1)}, u32[]{:S(2)}, u32[]{:S(2)}) collective-permute-start(bf16[64,1792]{1,0:T(8,128)(2,1)S(1)} %collective-permute-done.21.refs_0_), channel_id=1, source_target_pairs={{0,4},{1,5},{4,8},{5,9},{8,12},{9,13},{12,14},{13,15},{14,10},{15,... | collective-permute-start | bytes 688136 | tf_op jit(solution)/shard_map/ppermute | solution.py:64
  53.9 2.4 %collective-permute-done.22.refs_1_ = bf16[64,1792]{1,0:T(8,128)(2,1)S(1)} collective-permute-done((bf16[64,1792]{1,0:T(8,128)(2,1)S(1)}, bf16[64,1792]{1,0:T(8,128)(2,1)S(1)}, u32[]{:S(2)}, u32[]{:S(2)}) %collective-permute-start.22) | collective-permute-done | bytes 229408 | tf_op jit(solution)/shard_map/ppermute | solution.py:64
  57.8 1.6 %collective-permute-start.27 = (bf16[256,224]{1,0:T(8,128)(2,1)S(1)}, bf16[256,224]{1,0:T(8,128)(2,1)S(1)}, u32[]{:S(2)}, u32[]{:S(2)}) collective-permute-start(bf16[256,224]{1,0:T(8,128)(2,1)S(1)} %shard_map.55.refs_6_), channel_id=1, source_target_pairs={{0,16},{16,0},{1,17},{17,1},{2,18},{18,2},{3,19},{19,3},{4,20},{20... | collective-permute-start | bytes 344072 | tf_op jit(solution)/shard_map/ppermute | solution.py:267
  59.3 1.3 collective-permute-done.26.refs_1_.refs_5_
  61.2 1.6 %collective-permute-start.28 = (bf16[128,224]{1,0:T(8,128)(2,1)S(1)}, bf16[128,224]{1,0:T(8,128)(2,1)S(1)}, u32[]{:S(2)}, u32[]{:S(2)}) collective-permute-start(bf16[128,224]{1,0:T(8,128)(2,1)S(1)} %shard_map.56.refs_8_), channel_id=1, source_target_pairs={{0,16},{16,0},{1,17},{17,1},{2,18},{18,2},{3,19},{19,3},{4,20},{20... | collective-permute-start | bytes 172040 | tf_op jit(solution)/shard_map/ppermute | solution.py:267
  63.7 1.9 %collective-permute-done.28.refs_9_ = bf16[128,224]{1,0:T(8,128)(2,1)S(1)} collective-permute-done((bf16[128,224]{1,0:T(8,128)(2,1)S(1)}, bf16[128,224]{1,0:T(8,128)(2,1)S(1)}, u32[]{:S(2)}, u32[]{:S(2)}) %collective-permute-start.28) | collective-permute-done | bytes 57376 | tf_op jit(solution)/shard_map/ppermute | solution.py:267
  66.3 1.5 %collective-permute-start.20 = (bf16[128,224]{1,0:T(8,128)(2,1)S(1)}, bf16[128,224]{1,0:T(8,128)(2,1)S(1)}, u32[]{:S(2)}, u32[]{:S(2)}) collective-permute-start(bf16[128,224]{1,0:T(8,128)(2,1)S(1)} %get-tuple-element.32), channel_id=1, source_target_pairs={{0,8},{1,9},{4,12},{5,13},{8,14},{9,15},{12,10},{13,11},{14,6},{15... | collective-permute-start | bytes 172040 | tf_op jit(solution)/shard_map/ppermute | solution.py:64
  67.8 1.5 %collective-permute-start.19 = (bf16[128,224]{1,0:T(8,128)(2,1)S(1)}, bf16[128,224]{1,0:T(8,128)(2,1)S(1)}, u32[]{:S(2)}, u32[]{:S(2)}) collective-permute-start(bf16[128,224]{1,0:T(8,128)(2,1)S(1)} %get-tuple-element.33), channel_id=1, source_target_pairs={{0,6},{1,7},{4,2},{5,3},{8,0},{9,1},{12,4},{13,5},{14,8},{15,9},{1... | collective-permute-start | bytes 172040 | tf_op jit(solution)/shard_map/ppermute | solution.py:64
  69.3 1.7 %collective-permute-start.18 = (bf16[128,224]{1,0:T(8,128)(2,1)S(1)}, bf16[128,224]{1,0:T(8,128)(2,1)S(1)}, u32[]{:S(2)}, u32[]{:S(2)}) collective-permute-start(bf16[128,224]{1,0:T(8,128)(2,1)S(1)} %get-tuple-element.34), channel_id=1, source_target_pairs={{0,4},{1,5},{4,8},{5,9},{8,12},{9,13},{12,14},{13,15},{14,10},{15,... | collective-permute-start | bytes 172040 | tf_op jit(solution)/shard_map/ppermute | solution.py:64
  71.4 2.4 %collective-permute-start.31 = (bf16[128,224]{1,0:T(8,128)(2,1)S(1)}, bf16[128,224]{1,0:T(8,128)(2,1)S(1)}, u32[]{:S(2)}, u32[]{:S(2)}) collective-permute-start(bf16[128,224]{1,0:T(8,128)(2,1)S(1)} %get-tuple-element.37), channel_id=1, source_target_pairs={{0,14},{1,15},{4,10},{5,11},{8,6},{9,7},{12,2},{13,3},{14,0},{15,1... | collective-permute-start | bytes 172040 | tf_op jit(solution)/shard_map/ppermute | solution.py:64
  73.9 1.4 %collective-permute-start.30 = (bf16[128,224]{1,0:T(8,128)(2,1)S(1)}, bf16[128,224]{1,0:T(8,128)(2,1)S(1)}, u32[]{:S(2)}, u32[]{:S(2)}) collective-permute-start(bf16[128,224]{1,0:T(8,128)(2,1)S(1)} %get-tuple-element.38), channel_id=1, source_target_pairs={{0,12},{1,13},{4,14},{5,15},{8,10},{9,11},{12,6},{13,7},{14,2},{15... | collective-permute-start | bytes 172040 | tf_op jit(solution)/shard_map/ppermute | solution.py:64
  75.3 2.5 %collective-permute-start.29 = (bf16[128,224]{1,0:T(8,128)(2,1)S(1)}, bf16[128,224]{1,0:T(8,128)(2,1)S(1)}, u32[]{:S(2)}, u32[]{:S(2)}) collective-permute-start(bf16[128,224]{1,0:T(8,128)(2,1)S(1)} %get-tuple-element.39), channel_id=1, source_target_pairs={{0,10},{1,11},{4,6},{5,7},{8,2},{9,3},{12,0},{13,1},{14,4},{15,5},... | collective-permute-start | bytes 172040 | tf_op jit(solution)/shard_map/ppermute | solution.py:64
  78.9 2.5 %collective-permute-start.34 = (bf16[112,896]{1,0:T(8,128)(2,1)S(1)}, bf16[112,896]{1,0:T(8,128)(2,1)S(1)}, u32[]{:S(2)}, u32[]{:S(2)}) collective-permute-start(bf16[112,896]{1,0:T(8,128)(2,1)S(1)} %get-tuple-element.30.refs_1_), channel_id=1, source_target_pairs={{0,4},{1,5},{4,8},{5,9},{8,12},{9,13},{12,14},{13,15},{14,10},{15,... | collective-permute-start | bytes 602120 | tf_op jit(solution)/shard_map/ppermute | solution.py:64
  81.5 1.3 collective-permute-done.30.refs_6_
  82.7 1.8 %collective-permute-start.35 = (bf16[112,896]{1,0:T(8,128)(2,1)S(1)}, bf16[112,896]{1,0:T(8,128)(2,1)S(1)}, u32[]{:S(2)}, u32[]{:S(2)}) collective-permute-start(bf16[112,896]{1,0:T(8,128)(2,1)S(1)} %get-tuple-element.31.refs_0_), channel_id=1, source_target_pairs={{0,2},{1,3},{4,0},{5,1},{8,4},{9,5},{12,8},{13,9},{14,12},{15,13},... | collective-permute-start | bytes 602120 | tf_op jit(solution)/shard_map/ppermute | solution.py:64
  84.8 2.3 %collective-permute-done.36.refs_5_ = bf16[112,896]{1,0:T(8,128)(2,1)S(1)} collective-permute-done((bf16[112,896]{1,0:T(8,128)(2,1)S(1)}, bf16[112,896]{1,0:T(8,128)(2,1)S(1)}, u32[]{:S(2)}, u32[]{:S(2)}) %collective-permute-start.36) | collective-permute-done | bytes 200736 | tf_op jit(solution)/shard_map/ppermute | solution.py:64
  87.1 1.5 %collective-permute-start.40 = (bf16[112,896]{1,0:T(8,128)(2,1)S(1)}, bf16[112,896]{1,0:T(8,128)(2,1)S(1)}, u32[]{:S(2)}, u32[]{:S(2)}) collective-permute-start(bf16[112,896]{1,0:T(8,128)(2,1)S(1)} %collective-permute-done.36.refs_5_), channel_id=1, source_target_pairs={{0,2},{1,3},{4,0},{5,1},{8,4},{9,5},{12,8},{13,9},{14,12},{15,13},... | collective-permute-start | bytes 602120 | tf_op jit(solution)/shard_map/ppermute | solution.py:64
  88.6 2.8 %collective-permute-done.35.refs_4_ = bf16[112,896]{1,0:T(8,128)(2,1)S(1)} collective-permute-done((bf16[112,896]{1,0:T(8,128)(2,1)S(1)}, bf16[112,896]{1,0:T(8,128)(2,1)S(1)}, u32[]{:S(2)}, u32[]{:S(2)}) %collective-permute-start.35) | collective-permute-done | bytes 200736 | tf_op jit(solution)/shard_map/ppermute | solution.py:64
  92.2 1.2 collective-permute-start.39
  93.5 2.2 %collective-permute-done.40.refs_9_ = bf16[112,896]{1,0:T(8,128)(2,1)S(1)} collective-permute-done((bf16[112,896]{1,0:T(8,128)(2,1)S(1)}, bf16[112,896]{1,0:T(8,128)(2,1)S(1)}, u32[]{:S(2)}, u32[]{:S(2)}) %collective-permute-start.40) | collective-permute-done | bytes 200736 | tf_op jit(solution)/shard_map/ppermute | solution.py:64
  96.5 1.6 %collective-permute-done.38.refs_7_ = bf16[112,896]{1,0:T(8,128)(2,1)S(1)} collective-permute-done((bf16[112,896]{1,0:T(8,128)(2,1)S(1)}, bf16[112,896]{1,0:T(8,128)(2,1)S(1)}, u32[]{:S(2)}, u32[]{:S(2)}) %collective-permute-start.38) | collective-permute-done | bytes 200736 | tf_op jit(solution)/shard_map/ppermute | solution.py:64
  98.2 1.7 %collective-permute-done.39.refs_8_ = bf16[112,896]{1,0:T(8,128)(2,1)S(1)} collective-permute-done((bf16[112,896]{1,0:T(8,128)(2,1)S(1)}, bf16[112,896]{1,0:T(8,128)(2,1)S(1)}, u32[]{:S(2)}, u32[]{:S(2)}) %collective-permute-start.39) | collective-permute-done | bytes 200736 | tf_op jit(solution)/shard_map/ppermute | solution.py:64
  100.6 2.5 %collective-permute-done.37.refs_6_ = bf16[112,896]{1,0:T(8,128)(2,1)S(1)} collective-permute-done((bf16[112,896]{1,0:T(8,128)(2,1)S(1)}, bf16[112,896]{1,0:T(8,128)(2,1)S(1)}, u32[]{:S(2)}, u32[]{:S(2)}) %collective-permute-start.37) | collective-permute-done | bytes 200736 | tf_op jit(solution)/shard_map/ppermute | solution.py:64
  104.2 1.4 %collective-permute-done.44.refs_13_ = bf16[112,896]{1,0:T(8,128)(2,1)S(1)} collective-permute-done((bf16[112,896]{1,0:T(8,128)(2,1)S(1)}, bf16[112,896]{1,0:T(8,128)(2,1)S(1)}, u32[]{:S(2)}, u32[]{:S(2)}) %collective-permute-start.44) | collective-permute-done | bytes 200736 | tf_op jit(solution)/shard_map/ppermute | solution.py:64
  105.9 1.8 %collective-permute-done.42.refs_11_ = bf16[112,896]{1,0:T(8,128)(2,1)S(1)} collective-permute-done((bf16[112,896]{1,0:T(8,128)(2,1)S(1)}, bf16[112,896]{1,0:T(8,128)(2,1)S(1)}, u32[]{:S(2)}, u32[]{:S(2)}) %collective-permute-start.42) | collective-permute-done | bytes 200736 | tf_op jit(solution)/shard_map/ppermute | solution.py:64
  108.6 3.1 %collective-permute-done.41.refs_10_ = bf16[112,896]{1,0:T(8,128)(2,1)S(1)} collective-permute-done((bf16[112,896]{1,0:T(8,128)(2,1)S(1)}, bf16[112,896]{1,0:T(8,128)(2,1)S(1)}, u32[]{:S(2)}, u32[]{:S(2)}) %collective-permute-start.41) | collective-permute-done | bytes 200736 | tf_op jit(solution)/shard_map/ppermute | solution.py:64
  114.1 2.4 %collective-permute-done.46.refs_15_ = bf16[112,896]{1,0:T(8,128)(2,1)S(1)} collective-permute-done((bf16[112,896]{1,0:T(8,128)(2,1)S(1)}, bf16[112,896]{1,0:T(8,128)(2,1)S(1)}, u32[]{:S(2)}, u32[]{:S(2)}) %collective-permute-start.46) | collective-permute-done | bytes 200736 | tf_op jit(solution)/shard_map/ppermute | solution.py:64
  116.5 1.9 %collective-permute-done.45.refs_14_ = bf16[112,896]{1,0:T(8,128)(2,1)S(1)} collective-permute-done((bf16[112,896]{1,0:T(8,128)(2,1)S(1)}, bf16[112,896]{1,0:T(8,128)(2,1)S(1)}, u32[]{:S(2)}, u32[]{:S(2)}) %collective-permute-start.45) | collective-permute-done | bytes 200736 | tf_op jit(solution)/shard_map/ppermute | solution.py:64
  119.8 13.9 %shard_map.59 = bf16[112,1792]{1,0:T(8,128)(2,1)} custom-call(bf16[112,896]{1,0:T(8,128)(2,1)S(1)} %get-tuple-element.31.refs_0_, bf16[112,896]{1,0:T(8,128)(2,1)S(1)} %get-tuple-element.30.refs_1_, bf16[112,896]{1,0:T(8,128)(2,1)S(1)} %collective-permute-done.33.refs_2_, bf16[112,896]{1,0:T(8,128)(2,1)S(1)} %collective-permute-done.34.refs_3_, ...), custom_call_target="tpu_custom_call" | custom-call | flops 6576668672 | bytes 14163968 | tf_op jit(solution)/shard_map/pallas_call | solution.py:33
  (99 shorter events, 20.1 us)
Async XLA Ops:
  2.7 30.3 %collective-permute-start.3 = (bf16[64,1792]{1,0:T(8,128)(2,1)S(1)}, bf16[64,1792]{1,0:T(8,128)(2,1)S(1)}, u32[]{:S(2)}, u32[]{:S(2)}) collective-permute-start(bf16[64,1792]{1,0:T(8,128)(2,1)S(1)} %get-tuple-element.28.refs_1_), channel_id=1, source_target_pairs={{0,2},{1,3},{4,0},{5,1},{8,4},{9,5},{12,8},{13,9},{14,12},{15,13},... | collective-permute-start | bytes 688136 | tf_op jit(solution)/shard_map/ppermute | solution.py:64
  5.7 27.5 %collective-permute-start = (bf16[64,1792]{1,0:T(8,128)(2,1)S(1)}, bf16[64,1792]{1,0:T(8,128)(2,1)S(1)}, u32[]{:S(2)}, u32[]{:S(2)}) collective-permute-start(bf16[64,1792]{1,0:T(8,128)(2,1)S(1)} %get-tuple-element.29.refs_0_), channel_id=1, source_target_pairs={{0,4},{1,5},{4,8},{5,9},{8,12},{9,13},{12,14},{13,15},{14,10},{15,... | collective-permute-start | bytes 688136 | tf_op jit(solution)/shard_map/ppermute | solution.py:64
  6.1 7.7 %collective-permute-start.8 = (bf16[112,224]{1,0:T(8,128)(2,1)S(1)}, bf16[112,224]{1,0:T(8,128)(2,1)S(1)}, u32[]{:S(2)}, u32[]{:S(2)}) collective-permute-start(bf16[112,224]{1,0:T(8,128)(2,1)S(1)} %get-tuple-element.16), channel_id=1, source_target_pairs={{0,2},{1,3},{4,0},{5,1},{8,4},{9,5},{12,8},{13,9},{14,12},{15,13},... | collective-permute-start | bytes 150536 | tf_op jit(solution)/shard_map/ppermute | solution.py:64
  8.0 7.9 %collective-permute-start.9 = (bf16[112,224]{1,0:T(8,128)(2,1)S(1)}, bf16[112,224]{1,0:T(8,128)(2,1)S(1)}, u32[]{:S(2)}, u32[]{:S(2)}) collective-permute-start(bf16[112,224]{1,0:T(8,128)(2,1)S(1)} %get-tuple-element.17), channel_id=1, source_target_pairs={{0,4},{1,5},{4,8},{5,9},{8,12},{9,13},{12,14},{13,15},{14,10},{15,... | collective-permute-start | bytes 150536 | tf_op jit(solution)/shard_map/ppermute | solution.py:64
  8.1 10.5 %collective-permute-start.10 = (bf16[112,224]{1,0:T(8,128)(2,1)S(1)}, bf16[112,224]{1,0:T(8,128)(2,1)S(1)}, u32[]{:S(2)}, u32[]{:S(2)}) collective-permute-start(bf16[112,224]{1,0:T(8,128)(2,1)S(1)} %get-tuple-element.18), channel_id=1, source_target_pairs={{0,6},{1,7},{4,2},{5,3},{8,0},{9,1},{12,4},{13,5},{14,8},{15,9},{1... | collective-permute-start | bytes 150536 | tf_op jit(solution)/shard_map/ppermute | solution.py:64
  13.7 6.1 %collective-permute-start.11 = (bf16[112,224]{1,0:T(8,128)(2,1)S(1)}, bf16[112,224]{1,0:T(8,128)(2,1)S(1)}, u32[]{:S(2)}, u32[]{:S(2)}) collective-permute-start(bf16[112,224]{1,0:T(8,128)(2,1)S(1)} %get-tuple-element.19), channel_id=1, source_target_pairs={{0,8},{1,9},{4,12},{5,13},{8,14},{9,15},{12,10},{13,11},{14,6},{15... | collective-permute-start | bytes 150536 | tf_op jit(solution)/shard_map/ppermute | solution.py:64
  16.0 6.6 %collective-permute-start.12 = (bf16[112,224]{1,0:T(8,128)(2,1)S(1)}, bf16[112,224]{1,0:T(8,128)(2,1)S(1)}, u32[]{:S(2)}, u32[]{:S(2)}) collective-permute-start(bf16[112,224]{1,0:T(8,128)(2,1)S(1)} %get-tuple-element.20), channel_id=1, source_target_pairs={{0,10},{1,11},{4,6},{5,7},{8,2},{9,3},{12,0},{13,1},{14,4},{15,5},... | collective-permute-start | bytes 150536 | tf_op jit(solution)/shard_map/ppermute | solution.py:64
  18.6 7.3 %collective-permute-start.13 = (bf16[112,224]{1,0:T(8,128)(2,1)S(1)}, bf16[112,224]{1,0:T(8,128)(2,1)S(1)}, u32[]{:S(2)}, u32[]{:S(2)}) collective-permute-start(bf16[112,224]{1,0:T(8,128)(2,1)S(1)} %get-tuple-element.21), channel_id=1, source_target_pairs={{0,12},{1,13},{4,14},{5,15},{8,10},{9,11},{12,6},{13,7},{14,2},{15... | collective-permute-start | bytes 150536 | tf_op jit(solution)/shard_map/ppermute | solution.py:64
  19.8 15.3 %collective-permute-start.1 = (bf16[64,1792]{1,0:T(8,128)(2,1)S(1)}, bf16[64,1792]{1,0:T(8,128)(2,1)S(1)}, u32[]{:S(2)}, u32[]{:S(2)}) collective-permute-start(bf16[64,1792]{1,0:T(8,128)(2,1)S(1)} %get-tuple-element.28.refs_1_), channel_id=1, source_target_pairs={{0,4},{1,5},{4,8},{5,9},{8,12},{9,13},{12,14},{13,15},{14,10},{15,... | collective-permute-start | bytes 688136 | tf_op jit(solution)/shard_map/ppermute | solution.py:64
  22.6 12.6 %collective-permute-start.2 = (bf16[64,1792]{1,0:T(8,128)(2,1)S(1)}, bf16[64,1792]{1,0:T(8,128)(2,1)S(1)}, u32[]{:S(2)}, u32[]{:S(2)}) collective-permute-start(bf16[64,1792]{1,0:T(8,128)(2,1)S(1)} %get-tuple-element.29.refs_0_), channel_id=1, source_target_pairs={{0,2},{1,3},{4,0},{5,1},{8,4},{9,5},{12,8},{13,9},{14,12},{15,13},... | collective-permute-start | bytes 688136 | tf_op jit(solution)/shard_map/ppermute | solution.py:64
  25.9 6.9 %collective-permute-start.14 = (bf16[112,224]{1,0:T(8,128)(2,1)S(1)}, bf16[112,224]{1,0:T(8,128)(2,1)S(1)}, u32[]{:S(2)}, u32[]{:S(2)}) collective-permute-start(bf16[112,224]{1,0:T(8,128)(2,1)S(1)} %get-tuple-element.22), channel_id=1, source_target_pairs={{0,14},{1,15},{4,10},{5,11},{8,6},{9,7},{12,2},{13,3},{14,0},{15,1... | collective-permute-start | bytes 150536 | tf_op jit(solution)/shard_map/ppermute | solution.py:64
  32.9 15.7 %collective-permute-start.15 = (bf16[896,224]{1,0:T(8,128)(2,1)S(1)}, bf16[896,224]{1,0:T(8,128)(2,1)S(1)}, u32[]{:S(2)}, u32[]{:S(2)}) collective-permute-start(bf16[896,224]{1,0:T(8,128)(2,1)S(1)} %shard_map.52.refs_10_.refs_4_.refs_2_), channel_id=1, source_target_pairs={{0,1},{1,0},{2,3},{3,2},{4,5},{5,4},{6,7},{7,6},{8,9},{9,8},{10,11... | collective-permute-start | bytes 1204232 | tf_op jit(solution)/shard_map/ppermute | solution.py:246
  33.0 8.5 %collective-permute-start.7 = (bf16[64,1792]{1,0:T(8,128)(2,1)S(1)}, bf16[64,1792]{1,0:T(8,128)(2,1)S(1)}, u32[]{:S(2)}, u32[]{:S(2)}) collective-permute-start(bf16[64,1792]{1,0:T(8,128)(2,1)S(1)} %collective-permute-done.3.refs_5_), channel_id=1, source_target_pairs={{0,2},{1,3},{4,0},{5,1},{8,4},{9,5},{12,8},{13,9},{14,12},{15,13},... | collective-permute-start | bytes 688136 | tf_op jit(solution)/shard_map/ppermute | solution.py:64
  33.2 8.4 %collective-permute-start.4 = (bf16[64,1792]{1,0:T(8,128)(2,1)S(1)}, bf16[64,1792]{1,0:T(8,128)(2,1)S(1)}, u32[]{:S(2)}, u32[]{:S(2)}) collective-permute-start(bf16[64,1792]{1,0:T(8,128)(2,1)S(1)} %collective-permute-done.refs_2_), channel_id=1, source_target_pairs={{0,4},{1,5},{4,8},{5,9},{8,12},{9,13},{12,14},{13,15},{14,10},{15,... | collective-permute-start | bytes 688136 | tf_op jit(solution)/shard_map/ppermute | solution.py:64
  35.1 11.5 %collective-permute-start.5 = (bf16[64,1792]{1,0:T(8,128)(2,1)S(1)}, bf16[64,1792]{1,0:T(8,128)(2,1)S(1)}, u32[]{:S(2)}, u32[]{:S(2)}) collective-permute-start(bf16[64,1792]{1,0:T(8,128)(2,1)S(1)} %collective-permute-done.1.refs_3_), channel_id=1, source_target_pairs={{0,4},{1,5},{4,8},{5,9},{8,12},{9,13},{12,14},{13,15},{14,10},{15,... | collective-permute-start | bytes 688136 | tf_op jit(solution)/shard_map/ppermute | solution.py:64
  35.1 13.3 %collective-permute-start.6 = (bf16[64,1792]{1,0:T(8,128)(2,1)S(1)}, bf16[64,1792]{1,0:T(8,128)(2,1)S(1)}, u32[]{:S(2)}, u32[]{:S(2)}) collective-permute-start(bf16[64,1792]{1,0:T(8,128)(2,1)S(1)} %collective-permute-done.2.refs_4_), channel_id=1, source_target_pairs={{0,2},{1,3},{4,0},{5,1},{8,4},{9,5},{12,8},{13,9},{14,12},{15,13},... | collective-permute-start | bytes 688136 | tf_op jit(solution)/shard_map/ppermute | solution.py:64
  41.4 10.5 %collective-permute-start.24 = (bf16[64,1792]{1,0:T(8,128)(2,1)S(1)}, bf16[64,1792]{1,0:T(8,128)(2,1)S(1)}, u32[]{:S(2)}, u32[]{:S(2)}) collective-permute-start(bf16[64,1792]{1,0:T(8,128)(2,1)S(1)} %collective-permute-done.7.refs_9_), channel_id=1, source_target_pairs={{0,2},{1,3},{4,0},{5,1},{8,4},{9,5},{12,8},{13,9},{14,12},{15,13},... | collective-permute-start | bytes 688136 | tf_op jit(solution)/shard_map/ppermute | solution.py:64
  41.6 10.9 %collective-permute-start.21 = (bf16[64,1792]{1,0:T(8,128)(2,1)S(1)}, bf16[64,1792]{1,0:T(8,128)(2,1)S(1)}, u32[]{:S(2)}, u32[]{:S(2)}) collective-permute-start(bf16[64,1792]{1,0:T(8,128)(2,1)S(1)} %collective-permute-done.4.refs_6_), channel_id=1, source_target_pairs={{0,4},{1,5},{4,8},{5,9},{8,12},{9,13},{12,14},{13,15},{14,10},{15,... | collective-permute-start | bytes 688136 | tf_op jit(solution)/shard_map/ppermute | solution.py:64
  46.6 9.8 %collective-permute-start.22 = (bf16[64,1792]{1,0:T(8,128)(2,1)S(1)}, bf16[64,1792]{1,0:T(8,128)(2,1)S(1)}, u32[]{:S(2)}, u32[]{:S(2)}) collective-permute-start(bf16[64,1792]{1,0:T(8,128)(2,1)S(1)} %collective-permute-done.5.refs_7_), channel_id=1, source_target_pairs={{0,4},{1,5},{4,8},{5,9},{8,12},{9,13},{12,14},{13,15},{14,10},{15,... | collective-permute-start | bytes 688136 | tf_op jit(solution)/shard_map/ppermute | solution.py:64
  48.4 8.5 %collective-permute-start.23 = (bf16[64,1792]{1,0:T(8,128)(2,1)S(1)}, bf16[64,1792]{1,0:T(8,128)(2,1)S(1)}, u32[]{:S(2)}, u32[]{:S(2)}) collective-permute-start(bf16[64,1792]{1,0:T(8,128)(2,1)S(1)} %collective-permute-done.6.refs_8_), channel_id=1, source_target_pairs={{0,2},{1,3},{4,0},{5,1},{8,4},{9,5},{12,8},{13,9},{14,12},{15,13},... | collective-permute-start | bytes 688136 | tf_op jit(solution)/shard_map/ppermute | solution.py:64
  50.4 12.4 %collective-permute-start.16 = (bf16[640,224]{1,0:T(8,128)(2,1)S(1)}, bf16[640,224]{1,0:T(8,128)(2,1)S(1)}, u32[]{:S(2)}, u32[]{:S(2)}) collective-permute-start(bf16[640,224]{1,0:T(8,128)(2,1)S(1)} %shard_map.53.refs_10_), channel_id=1, source_target_pairs={{0,16},{16,0},{1,17},{17,1},{2,18},{18,2},{3,19},{19,3},{4,20},{20... | collective-permute-start | bytes 860168 | tf_op jit(solution)/shard_map/ppermute | solution.py:267
  51.9 8.7 %collective-permute-start.26 = (bf16[64,1792]{1,0:T(8,128)(2,1)S(1)}, bf16[64,1792]{1,0:T(8,128)(2,1)S(1)}, u32[]{:S(2)}, u32[]{:S(2)}) collective-permute-start(bf16[64,1792]{1,0:T(8,128)(2,1)S(1)} %collective-permute-done.24.refs_3_), channel_id=1, source_target_pairs={{0,2},{1,3},{4,0},{5,1},{8,4},{9,5},{12,8},{13,9},{14,12},{15,13},... | collective-permute-start | bytes 688136 | tf_op jit(solution)/shard_map/ppermute | solution.py:64
  52.5 8.2 %collective-permute-start.25 = (bf16[64,1792]{1,0:T(8,128)(2,1)S(1)}, bf16[64,1792]{1,0:T(8,128)(2,1)S(1)}, u32[]{:S(2)}, u32[]{:S(2)}) collective-permute-start(bf16[64,1792]{1,0:T(8,128)(2,1)S(1)} %collective-permute-done.21.refs_0_), channel_id=1, source_target_pairs={{0,4},{1,5},{4,8},{5,9},{8,12},{9,13},{12,14},{13,15},{14,10},{15,... | collective-permute-start | bytes 688136 | tf_op jit(solution)/shard_map/ppermute | solution.py:64
  66.3 7.5 %collective-permute-start.20 = (bf16[128,224]{1,0:T(8,128)(2,1)S(1)}, bf16[128,224]{1,0:T(8,128)(2,1)S(1)}, u32[]{:S(2)}, u32[]{:S(2)}) collective-permute-start(bf16[128,224]{1,0:T(8,128)(2,1)S(1)} %get-tuple-element.32), channel_id=1, source_target_pairs={{0,8},{1,9},{4,12},{5,13},{8,14},{9,15},{12,10},{13,11},{14,6},{15... | collective-permute-start | bytes 172040 | tf_op jit(solution)/shard_map/ppermute | solution.py:64
  67.8 7.5 %collective-permute-start.19 = (bf16[128,224]{1,0:T(8,128)(2,1)S(1)}, bf16[128,224]{1,0:T(8,128)(2,1)S(1)}, u32[]{:S(2)}, u32[]{:S(2)}) collective-permute-start(bf16[128,224]{1,0:T(8,128)(2,1)S(1)} %get-tuple-element.33), channel_id=1, source_target_pairs={{0,6},{1,7},{4,2},{5,3},{8,0},{9,1},{12,4},{13,5},{14,8},{15,9},{1... | collective-permute-start | bytes 172040 | tf_op jit(solution)/shard_map/ppermute | solution.py:64
  69.3 8.5 %collective-permute-start.18 = (bf16[128,224]{1,0:T(8,128)(2,1)S(1)}, bf16[128,224]{1,0:T(8,128)(2,1)S(1)}, u32[]{:S(2)}, u32[]{:S(2)}) collective-permute-start(bf16[128,224]{1,0:T(8,128)(2,1)S(1)} %get-tuple-element.34), channel_id=1, source_target_pairs={{0,4},{1,5},{4,8},{5,9},{8,12},{9,13},{12,14},{13,15},{14,10},{15,... | collective-permute-start | bytes 172040 | tf_op jit(solution)/shard_map/ppermute | solution.py:64
  71.0 6.9 %collective-permute-start.17 = (bf16[128,224]{1,0:T(8,128)(2,1)S(1)}, bf16[128,224]{1,0:T(8,128)(2,1)S(1)}, u32[]{:S(2)}, u32[]{:S(2)}) collective-permute-start(bf16[128,224]{1,0:T(8,128)(2,1)S(1)} %get-tuple-element.35), channel_id=1, source_target_pairs={{0,2},{1,3},{4,0},{5,1},{8,4},{9,5},{12,8},{13,9},{14,12},{15,13},... | collective-permute-start | bytes 172040 | tf_op jit(solution)/shard_map/ppermute | solution.py:64
  71.4 7.6 %collective-permute-start.31 = (bf16[128,224]{1,0:T(8,128)(2,1)S(1)}, bf16[128,224]{1,0:T(8,128)(2,1)S(1)}, u32[]{:S(2)}, u32[]{:S(2)}) collective-permute-start(bf16[128,224]{1,0:T(8,128)(2,1)S(1)} %get-tuple-element.37), channel_id=1, source_target_pairs={{0,14},{1,15},{4,10},{5,11},{8,6},{9,7},{12,2},{13,3},{14,0},{15,1... | collective-permute-start | bytes 172040 | tf_op jit(solution)/shard_map/ppermute | solution.py:64
  73.9 8.8 %collective-permute-start.30 = (bf16[128,224]{1,0:T(8,128)(2,1)S(1)}, bf16[128,224]{1,0:T(8,128)(2,1)S(1)}, u32[]{:S(2)}, u32[]{:S(2)}) collective-permute-start(bf16[128,224]{1,0:T(8,128)(2,1)S(1)} %get-tuple-element.38), channel_id=1, source_target_pairs={{0,12},{1,13},{4,14},{5,15},{8,10},{9,11},{12,6},{13,7},{14,2},{15... | collective-permute-start | bytes 172040 | tf_op jit(solution)/shard_map/ppermute | solution.py:64
  75.3 7.5 %collective-permute-start.29 = (bf16[128,224]{1,0:T(8,128)(2,1)S(1)}, bf16[128,224]{1,0:T(8,128)(2,1)S(1)}, u32[]{:S(2)}, u32[]{:S(2)}) collective-permute-start(bf16[128,224]{1,0:T(8,128)(2,1)S(1)} %get-tuple-element.39), channel_id=1, source_target_pairs={{0,10},{1,11},{4,6},{5,7},{8,2},{9,3},{12,0},{13,1},{14,4},{15,5},... | collective-permute-start | bytes 172040 | tf_op jit(solution)/shard_map/ppermute | solution.py:64
  77.8 6.7 %collective-permute-start.48 = (bf16[112,896]{1,0:T(8,128)(2,1)S(1)}, bf16[112,896]{1,0:T(8,128)(2,1)S(1)}, u32[]{:S(2)}, u32[]{:S(2)}) collective-permute-start(bf16[112,896]{1,0:T(8,128)(2,1)S(1)} %get-tuple-element.30.refs_1_), channel_id=1, source_target_pairs={{0,1},{1,0},{2,3},{3,2},{4,5},{5,4},{6,7},{7,6},{8,9},{9,8},{10,11... | collective-permute-start | bytes 602120 | tf_op jit(solution)/shard_map/ppermute | solution.py:296
  77.9 9.2 %collective-permute-start.36 = (bf16[112,896]{1,0:T(8,128)(2,1)S(1)}, bf16[112,896]{1,0:T(8,128)(2,1)S(1)}, u32[]{:S(2)}, u32[]{:S(2)}) collective-permute-start(bf16[112,896]{1,0:T(8,128)(2,1)S(1)} %get-tuple-element.30.refs_1_), channel_id=1, source_target_pairs={{0,2},{1,3},{4,0},{5,1},{8,4},{9,5},{12,8},{13,9},{14,12},{15,13},... | collective-permute-start | bytes 602120 | tf_op jit(solution)/shard_map/ppermute | solution.py:64
  78.9 8.1 %collective-permute-start.34 = (bf16[112,896]{1,0:T(8,128)(2,1)S(1)}, bf16[112,896]{1,0:T(8,128)(2,1)S(1)}, u32[]{:S(2)}, u32[]{:S(2)}) collective-permute-start(bf16[112,896]{1,0:T(8,128)(2,1)S(1)} %get-tuple-element.30.refs_1_), channel_id=1, source_target_pairs={{0,4},{1,5},{4,8},{5,9},{8,12},{9,13},{12,14},{13,15},{14,10},{15,... | collective-permute-start | bytes 602120 | tf_op jit(solution)/shard_map/ppermute | solution.py:64
  82.7 8.6 %collective-permute-start.35 = (bf16[112,896]{1,0:T(8,128)(2,1)S(1)}, bf16[112,896]{1,0:T(8,128)(2,1)S(1)}, u32[]{:S(2)}, u32[]{:S(2)}) collective-permute-start(bf16[112,896]{1,0:T(8,128)(2,1)S(1)} %get-tuple-element.31.refs_0_), channel_id=1, source_target_pairs={{0,2},{1,3},{4,0},{5,1},{8,4},{9,5},{12,8},{13,9},{14,12},{15,13},... | collective-permute-start | bytes 602120 | tf_op jit(solution)/shard_map/ppermute | solution.py:64
  84.5 7.7 %collective-permute-start.33 = (bf16[112,896]{1,0:T(8,128)(2,1)S(1)}, bf16[112,896]{1,0:T(8,128)(2,1)S(1)}, u32[]{:S(2)}, u32[]{:S(2)}) collective-permute-start(bf16[112,896]{1,0:T(8,128)(2,1)S(1)} %get-tuple-element.31.refs_0_), channel_id=1, source_target_pairs={{0,4},{1,5},{4,8},{5,9},{8,12},{9,13},{12,14},{13,15},{14,10},{15,... | collective-permute-start | bytes 602120 | tf_op jit(solution)/shard_map/ppermute | solution.py:64
  87.1 8.6 %collective-permute-start.40 = (bf16[112,896]{1,0:T(8,128)(2,1)S(1)}, bf16[112,896]{1,0:T(8,128)(2,1)S(1)}, u32[]{:S(2)}, u32[]{:S(2)}) collective-permute-start(bf16[112,896]{1,0:T(8,128)(2,1)S(1)} %collective-permute-done.36.refs_5_), channel_id=1, source_target_pairs={{0,2},{1,3},{4,0},{5,1},{8,4},{9,5},{12,8},{13,9},{14,12},{15,13},... | collective-permute-start | bytes 602120 | tf_op jit(solution)/shard_map/ppermute | solution.py:64
  88.6 7.1 %collective-permute-start.50 = (bf16[112,896]{1,0:T(8,128)(2,1)S(1)}, bf16[112,896]{1,0:T(8,128)(2,1)S(1)}, u32[]{:S(2)}, u32[]{:S(2)}) collective-permute-start(bf16[112,896]{1,0:T(8,128)(2,1)S(1)} %collective-permute-done.34.refs_3_), channel_id=1, source_target_pairs={{0,1},{1,0},{2,3},{3,2},{4,5},{5,4},{6,7},{7,6},{8,9},{9,8},{10,11... | collective-permute-start | bytes 602120 | tf_op jit(solution)/shard_map/ppermute | solution.py:296
  91.4 6.8 %collective-permute-start.38 = (bf16[112,896]{1,0:T(8,128)(2,1)S(1)}, bf16[112,896]{1,0:T(8,128)(2,1)S(1)}, u32[]{:S(2)}, u32[]{:S(2)}) collective-permute-start(bf16[112,896]{1,0:T(8,128)(2,1)S(1)} %collective-permute-done.34.refs_3_), channel_id=1, source_target_pairs={{0,4},{1,5},{4,8},{5,9},{8,12},{9,13},{12,14},{13,15},{14,10},{15,... | collective-permute-start | bytes 602120 | tf_op jit(solution)/shard_map/ppermute | solution.py:64
  92.2 7.6 %collective-permute-start.39 = (bf16[112,896]{1,0:T(8,128)(2,1)S(1)}, bf16[112,896]{1,0:T(8,128)(2,1)S(1)}, u32[]{:S(2)}, u32[]{:S(2)}) collective-permute-start(bf16[112,896]{1,0:T(8,128)(2,1)S(1)} %collective-permute-done.35.refs_4_), channel_id=1, source_target_pairs={{0,2},{1,3},{4,0},{5,1},{8,4},{9,5},{12,8},{13,9},{14,12},{15,13},... | collective-permute-start | bytes 602120 | tf_op jit(solution)/shard_map/ppermute | solution.py:64
  95.7 7.4 %collective-permute-start.37 = (bf16[112,896]{1,0:T(8,128)(2,1)S(1)}, bf16[112,896]{1,0:T(8,128)(2,1)S(1)}, u32[]{:S(2)}, u32[]{:S(2)}) collective-permute-start(bf16[112,896]{1,0:T(8,128)(2,1)S(1)} %collective-permute-done.33.refs_2_), channel_id=1, source_target_pairs={{0,4},{1,5},{4,8},{5,9},{8,12},{9,13},{12,14},{13,15},{14,10},{15,... | collective-permute-start | bytes 602120 | tf_op jit(solution)/shard_map/ppermute | solution.py:64
  98.2 7.4 %collective-permute-start.44 = (bf16[112,896]{1,0:T(8,128)(2,1)S(1)}, bf16[112,896]{1,0:T(8,128)(2,1)S(1)}, u32[]{:S(2)}, u32[]{:S(2)}) collective-permute-start(bf16[112,896]{1,0:T(8,128)(2,1)S(1)} %collective-permute-done.40.refs_9_), channel_id=1, source_target_pairs={{0,2},{1,3},{4,0},{5,1},{8,4},{9,5},{12,8},{13,9},{14,12},{15,13},... | collective-permute-start | bytes 602120 | tf_op jit(solution)/shard_map/ppermute | solution.py:64
  99.9 7.8 %collective-permute-start.42 = (bf16[112,896]{1,0:T(8,128)(2,1)S(1)}, bf16[112,896]{1,0:T(8,128)(2,1)S(1)}, u32[]{:S(2)}, u32[]{:S(2)}) collective-permute-start(bf16[112,896]{1,0:T(8,128)(2,1)S(1)} %collective-permute-done.38.refs_7_), channel_id=1, source_target_pairs={{0,4},{1,5},{4,8},{5,9},{8,12},{9,13},{12,14},{13,15},{14,10},{15,... | collective-permute-start | bytes 602120 | tf_op jit(solution)/shard_map/ppermute | solution.py:64
  103.1 8.6 %collective-permute-start.41 = (bf16[112,896]{1,0:T(8,128)(2,1)S(1)}, bf16[112,896]{1,0:T(8,128)(2,1)S(1)}, u32[]{:S(2)}, u32[]{:S(2)}) collective-permute-start(bf16[112,896]{1,0:T(8,128)(2,1)S(1)} %collective-permute-done.37.refs_6_), channel_id=1, source_target_pairs={{0,4},{1,5},{4,8},{5,9},{8,12},{9,13},{12,14},{13,15},{14,10},{15,... | collective-permute-start | bytes 602120 | tf_op jit(solution)/shard_map/ppermute | solution.py:64
  105.6 7.9 %collective-permute-start.43 = (bf16[112,896]{1,0:T(8,128)(2,1)S(1)}, bf16[112,896]{1,0:T(8,128)(2,1)S(1)}, u32[]{:S(2)}, u32[]{:S(2)}) collective-permute-start(bf16[112,896]{1,0:T(8,128)(2,1)S(1)} %collective-permute-done.39.refs_8_), channel_id=1, source_target_pairs={{0,2},{1,3},{4,0},{5,1},{8,4},{9,5},{12,8},{13,9},{14,12},{15,13},... | collective-permute-start | bytes 602120 | tf_op jit(solution)/shard_map/ppermute | solution.py:64
  105.9 7.6 %collective-permute-start.53 = (bf16[112,896]{1,0:T(8,128)(2,1)S(1)}, bf16[112,896]{1,0:T(8,128)(2,1)S(1)}, u32[]{:S(2)}, u32[]{:S(2)}) collective-permute-start(bf16[112,896]{1,0:T(8,128)(2,1)S(1)} %collective-permute-done.37.refs_6_), channel_id=1, source_target_pairs={{0,1},{1,0},{2,3},{3,2},{4,5},{5,4},{6,7},{7,6},{8,9},{9,8},{10,11... | collective-permute-start | bytes 602120 | tf_op jit(solution)/shard_map/ppermute | solution.py:296
  107.7 6.3 %collective-permute-start.60 = (bf16[112,896]{1,0:T(8,128)(2,1)S(1)}, bf16[112,896]{1,0:T(8,128)(2,1)S(1)}, u32[]{:S(2)}, u32[]{:S(2)}) collective-permute-start(bf16[112,896]{1,0:T(8,128)(2,1)S(1)} %collective-permute-done.44.refs_13_), channel_id=1, source_target_pairs={{0,1},{1,0},{2,3},{3,2},{4,5},{5,4},{6,7},{7,6},{8,9},{9,8},{10,11... | collective-permute-start | bytes 602120 | tf_op jit(solution)/shard_map/ppermute | solution.py:296
  107.7 8.8 %collective-permute-start.46 = (bf16[112,896]{1,0:T(8,128)(2,1)S(1)}, bf16[112,896]{1,0:T(8,128)(2,1)S(1)}, u32[]{:S(2)}, u32[]{:S(2)}) collective-permute-start(bf16[112,896]{1,0:T(8,128)(2,1)S(1)} %collective-permute-done.44.refs_13_), channel_id=1, source_target_pairs={{0,2},{1,3},{4,0},{5,1},{8,4},{9,5},{12,8},{13,9},{14,12},{15,13},... | collective-permute-start | bytes 602120 | tf_op jit(solution)/shard_map/ppermute | solution.py:64
  111.7 6.7 %collective-permute-start.45 = (bf16[112,896]{1,0:T(8,128)(2,1)S(1)}, bf16[112,896]{1,0:T(8,128)(2,1)S(1)}, u32[]{:S(2)}, u32[]{:S(2)}) collective-permute-start(bf16[112,896]{1,0:T(8,128)(2,1)S(1)} %collective-permute-done.41.refs_10_), channel_id=1, source_target_pairs={{0,4},{1,5},{4,8},{5,9},{8,12},{9,13},{12,14},{13,15},{14,10},{15,... | collective-permute-start | bytes 602120 | tf_op jit(solution)/shard_map/ppermute | solution.py:64
  (18 other events, 78.7 us)

commit v3 on v2

--- a/solution.py
+++ b/solution.py
@@ -10,6 +10,7 @@
 
 BF16 = jnp.bfloat16
 F32 = jnp.float32
+STREAMS = ((1, 0), (1, 1), (-1, 0), (-1, 1))
 VMEM = pl.BlockSpec(memory_space=pltpu.VMEM)
 SMEM = pl.BlockSpec(memory_space=pltpu.SMEM)
 
@@ -75,6 +76,27 @@
     return blocks
 
 
+def halve_kernel(ahead_ref, behind_ref, upper_ref, lower_ref):
+    half = upper_ref.shape[0]
+    upper_ref[...] = ahead_ref[:half]
+    lower_ref[...] = behind_ref[half:]
+
+
+def ring_whole(block, chips):
+    blocks, ahead, behind = [[block]], block, block
+    for _ in range(chips // 2 - 1):
+        ahead, behind = shift(ahead, 1, chips), shift(behind, -1, chips)
+        blocks += [[ahead], [behind]]
+    rows, width = block.shape
+    upper, lower = call(halve_kernel, [shape((rows // 2, width), BF16)] * 2, [], [ahead, behind])
+    blocks.append([shift(upper, 1, chips), shift(lower, -1, chips)])
+    return blocks
+
+
+def tie(arrays, others):
+    return lax.optimization_barrier((arrays, others))[0]
+
+
 def ring_offsets(chips):
     near = [sign * step for step in range(1, chips // 2) for sign in (-1, 1)]
     return [0] + near + [chips // 2]
@@ -86,38 +108,67 @@
     out_ref[...] = contract(picks.astype(BF16), rows_ref[...], 0, 0).astype(BF16)
 
 
-def pieces_kernel(chips, rows_ref, *refs):
-    outs, held = refs[:chips], refs[chips]
+def cut_kernel(chips, rows_ref, out_ref):
+    cols = out_ref.shape[2]
+    for chip in range(chips):
+        out_ref[chip] = rows_ref[:, chip * cols : (chip + 1) * cols]
+
+
+def fold(rows, groups):
+    size = rows.shape[0] // groups
+    return [rows[i * size : (i + 1) * size] for i in range(groups)]
+
+
+def pack_kernel(chips, count, keep_ref, come_ref, early_ref, late_ref, *outs):
+    first_ref, second_ref, *streams = outs
+    slab, half = first_ref.shape
+    groups, offsets = chips // 2, ring_offsets(chips)
+    own = (keep_ref[...] + come_ref[...].astype(F32)).astype(BF16)
+    cols = half // groups
+    blocks = [early_ref[i : i + count] for i in range(0, early_ref.shape[0], count)]
+    blocks += [late_ref[i : i + count] for i in range(0, late_ref.shape[0], count)]
+    for ref, (sign, side) in zip(streams, STREAMS, strict=True):
+        ref[:slab] = own[:, side * half : (side + 1) * half]
+        last = chips // 2 if (sign == 1) == (side == 0) else chips // 2 - 1
+        row = slab
+        for step in range(last, 0, -1):
+            block = blocks[offsets.index(sign * step if step < chips // 2 else step)]
+            parts = fold(block[side * count // 2 : (side + 1) * count // 2], groups)
+            for i, part in enumerate(parts):
+                ref[row : row + part.shape[0], i * cols : (i + 1) * cols] = part
+            row += parts[0].shape[0]
+    first_ref[...] = own[:, :half]
+    second_ref[...] = own[:, half:]
+
+
+def trim_kernel(message_ref, block_ref, piece_ref, *rest_ref):
+    slab, size = block_ref.shape[0], piece_ref.shape[0]
+    rest = message_ref.shape[0] - size
+    block_ref[...] = message_ref[:slab]
+    piece_ref[...] = message_ref[rest:]
+    for ref in rest_ref:
+        ref[...] = message_ref[:rest]
+
+
+def join_kernel(chips, slab, places, first_ref, *refs):
+    pieces, out_ref, held = refs[:-2], refs[-2], refs[-1]
     _, _, position = me(chips)
-    cols = held.shape[2]
-    for chip in range(chips):
-        held[chip] = rows_ref[:, chip * cols : (chip + 1) * cols]
-    for out, offset in zip(outs, ring_offsets(chips), strict=True):
-        out[...] = held[chip_at((position + offset + chips) % chips, chips)]
-
-
-def stack_kernel(chips, *refs):
-    pieces, out_ref = refs[:chips], refs[chips]
-    _, _, position = me(chips)
-    slab = pieces[0].shape[0]
-    for piece, offset in zip(pieces, ring_offsets(chips), strict=True):
-        chip = chip_at((position - offset + chips) % chips, chips)
-        out_ref[pl.ds(pl.multiple_of(chip * slab, 16), slab), :] = piece[...]
-
-
-def join_kernel(chips, *refs):
-    pieces, out_ref, held = refs[:chips], refs[chips], refs[chips + 1]
-    _, _, position = me(chips)
-    cols = held.shape[2]
-    for piece, offset in zip(pieces, ring_offsets(chips), strict=True):
-        held[chip_at((position - offset + chips) % chips, chips)] = piece[...]
+    count, cols = held.shape[1:]
+    groups = chips // 2
+    size = count // 2 // groups
+    held[chip_at(position, chips)] = first_ref[...]
+    for ref, (offset, side) in zip(pieces, places, strict=True):
+        chip = chip_at((position + offset + chips) % chips, chips)
+        piece = ref[ref.shape[0] - size :]
+        for j in range(groups):
+            base = side * count // 2 + j * size
+            held[chip, base : base + size, :] = piece[:, j * cols : (j + 1) * cols]
     for chip in range(chips):
         out_ref[:, chip * cols : (chip + 1) * cols] = held[chip]
 
 
 def rotate_kernel(count, chips, *refs):
     halves = refs[:count]
-    size = halves[0].shape[0]
     if len(refs) == count + 2:
         cols_ref, out_ref = refs[count:]
     else:
@@ -128,16 +179,19 @@
             for ref, parity in ((own_ref, core), (sibling_ref, 1 - core)):
                 row = pl.multiple_of((2 * chip + parity) * slab, 16)
                 cols_ref[pl.ds(row, slab), :] = ref[chip * slab : (chip + 1) * slab, :]
-    for i, half in enumerate(halves):
-        out_ref[i * size : (i + 1) * size, :] = jnp.dot(
+    at = 0
+    for half in halves:
+        out_ref[at : at + half.shape[0], :] = jnp.dot(
             half[...], cols_ref[...], preferred_element_type=F32
         ).astype(BF16)
+        at += half.shape[0]
 
 
 def cov_sum(halves, groups, cons_ref, rows_ref):
-    size = halves[0].shape[0]
-    for i, half in enumerate(halves):
-        rows_ref[i * size : (i + 1) * size, :] = half[...]
+    at = 0
+    for half in halves:
+        rows_ref[at : at + half.shape[0], :] = half[...]
+        at += half.shape[0]
     at = 0
     for parts in groups:
         total = parts[0][...].astype(F32)
@@ -176,7 +230,7 @@
     squares = jnp.zeros((1, width), F32)
     for i in range(count):
         for side in range(2):
-            whole[i * size : (i + 1) * size, side * half : (side + 1) * half] = blocks[2 * i + side][...]
+            whole[i * size : (i + 1) * size, side * half : (side + 1) * half] = blocks[2 * i + side][:size]
         values = whole[i * size : (i + 1) * size, :].astype(F32)
         squares = squares + jnp.sum(values * values, axis=0, keepdims=True)
     inverse = 1.0 / (2.0 * jnp.sqrt(jnp.sum(squares, axis=1, keepdims=True) / width + 1e-06))
@@ -224,32 +278,22 @@
     parity = [[2 * i + c for i in range(chips)] for c in (0, 1)]
     pairs = [[2 * i, 2 * i + 1] for i in range(chips)]
     offsets = ring_offsets(chips)
-    tiled = slab % 16 == 0
+    tiled = slab % 16 == 0 and count % (16 * chips) == 0
 
     aligned = call(align_kernel, shape((count, width), BF16), [], [own_order, own_rows])
-    blocks = ring_gather(jnp.split(aligned, 2, axis=0), chips)
-
+    blocks = ring_whole(aligned, chips)
+
+    pieces = call(
+        functools.partial(cut_kernel, chips), shape((chips, slab, cols), BF16), [], [rot_rows]
+    )
+    pieces = lax.all_to_all(
+        pieces, "tok", split_axis=0, concat_axis=0, tiled=True, axis_index_groups=parity
+    )
     if tiled:
-        pieces = call(
-            functools.partial(pieces_kernel, chips),
-            [shape((slab, cols), BF16)] * chips,
-            [],
-            [rot_rows],
-            [shape((chips, slab, cols), BF16)],
-        )
-        pieces = [pieces[0]] + [
-            shift(piece, offset, chips) for piece, offset in zip(pieces[1:], offsets[1:], strict=True)
-        ]
-        stacked = call(
-            functools.partial(stack_kernel, chips), shape((chips * slab, cols), BF16), [], pieces
-        )
+        stacked = pieces.reshape(chips * slab, cols)
         rot_cols = [stacked, lax.ppermute(stacked, "tok", siblings)]
         rot_scratch = [shape((width, cols), BF16)]
     else:
-        pieces = rot_rows.reshape(slab, chips, cols).transpose(1, 0, 2)
-        pieces = lax.all_to_all(
-            pieces, "tok", split_axis=0, concat_axis=0, tiled=True, axis_index_groups=parity
-        )
         pieces = lax.all_gather(pieces, "tok", axis=1, axis_index_groups=pairs)
         rot_cols, rot_scratch = [pieces.reshape(width, cols)], []
 
@@ -289,13 +333,40 @@
         [shape((3 * count, width), BF16)],
         flops=2 * 3 * count * cols * width,
     )
-    own = (keep + lax.ppermute(give, "tok", siblings).astype(F32)).astype(BF16)
+    come = lax.ppermute(give, "tok", siblings)
 
     if tiled:
-        same = ring_gather(jnp.split(own, 2, axis=1), chips)
-        other = [[lax.ppermute(half, "tok", siblings) for half in block] for block in same]
+        half, last = width // 2, chips // 2 - 1
+        size = count // chips
+        sizes = [slab + size * (last + (sign == 1) * (side == 0) + (sign == -1) * (side == 1)) for sign, side in STREAMS]
+        first, second, *streams = call(
+            functools.partial(pack_kernel, chips, count),
+            [shape((slab, half), BF16)] * 2 + [shape((rows, half), BF16) for rows in sizes],
+            [],
+            [keep, come, early_cons, late_cons],
+        )
+        same, pieces, places = [[first, second]], [], []
+        for step in range(1, last + 1):
+            parts = []
+            for i, (sign, side) in enumerate(STREAMS):
+                message = shift(streams[i], sign, chips)
+                outs = [shape((rows, half), BF16) for rows in (slab, size, message.shape[0] - size)]
+                if outs[2].shape == outs[0].shape:
+                    outs = outs[:2]
+                block, piece, *rest = call(trim_kernel, outs, [], [message])
+                streams[i] = rest[0] if rest else block
+                parts.append(block)
+                pieces.append(piece)
+                places.append((-sign * step, side))
+            same += [parts[:2], parts[2:]]
+        far = [shift(streams[0], 1, chips), shift(streams[3], -1, chips)]
+        same.append(far)
+        pieces += far
+        places += [(chips // 2, 0), (chips // 2, 1)]
+        other = [[lax.ppermute(part, "tok", siblings) for part in block] for block in same]
         gathered = sum(same + other, [])
     else:
+        own = (keep + come.astype(F32)).astype(BF16)
         gathered = jnp.split(lax.all_gather(own, "tok", axis=0, tiled=True), 2, axis=1)
     rows = -(-slab // 128) * 128
     rotation_next = call(
@@ -308,23 +379,19 @@
         room=10,
     )
 
-    cons = [early_cons[i : i + count] for i in range(0, near, count)]
-    cons += [late_cons[i : i + count] for i in range(0, 3 * count, count)]
     if tiled:
-        cons = cons[:1] + [
-            shift(block, offset, chips) for block, offset in zip(cons[1:], offsets[1:], strict=True)
-        ]
         consensus = call(
-            functools.partial(join_kernel, chips),
+            functools.partial(join_kernel, chips, slab, places),
             shape((count, width), BF16),
             [],
-            cons,
+            [early_cons[:count]] + pieces,
             [shape((chips, count, cols), BF16)],
         )
     else:
+        cons = jnp.concatenate([early_cons, late_cons]).reshape(chips, count, cols)
         _, _, position = me(chips)
         natural = jnp.stack([chip_at((position + offset + chips) % chips, chips) for offset in offsets])
-        ordered = jnp.zeros((chips, count, cols), BF16).at[natural].set(jnp.stack(cons), unique_indices=True)
+        ordered = jnp.zeros((chips, count, cols), BF16).at[natural].set(cons, unique_indices=True)
         consensus = lax.all_to_all(
             ordered, "tok", split_axis=0, concat_axis=0, tiled=True, axis_index_groups=parity
         )

time: 134 us -> 124 us (0.925)
  starting transfers between devices: 59.1 us -> 46.2 us
  waiting for transfers between devices: 51.7 us -> 53.8 us
    ppermute x42 -> x22, starting transfers between devices: 53.6 us -> 33 us  [shift(): lax.ppermute(block, 'tok', [(2 * a + c, 2 * b + c) for a, b in pairs for...]
    all_to_all x0 -> x1, waiting for transfers between devices: none -> 8 us  [shards(): lax.all_to_all(pieces, 'tok', split_axis=0, concat_axis=0, tiled=True, ax...]
    ppermute x42 -> x22, waiting for transfers between devices: 49.4 us -> 42.1 us  [shift(): lax.ppermute(block, 'tok', [(2 * a + c, 2 * b + c) for a, b in pairs for...]
    all_to_all x0 -> x1, starting transfers between devices: none -> 6.22 us  [shards(): lax.all_to_all(pieces, 'tok', split_axis=0, concat_axis=0, tiled=True, ax...]
    ppermute x17, starting transfers between devices: 0.75 us -> 2.33 us  [the longest x16 2.26 us: shards(): lax.ppermute(part, 'tok', siblings)]
    pallas_call x10 -> x23, Pallas kernels: 20.1 us -> 20.7 us  [call(): pl.pallas_call(kernel, out_shape=outs, in_specs=[SMEM] * len(smem) + [VME...]
  transfers between devices with their start and end apart: 63 -> 44, of which waited for: 26 -> 19; matrix products, arithmetic and copies ran while one was open for 0% -> 0% of each run, Pallas kernels for 4% -> 4%
where the time goes in v3:
time: 124 us
  waiting for transfers between devices  53.8 us (43%)
  starting transfers between devices  46.2 us (37%)
  Pallas kernels  20.7 us (17%)
  local copies, waits for them, and re-layouts  2.67 us (2%)
    ppermute x22, waiting for transfers between devices, shift(): lax.ppermute(block, 'tok', [(2 * a + c, 2 * b + c) for a, b in pairs for...  42.1 us
    ppermute x22, starting transfers between devices, shift(): lax.ppermute(block, 'tok', [(2 * a + c, 2 * b + c) for a, b in pairs for...  33 us
    pallas_call x23, Pallas kernels, call(): pl.pallas_call(kernel, out_shape=outs, in_specs=[SMEM] * len(smem) + [VME...  20.7 us
    all_to_all x1, waiting for transfers between devices, shards(): lax.all_to_all(pieces, 'tok', split_axis=0, concat_axis=0, tiled=True, ax...  8 us
    all_to_all x1, starting transfers between devices, shards(): lax.all_to_all(pieces, 'tok', split_axis=0, concat_axis=0, tiled=True, ax...  6.22 us
    ppermute x3, starting transfers between devices, rotate(): return (halves, [rotated, lax.ppermute(rotated, 'ckpt', [(0, 1), (1, 0)])])  4.65 us
    unnamed x6, local copies, waits for them, and re-layouts  2.66 us
  transfers between devices with their start and end apart: 44, of which 19 were waited for; matrix products, arithmetic and copies ran while one was open for 0% of the time, Pallas kernels for 4%

profile of v3, /device:TPU:0, one launch (start us, length us, event | category | flops | bytes accessed | tf_op | source)
XLA Modules:
  0.0 124.2 jit_solution(17006833737055116629)
XLA Ops:
  0.6 1.0 copy-done
  1.7 0.7 copy-done.2
  2.6 3.0 %collective-permute-start.1 = (bf16[128,1792]{1,0:T(8,128)(2,1)S(1)}, bf16[128,1792]{1,0:T(8,128)(2,1)S(1)}, u32[]{:S(2)}, u32[]{:S(2)}) collective-permute-start(bf16[128,1792]{1,0:T(8,128)(2,1)S(1)} %shard_map.50.refs_0_), channel_id=1, source_target_pairs={{0,2},{1,3},{4,0},{5,1},{8,4},{9,5},{12,8},{13,9},{14,12},{15,13},... | collective-permute-start | bytes 1376264 | tf_op jit(solution)/shard_map/ppermute | solution.py:65
  5.8 1.0 copy-done.1
  6.8 1.0 shard_map.51
  7.8 6.2 %all-to-all-start = ((bf16[8,112,224]{2,1,0:T(8,128)(2,1)}), bf16[8,112,224]{2,1,0:T(8,128)(2,1)S(1)}, u32[]{:S(2)}, u32[]{:S(2)}) async-start(bf16[8,112,224]{2,1,0:T(8,128)(2,1)} %shard_map.51), calls=%async_computation | async-start | bytes 917504 | tf_op jit(solution)/shard_map/all_to_all | solution.py:289
  14.0 2.7 %collective-permute-done.1.refs_2_ = bf16[128,1792]{1,0:T(8,128)(2,1)S(1)} collective-permute-done((bf16[128,1792]{1,0:T(8,128)(2,1)S(1)}, bf16[128,1792]{1,0:T(8,128)(2,1)S(1)}, u32[]{:S(2)}, u32[]{:S(2)}) %collective-permute-start.1) | collective-permute-done | bytes 458784 | tf_op jit(solution)/shard_map/ppermute | solution.py:65
  16.7 2.5 %collective-permute-start.3 = (bf16[128,1792]{1,0:T(8,128)(2,1)S(1)}, bf16[128,1792]{1,0:T(8,128)(2,1)S(1)}, u32[]{:S(2)}, u32[]{:S(2)}) collective-permute-start(bf16[128,1792]{1,0:T(8,128)(2,1)S(1)} %collective-permute-done.1.refs_2_), channel_id=1, source_target_pairs={{0,2},{1,3},{4,0},{5,1},{8,4},{9,5},{12,8},{13,9},{14,12},{15,13},... | collective-permute-start | bytes 1376264 | tf_op jit(solution)/shard_map/ppermute | solution.py:65
  19.1 1.4 %collective-permute-start.2 = (bf16[128,1792]{1,0:T(8,128)(2,1)S(1)}, bf16[128,1792]{1,0:T(8,128)(2,1)S(1)}, u32[]{:S(2)}, u32[]{:S(2)}) collective-permute-start(bf16[128,1792]{1,0:T(8,128)(2,1)S(1)} %collective-permute-done.refs_1_), channel_id=1, source_target_pairs={{0,4},{1,5},{4,8},{5,9},{8,12},{9,13},{12,14},{13,15},{14,10},{15,... | collective-permute-start | bytes 1376264 | tf_op jit(solution)/shard_map/ppermute | solution.py:65
  20.5 8.0 %all-to-all-done = bf16[8,112,224]{2,1,0:T(8,128)(2,1)S(1)} async-done(((bf16[8,112,224]{2,1,0:T(8,128)(2,1)}), bf16[8,112,224]{2,1,0:T(8,128)(2,1)S(1)}, u32[]{:S(2)}, u32[]{:S(2)}) %all-to-all-start) | async-done | bytes 401440 | tf_op jit(solution)/shard_map/all_to_all | solution.py:289
  28.5 5.2 %collective-permute-done.3.refs_4_ = bf16[128,1792]{1,0:T(8,128)(2,1)S(1)} collective-permute-done((bf16[128,1792]{1,0:T(8,128)(2,1)S(1)}, bf16[128,1792]{1,0:T(8,128)(2,1)S(1)}, u32[]{:S(2)}, u32[]{:S(2)}) %collective-permute-start.3) | collective-permute-done | bytes 458784 | tf_op jit(solution)/shard_map/ppermute | solution.py:65
  34.3 3.4 %collective-permute-start.6 = (bf16[128,1792]{1,0:T(8,128)(2,1)S(1)}, bf16[128,1792]{1,0:T(8,128)(2,1)S(1)}, u32[]{:S(2)}, u32[]{:S(2)}) collective-permute-start(bf16[128,1792]{1,0:T(8,128)(2,1)S(1)} %collective-permute-done.2.refs_3_), channel_id=1, source_target_pairs={{0,4},{1,5},{4,8},{5,9},{8,12},{9,13},{12,14},{13,15},{14,10},{15,... | collective-permute-start | bytes 1376264 | tf_op jit(solution)/shard_map/ppermute | solution.py:65
  37.6 0.9 shard_map.52.refs_5_
  38.5 1.6 %collective-permute-start.5 = (bf16[640,224]{1,0:T(8,128)(2,1)S(1)}, bf16[640,224]{1,0:T(8,128)(2,1)S(1)}, u32[]{:S(2)}, u32[]{:S(2)}) collective-permute-start(bf16[640,224]{1,0:T(8,128)(2,1)S(1)} %shard_map.52.refs_5_), channel_id=1, source_target_pairs={{0,16},{16,0},{1,17},{17,1},{2,18},{18,2},{3,19},{19,3},{4,20},{20... | collective-permute-start | bytes 860168 | tf_op jit(solution)/shard_map/ppermute | solution.py:311
  40.1 7.0 %collective-permute-done.7.behind_ref.refs_1_ = bf16[128,1792]{1,0:T(8,128)(2,1)S(1)} collective-permute-done((bf16[128,1792]{1,0:T(8,128)(2,1)S(1)}, bf16[128,1792]{1,0:T(8,128)(2,1)S(1)}, u32[]{:S(2)}, u32[]{:S(2)}) %collective-permute-start.7) | collective-permute-done | bytes 458784 | tf_op jit(solution)/shard_map/ppermute | solution.py:65
  47.6 1.3 %collective-permute-start.8 = (bf16[64,1792]{1,0:T(8,128)(2,1)S(1)}, bf16[64,1792]{1,0:T(8,128)(2,1)S(1)}, u32[]{:S(2)}, u32[]{:S(2)}) collective-permute-start(bf16[64,1792]{1,0:T(8,128)(2,1)S(1)} %get-tuple-element.50), channel_id=1, source_target_pairs={{0,4},{1,5},{4,8},{5,9},{8,12},{9,13},{12,14},{13,15},{14,10},{15,... | collective-permute-start | bytes 688136 | tf_op jit(solution)/shard_map/ppermute | solution.py:65
  49.0 1.3 %collective-permute-start.9 = (bf16[64,1792]{1,0:T(8,128)(2,1)S(1)}, bf16[64,1792]{1,0:T(8,128)(2,1)S(1)}, u32[]{:S(2)}, u32[]{:S(2)}) collective-permute-start(bf16[64,1792]{1,0:T(8,128)(2,1)S(1)} %get-tuple-element.51), channel_id=1, source_target_pairs={{0,2},{1,3},{4,0},{5,1},{8,4},{9,5},{12,8},{13,9},{14,12},{15,13},... | collective-permute-start | bytes 688136 | tf_op jit(solution)/shard_map/ppermute | solution.py:65
  50.2 0.5 shard_map.55.refs_4_
  50.8 1.5 %collective-permute-start.10 = (bf16[256,224]{1,0:T(8,128)(2,1)S(1)}, bf16[256,224]{1,0:T(8,128)(2,1)S(1)}, u32[]{:S(2)}, u32[]{:S(2)}) collective-permute-start(bf16[256,224]{1,0:T(8,128)(2,1)S(1)} %shard_map.55.refs_4_), channel_id=1, source_target_pairs={{0,16},{16,0},{1,17},{17,1},{2,18},{18,2},{3,19},{19,3},{4,20},{20... | collective-permute-start | bytes 344072 | tf_op jit(solution)/shard_map/ppermute | solution.py:311
  52.3 1.8 %collective-permute-done.8.refs_0_.refs_2_ = bf16[64,1792]{1,0:T(8,128)(2,1)S(1)} collective-permute-done((bf16[64,1792]{1,0:T(8,128)(2,1)S(1)}, bf16[64,1792]{1,0:T(8,128)(2,1)S(1)}, u32[]{:S(2)}, u32[]{:S(2)}) %collective-permute-start.8) | collective-permute-done | bytes 229408 | tf_op jit(solution)/shard_map/ppermute | solution.py:65
  54.2 0.8 collective-permute-done.9.refs_1_.refs_3_
  55.5 1.6 %collective-permute-start.11 = (bf16[128,224]{1,0:T(8,128)(2,1)S(1)}, bf16[128,224]{1,0:T(8,128)(2,1)S(1)}, u32[]{:S(2)}, u32[]{:S(2)}) collective-permute-start(bf16[128,224]{1,0:T(8,128)(2,1)S(1)} %shard_map.56.refs_6_), channel_id=1, source_target_pairs={{0,16},{16,0},{1,17},{17,1},{2,18},{18,2},{3,19},{19,3},{4,20},{20... | collective-permute-start | bytes 172040 | tf_op jit(solution)/shard_map/ppermute | solution.py:311
  57.0 0.9 shard_map.53
  58.0 1.9 %collective-permute-done.11.refs_7_ = bf16[128,224]{1,0:T(8,128)(2,1)S(1)} collective-permute-done((bf16[128,224]{1,0:T(8,128)(2,1)S(1)}, bf16[128,224]{1,0:T(8,128)(2,1)S(1)}, u32[]{:S(2)}, u32[]{:S(2)}) %collective-permute-start.11) | collective-permute-done | bytes 57376 | tf_op jit(solution)/shard_map/ppermute | solution.py:311
  59.8 0.7 shard_map.57
  60.6 1.7 %collective-permute-done.12.come_ref = bf16[112,1792]{1,0:T(8,128)(2,1)S(1)} collective-permute-done((bf16[112,1792]{1,0:T(8,128)(2,1)S(1)}, bf16[112,1792]{1,0:T(8,128)(2,1)S(1)}, u32[]{:S(2)}, u32[]{:S(2)}) %collective-permute-start.12) | collective-permute-done | bytes 401440 | tf_op jit(solution)/shard_map/ppermute | solution.py:336
  62.6 1.8 %collective-permute-start.13 = (bf16[176,896]{1,0:T(8,128)(2,1)S(1)}, bf16[176,896]{1,0:T(8,128)(2,1)S(1)}, u32[]{:S(2)}, u32[]{:S(2)}) collective-permute-start(bf16[176,896]{1,0:T(8,128)(2,1)S(1)} %get-tuple-element.56), channel_id=1, source_target_pairs={{0,4},{1,5},{4,8},{5,9},{8,12},{9,13},{12,14},{13,15},{14,10},{15,... | collective-permute-start | bytes 946184 | tf_op jit(solution)/shard_map/ppermute | solution.py:65
  64.7 1.7 %collective-permute-start.14 = (bf16[160,896]{1,0:T(8,128)(2,1)S(1)}, bf16[160,896]{1,0:T(8,128)(2,1)S(1)}, u32[]{:S(2)}, u32[]{:S(2)}) collective-permute-start(bf16[160,896]{1,0:T(8,128)(2,1)S(1)} %get-tuple-element.58), channel_id=1, source_target_pairs={{0,4},{1,5},{4,8},{5,9},{8,12},{9,13},{12,14},{13,15},{14,10},{15,... | collective-permute-start | bytes 860168 | tf_op jit(solution)/shard_map/ppermute | solution.py:65
  66.7 6.2 %collective-permute-done.13.message_ref = bf16[176,896]{1,0:T(8,128)(2,1)S(1)} collective-permute-done((bf16[176,896]{1,0:T(8,128)(2,1)S(1)}, bf16[176,896]{1,0:T(8,128)(2,1)S(1)}, u32[]{:S(2)}, u32[]{:S(2)}) %collective-permute-start.13) | collective-permute-done | bytes 315424 | tf_op jit(solution)/shard_map/ppermute | solution.py:65
  73.0 1.8 %collective-permute-start.17 = (bf16[160,896]{1,0:T(8,128)(2,1)S(1)}, bf16[160,896]{1,0:T(8,128)(2,1)S(1)}, u32[]{:S(2)}, u32[]{:S(2)}) collective-permute-start(bf16[160,896]{1,0:T(8,128)(2,1)S(1)} %get-tuple-element.64), channel_id=1, source_target_pairs={{0,4},{1,5},{4,8},{5,9},{8,12},{9,13},{12,14},{13,15},{14,10},{15,... | collective-permute-start | bytes 860168 | tf_op jit(solution)/shard_map/ppermute | solution.py:65
  75.2 3.9 %collective-permute-done.14.message_ref = bf16[160,896]{1,0:T(8,128)(2,1)S(1)} collective-permute-done((bf16[160,896]{1,0:T(8,128)(2,1)S(1)}, bf16[160,896]{1,0:T(8,128)(2,1)S(1)}, u32[]{:S(2)}, u32[]{:S(2)}) %collective-permute-start.14) | collective-permute-done | bytes 286752 | tf_op jit(solution)/shard_map/ppermute | solution.py:65
  79.1 1.8 %collective-permute-start.18 = (bf16[144,896]{1,0:T(8,128)(2,1)S(1)}, bf16[144,896]{1,0:T(8,128)(2,1)S(1)}, u32[]{:S(2)}, u32[]{:S(2)}) collective-permute-start(bf16[144,896]{1,0:T(8,128)(2,1)S(1)} %get-tuple-element.66), channel_id=1, source_target_pairs={{0,4},{1,5},{4,8},{5,9},{8,12},{9,13},{12,14},{13,15},{14,10},{15,... | collective-permute-start | bytes 774152 | tf_op jit(solution)/shard_map/ppermute | solution.py:65
  81.5 3.7 %collective-permute-done.17.message_ref = bf16[160,896]{1,0:T(8,128)(2,1)S(1)} collective-permute-done((bf16[160,896]{1,0:T(8,128)(2,1)S(1)}, bf16[160,896]{1,0:T(8,128)(2,1)S(1)}, u32[]{:S(2)}, u32[]{:S(2)}) %collective-permute-start.17) | collective-permute-done | bytes 286752 | tf_op jit(solution)/shard_map/ppermute | solution.py:65
  85.3 1.3 %collective-permute-start.19 = (bf16[144,896]{1,0:T(8,128)(2,1)S(1)}, bf16[144,896]{1,0:T(8,128)(2,1)S(1)}, u32[]{:S(2)}, u32[]{:S(2)}) collective-permute-start(bf16[144,896]{1,0:T(8,128)(2,1)S(1)} %get-tuple-element.68), channel_id=1, source_target_pairs={{0,2},{1,3},{4,0},{5,1},{8,4},{9,5},{12,8},{13,9},{14,12},{15,13},... | collective-permute-start | bytes 774152 | tf_op jit(solution)/shard_map/ppermute | solution.py:65
  86.6 0.8 collective-permute-start.21
  87.4 1.3 %collective-permute-start.24 = (bf16[144,896]{1,0:T(8,128)(2,1)S(1)}, bf16[144,896]{1,0:T(8,128)(2,1)S(1)}, u32[]{:S(2)}, u32[]{:S(2)}) collective-permute-start(bf16[144,896]{1,0:T(8,128)(2,1)S(1)} %get-tuple-element.78), channel_id=1, source_target_pairs={{0,2},{1,3},{4,0},{5,1},{8,4},{9,5},{12,8},{13,9},{14,12},{15,13},... | collective-permute-start | bytes 774152 | tf_op jit(solution)/shard_map/ppermute | solution.py:65
  88.7 1.3 %collective-permute-done.18.message_ref = bf16[144,896]{1,0:T(8,128)(2,1)S(1)} collective-permute-done((bf16[144,896]{1,0:T(8,128)(2,1)S(1)}, bf16[144,896]{1,0:T(8,128)(2,1)S(1)}, u32[]{:S(2)}, u32[]{:S(2)}) %collective-permute-start.18) | collective-permute-done | bytes 258080 | tf_op jit(solution)/shard_map/ppermute | solution.py:65
  90.1 2.5 %collective-permute-start.22 = (bf16[128,896]{1,0:T(8,128)(2,1)S(1)}, bf16[128,896]{1,0:T(8,128)(2,1)S(1)}, u32[]{:S(2)}, u32[]{:S(2)}) collective-permute-start(bf16[128,896]{1,0:T(8,128)(2,1)S(1)} %get-tuple-element.74), channel_id=1, source_target_pairs={{0,4},{1,5},{4,8},{5,9},{8,12},{9,13},{12,14},{13,15},{14,10},{15,... | collective-permute-start | bytes 688136 | tf_op jit(solution)/shard_map/ppermute | solution.py:65
  92.6 0.8 collective-permute-done.19.message_ref
  93.5 2.0 %collective-permute-start.23 = (bf16[128,896]{1,0:T(8,128)(2,1)S(1)}, bf16[128,896]{1,0:T(8,128)(2,1)S(1)}, u32[]{:S(2)}, u32[]{:S(2)}) collective-permute-start(bf16[128,896]{1,0:T(8,128)(2,1)S(1)} %get-tuple-element.76), channel_id=1, source_target_pairs={{0,2},{1,3},{4,0},{5,1},{8,4},{9,5},{12,8},{13,9},{14,12},{15,13},... | collective-permute-start | bytes 688136 | tf_op jit(solution)/shard_map/ppermute | solution.py:65
  95.8 2.3 %collective-permute-done.24.message_ref = bf16[144,896]{1,0:T(8,128)(2,1)S(1)} collective-permute-done((bf16[144,896]{1,0:T(8,128)(2,1)S(1)}, bf16[144,896]{1,0:T(8,128)(2,1)S(1)}, u32[]{:S(2)}, u32[]{:S(2)}) %collective-permute-start.24) | collective-permute-done | bytes 258080 | tf_op jit(solution)/shard_map/ppermute | solution.py:65
  98.2 1.8 %collective-permute-start.25 = (bf16[128,896]{1,0:T(8,128)(2,1)S(1)}, bf16[128,896]{1,0:T(8,128)(2,1)S(1)}, u32[]{:S(2)}, u32[]{:S(2)}) collective-permute-start(bf16[128,896]{1,0:T(8,128)(2,1)S(1)} %get-tuple-element.80), channel_id=1, source_target_pairs={{0,4},{1,5},{4,8},{5,9},{8,12},{9,13},{12,14},{13,15},{14,10},{15,... | collective-permute-start | bytes 688136 | tf_op jit(solution)/shard_map/ppermute | solution.py:65
  100.5 1.7 %collective-permute-start.26 = (bf16[128,896]{1,0:T(8,128)(2,1)S(1)}, bf16[128,896]{1,0:T(8,128)(2,1)S(1)}, u32[]{:S(2)}, u32[]{:S(2)}) collective-permute-start(bf16[128,896]{1,0:T(8,128)(2,1)S(1)} %get-tuple-element.81), channel_id=1, source_target_pairs={{0,2},{1,3},{4,0},{5,1},{8,4},{9,5},{12,8},{13,9},{14,12},{15,13},... | collective-permute-start | bytes 688136 | tf_op jit(solution)/shard_map/ppermute | solution.py:65
  102.9 3.4 %collective-permute-done.25.refs_12_.refs_14_ = bf16[128,896]{1,0:T(8,128)(2,1)S(1)} collective-permute-done((bf16[128,896]{1,0:T(8,128)(2,1)S(1)}, bf16[128,896]{1,0:T(8,128)(2,1)S(1)}, u32[]{:S(2)}, u32[]{:S(2)}) %collective-permute-start.25) | collective-permute-done | bytes 229408 | tf_op jit(solution)/shard_map/ppermute | solution.py:65
  106.3 1.6 %collective-permute-done.26.refs_13_.refs_15_ = bf16[128,896]{1,0:T(8,128)(2,1)S(1)} collective-permute-done((bf16[128,896]{1,0:T(8,128)(2,1)S(1)}, bf16[128,896]{1,0:T(8,128)(2,1)S(1)}, u32[]{:S(2)}, u32[]{:S(2)}) %collective-permute-start.26) | collective-permute-done | bytes 229408 | tf_op jit(solution)/shard_map/ppermute | solution.py:65
  107.9 0.6 collective-permute-start.39
  109.0 1.2 shard_map.71
  110.2 13.9 %shard_map.72 = bf16[112,1792]{1,0:T(8,128)(2,1)} custom-call(bf16[112,896]{1,0:T(8,128)(2,1)S(1)} %get-tuple-element.82.refs_0_, bf16[112,896]{1,0:T(8,128)(2,1)S(1)} %get-tuple-element.83.refs_1_, bf16[112,896]{1,0:T(8,128)(2,1)S(1)} %get-tuple-element.84.refs_2_, bf16[112,896]{1,0:T(8,128)(2,1)S(1)} %get-tuple-element.85.refs_3_, ...), custom_call_target="tpu_custom_call" | custom-call | flops 6576668672 | bytes 14278656 | tf_op jit(solution)/shard_map/pallas_call | solution.py:34
  (70 shorter events, 6.2 us)
Async XLA Ops:
  0.6 1.0 copy-start
  1.6 0.7 copy-start.2
  2.6 14.0 %collective-permute-start.1 = (bf16[128,1792]{1,0:T(8,128)(2,1)S(1)}, bf16[128,1792]{1,0:T(8,128)(2,1)S(1)}, u32[]{:S(2)}, u32[]{:S(2)}) collective-permute-start(bf16[128,1792]{1,0:T(8,128)(2,1)S(1)} %shard_map.50.refs_0_), channel_id=1, source_target_pairs={{0,2},{1,3},{4,0},{5,1},{8,4},{9,5},{12,8},{13,9},{14,12},{15,13},... | collective-permute-start | bytes 1376264 | tf_op jit(solution)/shard_map/ppermute | solution.py:65
  5.7 13.5 %collective-permute-start = (bf16[128,1792]{1,0:T(8,128)(2,1)S(1)}, bf16[128,1792]{1,0:T(8,128)(2,1)S(1)}, u32[]{:S(2)}, u32[]{:S(2)}) collective-permute-start(bf16[128,1792]{1,0:T(8,128)(2,1)S(1)} %shard_map.50.refs_0_), channel_id=1, source_target_pairs={{0,4},{1,5},{4,8},{5,9},{8,12},{9,13},{12,14},{13,15},{14,10},{15,... | collective-permute-start | bytes 1376264 | tf_op jit(solution)/shard_map/ppermute | solution.py:65
  5.8 1.0 copy-start.1
  7.8 20.8 %all-to-all-start = ((bf16[8,112,224]{2,1,0:T(8,128)(2,1)}), bf16[8,112,224]{2,1,0:T(8,128)(2,1)S(1)}, u32[]{:S(2)}, u32[]{:S(2)}) async-start(bf16[8,112,224]{2,1,0:T(8,128)(2,1)} %shard_map.51), calls=%async_computation | async-start | bytes 917504 | tf_op jit(solution)/shard_map/all_to_all | solution.py:289
  16.7 17.1 %collective-permute-start.3 = (bf16[128,1792]{1,0:T(8,128)(2,1)S(1)}, bf16[128,1792]{1,0:T(8,128)(2,1)S(1)}, u32[]{:S(2)}, u32[]{:S(2)}) collective-permute-start(bf16[128,1792]{1,0:T(8,128)(2,1)S(1)} %collective-permute-done.1.refs_2_), channel_id=1, source_target_pairs={{0,2},{1,3},{4,0},{5,1},{8,4},{9,5},{12,8},{13,9},{14,12},{15,13},... | collective-permute-start | bytes 1376264 | tf_op jit(solution)/shard_map/ppermute | solution.py:65
  19.1 15.1 %collective-permute-start.2 = (bf16[128,1792]{1,0:T(8,128)(2,1)S(1)}, bf16[128,1792]{1,0:T(8,128)(2,1)S(1)}, u32[]{:S(2)}, u32[]{:S(2)}) collective-permute-start(bf16[128,1792]{1,0:T(8,128)(2,1)S(1)} %collective-permute-done.refs_1_), channel_id=1, source_target_pairs={{0,4},{1,5},{4,8},{5,9},{8,12},{9,13},{12,14},{13,15},{14,10},{15,... | collective-permute-start | bytes 1376264 | tf_op jit(solution)/shard_map/ppermute | solution.py:65
  28.5 9.1 %collective-permute-start.4 = (bf16[896,224]{1,0:T(8,128)(2,1)S(1)}, bf16[896,224]{1,0:T(8,128)(2,1)S(1)}, u32[]{:S(2)}, u32[]{:S(2)}) collective-permute-start(bf16[896,224]{1,0:T(8,128)(2,1)S(1)} %bitcast.5), channel_id=1, source_target_pairs={{0,1},{1,0},{2,3},{3,2},{4,5},{5,4},{6,7},{7,6},{8,9},{9,8},{10,11... | collective-permute-start | bytes 1204232 | tf_op jit(solution)/shard_map/ppermute | solution.py:294
  33.7 13.4 %collective-permute-start.7 = (bf16[128,1792]{1,0:T(8,128)(2,1)S(1)}, bf16[128,1792]{1,0:T(8,128)(2,1)S(1)}, u32[]{:S(2)}, u32[]{:S(2)}) collective-permute-start(bf16[128,1792]{1,0:T(8,128)(2,1)S(1)} %collective-permute-done.3.refs_4_), channel_id=1, source_target_pairs={{0,2},{1,3},{4,0},{5,1},{8,4},{9,5},{12,8},{13,9},{14,12},{15,13},... | collective-permute-start | bytes 1376264 | tf_op jit(solution)/shard_map/ppermute | solution.py:65
  34.3 13.4 %collective-permute-start.6 = (bf16[128,1792]{1,0:T(8,128)(2,1)S(1)}, bf16[128,1792]{1,0:T(8,128)(2,1)S(1)}, u32[]{:S(2)}, u32[]{:S(2)}) collective-permute-start(bf16[128,1792]{1,0:T(8,128)(2,1)S(1)} %collective-permute-done.2.refs_3_), channel_id=1, source_target_pairs={{0,4},{1,5},{4,8},{5,9},{8,12},{9,13},{12,14},{13,15},{14,10},{15,... | collective-permute-start | bytes 1376264 | tf_op jit(solution)/shard_map/ppermute | solution.py:65
  38.5 18.5 %collective-permute-start.5 = (bf16[640,224]{1,0:T(8,128)(2,1)S(1)}, bf16[640,224]{1,0:T(8,128)(2,1)S(1)}, u32[]{:S(2)}, u32[]{:S(2)}) collective-permute-start(bf16[640,224]{1,0:T(8,128)(2,1)S(1)} %shard_map.52.refs_5_), channel_id=1, source_target_pairs={{0,16},{16,0},{1,17},{17,1},{2,18},{18,2},{3,19},{19,3},{4,20},{20... | collective-permute-start | bytes 860168 | tf_op jit(solution)/shard_map/ppermute | solution.py:311
  47.6 6.5 %collective-permute-start.8 = (bf16[64,1792]{1,0:T(8,128)(2,1)S(1)}, bf16[64,1792]{1,0:T(8,128)(2,1)S(1)}, u32[]{:S(2)}, u32[]{:S(2)}) collective-permute-start(bf16[64,1792]{1,0:T(8,128)(2,1)S(1)} %get-tuple-element.50), channel_id=1, source_target_pairs={{0,4},{1,5},{4,8},{5,9},{8,12},{9,13},{12,14},{13,15},{14,10},{15,... | collective-permute-start | bytes 688136 | tf_op jit(solution)/shard_map/ppermute | solution.py:65
  49.0 6.0 %collective-permute-start.9 = (bf16[64,1792]{1,0:T(8,128)(2,1)S(1)}, bf16[64,1792]{1,0:T(8,128)(2,1)S(1)}, u32[]{:S(2)}, u32[]{:S(2)}) collective-permute-start(bf16[64,1792]{1,0:T(8,128)(2,1)S(1)} %get-tuple-element.51), channel_id=1, source_target_pairs={{0,2},{1,3},{4,0},{5,1},{8,4},{9,5},{12,8},{13,9},{14,12},{15,13},... | collective-permute-start | bytes 688136 | tf_op jit(solution)/shard_map/ppermute | solution.py:65
  50.8 7.1 %collective-permute-start.10 = (bf16[256,224]{1,0:T(8,128)(2,1)S(1)}, bf16[256,224]{1,0:T(8,128)(2,1)S(1)}, u32[]{:S(2)}, u32[]{:S(2)}) collective-permute-start(bf16[256,224]{1,0:T(8,128)(2,1)S(1)} %shard_map.55.refs_4_), channel_id=1, source_target_pairs={{0,16},{16,0},{1,17},{17,1},{2,18},{18,2},{3,19},{19,3},{4,20},{20... | collective-permute-start | bytes 344072 | tf_op jit(solution)/shard_map/ppermute | solution.py:311
  55.5 4.3 %collective-permute-start.11 = (bf16[128,224]{1,0:T(8,128)(2,1)S(1)}, bf16[128,224]{1,0:T(8,128)(2,1)S(1)}, u32[]{:S(2)}, u32[]{:S(2)}) collective-permute-start(bf16[128,224]{1,0:T(8,128)(2,1)S(1)} %shard_map.56.refs_6_), channel_id=1, source_target_pairs={{0,16},{16,0},{1,17},{17,1},{2,18},{18,2},{3,19},{19,3},{4,20},{20... | collective-permute-start | bytes 172040 | tf_op jit(solution)/shard_map/ppermute | solution.py:311
  60.5 1.8 %collective-permute-start.12 = (bf16[112,1792]{1,0:T(8,128)(2,1)S(1)}, bf16[112,1792]{1,0:T(8,128)(2,1)S(1)}, u32[]{:S(2)}, u32[]{:S(2)}) collective-permute-start(bf16[112,1792]{1,0:T(8,128)(2,1)S(1)} %get-tuple-element.54), channel_id=1, source_target_pairs={{0,1},{1,0},{2,3},{3,2},{4,5},{5,4},{6,7},{7,6},{8,9},{9,8},{10,11... | collective-permute-start | bytes 1204232 | tf_op jit(solution)/shard_map/ppermute | solution.py:336
  62.6 10.3 %collective-permute-start.13 = (bf16[176,896]{1,0:T(8,128)(2,1)S(1)}, bf16[176,896]{1,0:T(8,128)(2,1)S(1)}, u32[]{:S(2)}, u32[]{:S(2)}) collective-permute-start(bf16[176,896]{1,0:T(8,128)(2,1)S(1)} %get-tuple-element.56), channel_id=1, source_target_pairs={{0,4},{1,5},{4,8},{5,9},{8,12},{9,13},{12,14},{13,15},{14,10},{15,... | collective-permute-start | bytes 946184 | tf_op jit(solution)/shard_map/ppermute | solution.py:65
  64.4 10.4 %collective-permute-start.16 = (bf16[176,896]{1,0:T(8,128)(2,1)S(1)}, bf16[176,896]{1,0:T(8,128)(2,1)S(1)}, u32[]{:S(2)}, u32[]{:S(2)}) collective-permute-start(bf16[176,896]{1,0:T(8,128)(2,1)S(1)} %get-tuple-element.62), channel_id=1, source_target_pairs={{0,2},{1,3},{4,0},{5,1},{8,4},{9,5},{12,8},{13,9},{14,12},{15,13},... | collective-permute-start | bytes 946184 | tf_op jit(solution)/shard_map/ppermute | solution.py:65
  64.7 14.4 %collective-permute-start.14 = (bf16[160,896]{1,0:T(8,128)(2,1)S(1)}, bf16[160,896]{1,0:T(8,128)(2,1)S(1)}, u32[]{:S(2)}, u32[]{:S(2)}) collective-permute-start(bf16[160,896]{1,0:T(8,128)(2,1)S(1)} %get-tuple-element.58), channel_id=1, source_target_pairs={{0,4},{1,5},{4,8},{5,9},{8,12},{9,13},{12,14},{13,15},{14,10},{15,... | collective-permute-start | bytes 860168 | tf_op jit(solution)/shard_map/ppermute | solution.py:65
  66.4 14.5 %collective-permute-start.15 = (bf16[160,896]{1,0:T(8,128)(2,1)S(1)}, bf16[160,896]{1,0:T(8,128)(2,1)S(1)}, u32[]{:S(2)}, u32[]{:S(2)}) collective-permute-start(bf16[160,896]{1,0:T(8,128)(2,1)S(1)} %get-tuple-element.60), channel_id=1, source_target_pairs={{0,2},{1,3},{4,0},{5,1},{8,4},{9,5},{12,8},{13,9},{14,12},{15,13},... | collective-permute-start | bytes 860168 | tf_op jit(solution)/shard_map/ppermute | solution.py:65
  66.7 14.2 %collective-permute-start.27 = (bf16[112,896]{1,0:T(8,128)(2,1)S(1)}, bf16[112,896]{1,0:T(8,128)(2,1)S(1)}, u32[]{:S(2)}, u32[]{:S(2)}) collective-permute-start(bf16[112,896]{1,0:T(8,128)(2,1)S(1)} %get-tuple-element.82.refs_0_), channel_id=1, source_target_pairs={{0,1},{1,0},{2,3},{3,2},{4,5},{5,4},{6,7},{7,6},{8,9},{9,8},{10,11... | collective-permute-start | bytes 602120 | tf_op jit(solution)/shard_map/ppermute | solution.py:366
  73.0 12.2 %collective-permute-start.17 = (bf16[160,896]{1,0:T(8,128)(2,1)S(1)}, bf16[160,896]{1,0:T(8,128)(2,1)S(1)}, u32[]{:S(2)}, u32[]{:S(2)}) collective-permute-start(bf16[160,896]{1,0:T(8,128)(2,1)S(1)} %get-tuple-element.64), channel_id=1, source_target_pairs={{0,4},{1,5},{4,8},{5,9},{8,12},{9,13},{12,14},{13,15},{14,10},{15,... | collective-permute-start | bytes 860168 | tf_op jit(solution)/shard_map/ppermute | solution.py:65
  74.8 11.7 %collective-permute-start.20 = (bf16[160,896]{1,0:T(8,128)(2,1)S(1)}, bf16[160,896]{1,0:T(8,128)(2,1)S(1)}, u32[]{:S(2)}, u32[]{:S(2)}) collective-permute-start(bf16[160,896]{1,0:T(8,128)(2,1)S(1)} %get-tuple-element.70), channel_id=1, source_target_pairs={{0,2},{1,3},{4,0},{5,1},{8,4},{9,5},{12,8},{13,9},{14,12},{15,13},... | collective-permute-start | bytes 860168 | tf_op jit(solution)/shard_map/ppermute | solution.py:65
  79.1 10.9 %collective-permute-start.18 = (bf16[144,896]{1,0:T(8,128)(2,1)S(1)}, bf16[144,896]{1,0:T(8,128)(2,1)S(1)}, u32[]{:S(2)}, u32[]{:S(2)}) collective-permute-start(bf16[144,896]{1,0:T(8,128)(2,1)S(1)} %get-tuple-element.66), channel_id=1, source_target_pairs={{0,4},{1,5},{4,8},{5,9},{8,12},{9,13},{12,14},{13,15},{14,10},{15,... | collective-permute-start | bytes 774152 | tf_op jit(solution)/shard_map/ppermute | solution.py:65
  80.9 5.7 %collective-permute-start.28 = (bf16[112,896]{1,0:T(8,128)(2,1)S(1)}, bf16[112,896]{1,0:T(8,128)(2,1)S(1)}, u32[]{:S(2)}, u32[]{:S(2)}) collective-permute-start(bf16[112,896]{1,0:T(8,128)(2,1)S(1)} %get-tuple-element.83.refs_1_), channel_id=1, source_target_pairs={{0,1},{1,0},{2,3},{3,2},{4,5},{5,4},{6,7},{7,6},{8,9},{9,8},{10,11... | collective-permute-start | bytes 602120 | tf_op jit(solution)/shard_map/ppermute | solution.py:366
  81.0 6.5 %collective-permute-start.30 = (bf16[112,896]{1,0:T(8,128)(2,1)S(1)}, bf16[112,896]{1,0:T(8,128)(2,1)S(1)}, u32[]{:S(2)}, u32[]{:S(2)}) collective-permute-start(bf16[112,896]{1,0:T(8,128)(2,1)S(1)} %get-tuple-element.85.refs_3_), channel_id=1, source_target_pairs={{0,1},{1,0},{2,3},{3,2},{4,5},{5,4},{6,7},{7,6},{8,9},{9,8},{10,11... | collective-permute-start | bytes 602120 | tf_op jit(solution)/shard_map/ppermute | solution.py:366
  85.3 8.2 %collective-permute-start.19 = (bf16[144,896]{1,0:T(8,128)(2,1)S(1)}, bf16[144,896]{1,0:T(8,128)(2,1)S(1)}, u32[]{:S(2)}, u32[]{:S(2)}) collective-permute-start(bf16[144,896]{1,0:T(8,128)(2,1)S(1)} %get-tuple-element.68), channel_id=1, source_target_pairs={{0,2},{1,3},{4,0},{5,1},{8,4},{9,5},{12,8},{13,9},{14,12},{15,13},... | collective-permute-start | bytes 774152 | tf_op jit(solution)/shard_map/ppermute | solution.py:65
  86.5 3.6 %collective-permute-start.31 = (bf16[112,896]{1,0:T(8,128)(2,1)S(1)}, bf16[112,896]{1,0:T(8,128)(2,1)S(1)}, u32[]{:S(2)}, u32[]{:S(2)}) collective-permute-start(bf16[112,896]{1,0:T(8,128)(2,1)S(1)} %get-tuple-element.86.refs_4_), channel_id=1, source_target_pairs={{0,1},{1,0},{2,3},{3,2},{4,5},{5,4},{6,7},{7,6},{8,9},{9,8},{10,11... | collective-permute-start | bytes 602120 | tf_op jit(solution)/shard_map/ppermute | solution.py:366
  86.6 9.1 %collective-permute-start.21 = (bf16[144,896]{1,0:T(8,128)(2,1)S(1)}, bf16[144,896]{1,0:T(8,128)(2,1)S(1)}, u32[]{:S(2)}, u32[]{:S(2)}) collective-permute-start(bf16[144,896]{1,0:T(8,128)(2,1)S(1)} %get-tuple-element.72), channel_id=1, source_target_pairs={{0,4},{1,5},{4,8},{5,9},{8,12},{9,13},{12,14},{13,15},{14,10},{15,... | collective-permute-start | bytes 774152 | tf_op jit(solution)/shard_map/ppermute | solution.py:65
  87.4 10.7 %collective-permute-start.24 = (bf16[144,896]{1,0:T(8,128)(2,1)S(1)}, bf16[144,896]{1,0:T(8,128)(2,1)S(1)}, u32[]{:S(2)}, u32[]{:S(2)}) collective-permute-start(bf16[144,896]{1,0:T(8,128)(2,1)S(1)} %get-tuple-element.78), channel_id=1, source_target_pairs={{0,2},{1,3},{4,0},{5,1},{8,4},{9,5},{12,8},{13,9},{14,12},{15,13},... | collective-permute-start | bytes 774152 | tf_op jit(solution)/shard_map/ppermute | solution.py:65
  90.0 3.4 %collective-permute-start.29 = (bf16[112,896]{1,0:T(8,128)(2,1)S(1)}, bf16[112,896]{1,0:T(8,128)(2,1)S(1)}, u32[]{:S(2)}, u32[]{:S(2)}) collective-permute-start(bf16[112,896]{1,0:T(8,128)(2,1)S(1)} %get-tuple-element.84.refs_2_), channel_id=1, source_target_pairs={{0,1},{1,0},{2,3},{3,2},{4,5},{5,4},{6,7},{7,6},{8,9},{9,8},{10,11... | collective-permute-start | bytes 602120 | tf_op jit(solution)/shard_map/ppermute | solution.py:366
  90.1 10.4 %collective-permute-start.22 = (bf16[128,896]{1,0:T(8,128)(2,1)S(1)}, bf16[128,896]{1,0:T(8,128)(2,1)S(1)}, u32[]{:S(2)}, u32[]{:S(2)}) collective-permute-start(bf16[128,896]{1,0:T(8,128)(2,1)S(1)} %get-tuple-element.74), channel_id=1, source_target_pairs={{0,4},{1,5},{4,8},{5,9},{8,12},{9,13},{12,14},{13,15},{14,10},{15,... | collective-permute-start | bytes 688136 | tf_op jit(solution)/shard_map/ppermute | solution.py:65
  93.4 4.8 %collective-permute-start.32 = (bf16[112,896]{1,0:T(8,128)(2,1)S(1)}, bf16[112,896]{1,0:T(8,128)(2,1)S(1)}, u32[]{:S(2)}, u32[]{:S(2)}) collective-permute-start(bf16[112,896]{1,0:T(8,128)(2,1)S(1)} %get-tuple-element.87.refs_5_), channel_id=1, source_target_pairs={{0,1},{1,0},{2,3},{3,2},{4,5},{5,4},{6,7},{7,6},{8,9},{9,8},{10,11... | collective-permute-start | bytes 602120 | tf_op jit(solution)/shard_map/ppermute | solution.py:366
  93.5 9.3 %collective-permute-start.23 = (bf16[128,896]{1,0:T(8,128)(2,1)S(1)}, bf16[128,896]{1,0:T(8,128)(2,1)S(1)}, u32[]{:S(2)}, u32[]{:S(2)}) collective-permute-start(bf16[128,896]{1,0:T(8,128)(2,1)S(1)} %get-tuple-element.76), channel_id=1, source_target_pairs={{0,2},{1,3},{4,0},{5,1},{8,4},{9,5},{12,8},{13,9},{14,12},{15,13},... | collective-permute-start | bytes 688136 | tf_op jit(solution)/shard_map/ppermute | solution.py:65
  95.8 6.5 %collective-permute-start.34 = (bf16[112,896]{1,0:T(8,128)(2,1)S(1)}, bf16[112,896]{1,0:T(8,128)(2,1)S(1)}, u32[]{:S(2)}, u32[]{:S(2)}) collective-permute-start(bf16[112,896]{1,0:T(8,128)(2,1)S(1)} %get-tuple-element.89.refs_7_), channel_id=1, source_target_pairs={{0,1},{1,0},{2,3},{3,2},{4,5},{5,4},{6,7},{7,6},{8,9},{9,8},{10,11... | collective-permute-start | bytes 602120 | tf_op jit(solution)/shard_map/ppermute | solution.py:366
  98.1 4.2 %collective-permute-start.35 = (bf16[112,896]{1,0:T(8,128)(2,1)S(1)}, bf16[112,896]{1,0:T(8,128)(2,1)S(1)}, u32[]{:S(2)}, u32[]{:S(2)}) collective-permute-start(bf16[112,896]{1,0:T(8,128)(2,1)S(1)} %get-tuple-element.90.refs_8_), channel_id=1, source_target_pairs={{0,1},{1,0},{2,3},{3,2},{4,5},{5,4},{6,7},{7,6},{8,9},{9,8},{10,11... | collective-permute-start | bytes 602120 | tf_op jit(solution)/shard_map/ppermute | solution.py:366
  98.2 8.1 %collective-permute-start.25 = (bf16[128,896]{1,0:T(8,128)(2,1)S(1)}, bf16[128,896]{1,0:T(8,128)(2,1)S(1)}, u32[]{:S(2)}, u32[]{:S(2)}) collective-permute-start(bf16[128,896]{1,0:T(8,128)(2,1)S(1)} %get-tuple-element.80), channel_id=1, source_target_pairs={{0,4},{1,5},{4,8},{5,9},{8,12},{9,13},{12,14},{13,15},{14,10},{15,... | collective-permute-start | bytes 688136 | tf_op jit(solution)/shard_map/ppermute | solution.py:65
  100.5 7.4 %collective-permute-start.26 = (bf16[128,896]{1,0:T(8,128)(2,1)S(1)}, bf16[128,896]{1,0:T(8,128)(2,1)S(1)}, u32[]{:S(2)}, u32[]{:S(2)}) collective-permute-start(bf16[128,896]{1,0:T(8,128)(2,1)S(1)} %get-tuple-element.81), channel_id=1, source_target_pairs={{0,2},{1,3},{4,0},{5,1},{8,4},{9,5},{12,8},{13,9},{14,12},{15,13},... | collective-permute-start | bytes 688136 | tf_op jit(solution)/shard_map/ppermute | solution.py:65
  102.2 5.7 %collective-permute-start.33 = (bf16[112,896]{1,0:T(8,128)(2,1)S(1)}, bf16[112,896]{1,0:T(8,128)(2,1)S(1)}, u32[]{:S(2)}, u32[]{:S(2)}) collective-permute-start(bf16[112,896]{1,0:T(8,128)(2,1)S(1)} %get-tuple-element.88.refs_6_), channel_id=1, source_target_pairs={{0,1},{1,0},{2,3},{3,2},{4,5},{5,4},{6,7},{7,6},{8,9},{9,8},{10,11... | collective-permute-start | bytes 602120 | tf_op jit(solution)/shard_map/ppermute | solution.py:366
  102.3 6.2 %collective-permute-start.36 = (bf16[112,896]{1,0:T(8,128)(2,1)S(1)}, bf16[112,896]{1,0:T(8,128)(2,1)S(1)}, u32[]{:S(2)}, u32[]{:S(2)}) collective-permute-start(bf16[112,896]{1,0:T(8,128)(2,1)S(1)} %get-tuple-element.91.refs_9_), channel_id=1, source_target_pairs={{0,1},{1,0},{2,3},{3,2},{4,5},{5,4},{6,7},{7,6},{8,9},{9,8},{10,11... | collective-permute-start | bytes 602120 | tf_op jit(solution)/shard_map/ppermute | solution.py:366
  102.8 5.8 %collective-permute-start.38 = (bf16[112,896]{1,0:T(8,128)(2,1)S(1)}, bf16[112,896]{1,0:T(8,128)(2,1)S(1)}, u32[]{:S(2)}, u32[]{:S(2)}) collective-permute-start(bf16[112,896]{1,0:T(8,128)(2,1)S(1)} %get-tuple-element.93.refs_11_), channel_id=1, source_target_pairs={{0,1},{1,0},{2,3},{3,2},{4,5},{5,4},{6,7},{7,6},{8,9},{9,8},{10,11... | collective-permute-start | bytes 602120 | tf_op jit(solution)/shard_map/ppermute | solution.py:366
  106.3 4.0 %collective-permute-start.41 = (bf16[128,896]{1,0:T(8,128)(2,1)S(1)}, bf16[128,896]{1,0:T(8,128)(2,1)S(1)}, u32[]{:S(2)}, u32[]{:S(2)}) collective-permute-start(bf16[128,896]{1,0:T(8,128)(2,1)S(1)} %collective-permute-done.25.refs_12_.refs_14_), channel_id=1, source_target_pairs={{0,1},{1,0},{2,3},{3,2},{4,5},{5,4},{6,7},{7,6},{8,9},{9,8},{10,11... | collective-permute-start | bytes 688136 | tf_op jit(solution)/shard_map/ppermute | solution.py:366
  107.9 2.4 %collective-permute-start.42 = (bf16[128,896]{1,0:T(8,128)(2,1)S(1)}, bf16[128,896]{1,0:T(8,128)(2,1)S(1)}, u32[]{:S(2)}, u32[]{:S(2)}) collective-permute-start(bf16[128,896]{1,0:T(8,128)(2,1)S(1)} %collective-permute-done.26.refs_13_.refs_15_), channel_id=1, source_target_pairs={{0,1},{1,0},{2,3},{3,2},{4,5},{5,4},{6,7},{7,6},{8,9},{9,8},{10,11... | collective-permute-start | bytes 688136 | tf_op jit(solution)/shard_map/ppermute | solution.py:366
  107.9 2.3 %collective-permute-start.39 = (bf16[112,896]{1,0:T(8,128)(2,1)S(1)}, bf16[112,896]{1,0:T(8,128)(2,1)S(1)}, u32[]{:S(2)}, u32[]{:S(2)}) collective-permute-start(bf16[112,896]{1,0:T(8,128)(2,1)S(1)} %get-tuple-element.94.refs_12_), channel_id=1, source_target_pairs={{0,1},{1,0},{2,3},{3,2},{4,5},{5,4},{6,7},{7,6},{8,9},{9,8},{10,11... | collective-permute-start | bytes 602120 | tf_op jit(solution)/shard_map/ppermute | solution.py:366
  108.5 1.7 %collective-permute-start.37 = (bf16[112,896]{1,0:T(8,128)(2,1)S(1)}, bf16[112,896]{1,0:T(8,128)(2,1)S(1)}, u32[]{:S(2)}, u32[]{:S(2)}) collective-permute-start(bf16[112,896]{1,0:T(8,128)(2,1)S(1)} %get-tuple-element.92.refs_10_), channel_id=1, source_target_pairs={{0,1},{1,0},{2,3},{3,2},{4,5},{5,4},{6,7},{7,6},{8,9},{9,8},{10,11... | collective-permute-start | bytes 602120 | tf_op jit(solution)/shard_map/ppermute | solution.py:366
  108.6 1.6 %collective-permute-start.40 = (bf16[112,896]{1,0:T(8,128)(2,1)S(1)}, bf16[112,896]{1,0:T(8,128)(2,1)S(1)}, u32[]{:S(2)}, u32[]{:S(2)}) collective-permute-start(bf16[112,896]{1,0:T(8,128)(2,1)S(1)} %get-tuple-element.95.refs_13_), channel_id=1, source_target_pairs={{0,1},{1,0},{2,3},{3,2},{4,5},{5,4},{6,7},{7,6},{8,9},{9,8},{10,11... | collective-permute-start | bytes 602120 | tf_op jit(solution)/shard_map/ppermute | solution.py:366

commit v4 on v3

--- a/solution.py
+++ b/solution.py
@@ -222,7 +222,7 @@
 
 def chain_kernel(count, slab, *refs):
     blocks = refs[: 2 * count]
-    out_ref, whole, turned = refs[2 * count :]
+    out_ref, whole, flipped, turned = refs[2 * count :]
     width = whole.shape[0]
     chips = width // slab // 2
     index, core, position = me(chips)
@@ -247,9 +247,11 @@
     own = contract(picks.astype(BF16), columns, 1, 1)
     start = (own * inverse).astype(BF16)
 
+    flipped[...] = whole[...].T
+
     def apply_once(vector):
         inner = jnp.dot(vector.astype(BF16), whole[...], preferred_element_type=F32) * inverse
-        return contract(inner.astype(BF16), whole[...], 1, 1) * inverse
+        return jnp.dot(inner.astype(BF16), flipped[...], preferred_element_type=F32) * inverse
 
     first = 1.5 * start.astype(F32) - 0.5 * apply_once(start)
     upper = 1.5 * first - 0.5 * apply_once(first)
@@ -374,7 +376,7 @@
         shape((slab, width), BF16),
         [],
         gathered,
-        [shape((width, width), BF16), shape((width, rows), F32)],
+        [shape((width, width), BF16)] * 2 + [shape((width, rows), F32)],
         flops=16 * rows * width * width,
         room=10,
     )

time: 124 us -> 120 us (0.968)
  Pallas kernels: 20.7 us -> 16 us
    pallas_call x23, Pallas kernels: 20.7 us -> 16 us  [call(): pl.pallas_call(kernel, out_shape=outs, in_specs=[SMEM] * len(smem) + [VME...]
  transfers between devices with their start and end apart: 44 -> 44, of which waited for: 19 -> 19; matrix products, arithmetic and copies ran while one was open for 0% -> 0% of each run, Pallas kernels for 4% -> 5%
where the time goes in v4:
time: 120 us
  waiting for transfers between devices  53.8 us (45%)
  starting transfers between devices  46.2 us (38%)
  Pallas kernels  16 us (13%)
  local copies, waits for them, and re-layouts  2.67 us (2%)
    ppermute x22, waiting for transfers between devices, shift(): lax.ppermute(block, 'tok', [(2 * a + c, 2 * b + c) for a, b in pairs for...  42.1 us
    ppermute x22, starting transfers between devices, shift(): lax.ppermute(block, 'tok', [(2 * a + c, 2 * b + c) for a, b in pairs for...  33 us
    pallas_call x23, Pallas kernels, call(): pl.pallas_call(kernel, out_shape=outs, in_specs=[SMEM] * len(smem) + [VME...  16 us
    all_to_all x1, waiting for transfers between devices, shards(): lax.all_to_all(pieces, 'tok', split_axis=0, concat_axis=0, tiled=True, ax...  8 us
    all_to_all x1, starting transfers between devices, shards(): lax.all_to_all(pieces, 'tok', split_axis=0, concat_axis=0, tiled=True, ax...  6.22 us
    ppermute x3, starting transfers between devices, rotate(): return (halves, [rotated, lax.ppermute(rotated, 'ckpt', [(0, 1), (1, 0)])])  4.65 us
    unnamed x6, local copies, waits for them, and re-layouts  2.66 us
  transfers between devices with their start and end apart: 44, of which 19 were waited for; matrix products, arithmetic and copies ran while one was open for 0% of the time, Pallas kernels for 5%

profile of v4, /device:TPU:0, one launch (start us, length us, event | category | flops | bytes accessed | tf_op | source)
XLA Modules:
  0.0 119.5 jit_solution(5822017543868600142)
XLA Ops:
  0.6 1.0 copy-done
  1.7 0.7 copy-done.2
  2.6 3.0 %collective-permute-start.1 = (bf16[128,1792]{1,0:T(8,128)(2,1)S(1)}, bf16[128,1792]{1,0:T(8,128)(2,1)S(1)}, u32[]{:S(2)}, u32[]{:S(2)}) collective-permute-start(bf16[128,1792]{1,0:T(8,128)(2,1)S(1)} %shard_map.50.refs_0_), channel_id=1, source_target_pairs={{0,2},{1,3},{4,0},{5,1},{8,4},{9,5},{12,8},{13,9},{14,12},{15,13},... | collective-permute-start | bytes 1376264 | tf_op jit(solution)/shard_map/ppermute | solution.py:65
  5.8 1.0 copy-done.1
  6.8 1.0 shard_map.51
  7.8 6.2 %all-to-all-start = ((bf16[8,112,224]{2,1,0:T(8,128)(2,1)}), bf16[8,112,224]{2,1,0:T(8,128)(2,1)S(1)}, u32[]{:S(2)}, u32[]{:S(2)}) async-start(bf16[8,112,224]{2,1,0:T(8,128)(2,1)} %shard_map.51), calls=%async_computation | async-start | bytes 917504 | tf_op jit(solution)/shard_map/all_to_all | solution.py:291
  14.0 2.7 %collective-permute-done.1.refs_2_ = bf16[128,1792]{1,0:T(8,128)(2,1)S(1)} collective-permute-done((bf16[128,1792]{1,0:T(8,128)(2,1)S(1)}, bf16[128,1792]{1,0:T(8,128)(2,1)S(1)}, u32[]{:S(2)}, u32[]{:S(2)}) %collective-permute-start.1) | collective-permute-done | bytes 458784 | tf_op jit(solution)/shard_map/ppermute | solution.py:65
  16.7 2.5 %collective-permute-start.3 = (bf16[128,1792]{1,0:T(8,128)(2,1)S(1)}, bf16[128,1792]{1,0:T(8,128)(2,1)S(1)}, u32[]{:S(2)}, u32[]{:S(2)}) collective-permute-start(bf16[128,1792]{1,0:T(8,128)(2,1)S(1)} %collective-permute-done.1.refs_2_), channel_id=1, source_target_pairs={{0,2},{1,3},{4,0},{5,1},{8,4},{9,5},{12,8},{13,9},{14,12},{15,13},... | collective-permute-start | bytes 1376264 | tf_op jit(solution)/shard_map/ppermute | solution.py:65
  19.1 1.4 %collective-permute-start.2 = (bf16[128,1792]{1,0:T(8,128)(2,1)S(1)}, bf16[128,1792]{1,0:T(8,128)(2,1)S(1)}, u32[]{:S(2)}, u32[]{:S(2)}) collective-permute-start(bf16[128,1792]{1,0:T(8,128)(2,1)S(1)} %collective-permute-done.refs_1_), channel_id=1, source_target_pairs={{0,4},{1,5},{4,8},{5,9},{8,12},{9,13},{12,14},{13,15},{14,10},{15,... | collective-permute-start | bytes 1376264 | tf_op jit(solution)/shard_map/ppermute | solution.py:65
  20.5 8.0 %all-to-all-done = bf16[8,112,224]{2,1,0:T(8,128)(2,1)S(1)} async-done(((bf16[8,112,224]{2,1,0:T(8,128)(2,1)}), bf16[8,112,224]{2,1,0:T(8,128)(2,1)S(1)}, u32[]{:S(2)}, u32[]{:S(2)}) %all-to-all-start) | async-done | bytes 401440 | tf_op jit(solution)/shard_map/all_to_all | solution.py:291
  28.5 5.2 %collective-permute-done.3.refs_4_ = bf16[128,1792]{1,0:T(8,128)(2,1)S(1)} collective-permute-done((bf16[128,1792]{1,0:T(8,128)(2,1)S(1)}, bf16[128,1792]{1,0:T(8,128)(2,1)S(1)}, u32[]{:S(2)}, u32[]{:S(2)}) %collective-permute-start.3) | collective-permute-done | bytes 458784 | tf_op jit(solution)/shard_map/ppermute | solution.py:65
  34.3 3.4 %collective-permute-start.6 = (bf16[128,1792]{1,0:T(8,128)(2,1)S(1)}, bf16[128,1792]{1,0:T(8,128)(2,1)S(1)}, u32[]{:S(2)}, u32[]{:S(2)}) collective-permute-start(bf16[128,1792]{1,0:T(8,128)(2,1)S(1)} %collective-permute-done.2.refs_3_), channel_id=1, source_target_pairs={{0,4},{1,5},{4,8},{5,9},{8,12},{9,13},{12,14},{13,15},{14,10},{15,... | collective-permute-start | bytes 1376264 | tf_op jit(solution)/shard_map/ppermute | solution.py:65
  37.6 0.9 shard_map.52.refs_5_
  38.5 1.6 %collective-permute-start.5 = (bf16[640,224]{1,0:T(8,128)(2,1)S(1)}, bf16[640,224]{1,0:T(8,128)(2,1)S(1)}, u32[]{:S(2)}, u32[]{:S(2)}) collective-permute-start(bf16[640,224]{1,0:T(8,128)(2,1)S(1)} %shard_map.52.refs_5_), channel_id=1, source_target_pairs={{0,16},{16,0},{1,17},{17,1},{2,18},{18,2},{3,19},{19,3},{4,20},{20... | collective-permute-start | bytes 860168 | tf_op jit(solution)/shard_map/ppermute | solution.py:313
  40.1 7.0 %collective-permute-done.7.behind_ref.refs_1_ = bf16[128,1792]{1,0:T(8,128)(2,1)S(1)} collective-permute-done((bf16[128,1792]{1,0:T(8,128)(2,1)S(1)}, bf16[128,1792]{1,0:T(8,128)(2,1)S(1)}, u32[]{:S(2)}, u32[]{:S(2)}) %collective-permute-start.7) | collective-permute-done | bytes 458784 | tf_op jit(solution)/shard_map/ppermute | solution.py:65
  47.6 1.3 %collective-permute-start.8 = (bf16[64,1792]{1,0:T(8,128)(2,1)S(1)}, bf16[64,1792]{1,0:T(8,128)(2,1)S(1)}, u32[]{:S(2)}, u32[]{:S(2)}) collective-permute-start(bf16[64,1792]{1,0:T(8,128)(2,1)S(1)} %get-tuple-element.50), channel_id=1, source_target_pairs={{0,4},{1,5},{4,8},{5,9},{8,12},{9,13},{12,14},{13,15},{14,10},{15,... | collective-permute-start | bytes 688136 | tf_op jit(solution)/shard_map/ppermute | solution.py:65
  49.0 1.3 %collective-permute-start.9 = (bf16[64,1792]{1,0:T(8,128)(2,1)S(1)}, bf16[64,1792]{1,0:T(8,128)(2,1)S(1)}, u32[]{:S(2)}, u32[]{:S(2)}) collective-permute-start(bf16[64,1792]{1,0:T(8,128)(2,1)S(1)} %get-tuple-element.51), channel_id=1, source_target_pairs={{0,2},{1,3},{4,0},{5,1},{8,4},{9,5},{12,8},{13,9},{14,12},{15,13},... | collective-permute-start | bytes 688136 | tf_op jit(solution)/shard_map/ppermute | solution.py:65
  50.2 0.5 shard_map.55.refs_4_
  50.8 1.5 %collective-permute-start.10 = (bf16[256,224]{1,0:T(8,128)(2,1)S(1)}, bf16[256,224]{1,0:T(8,128)(2,1)S(1)}, u32[]{:S(2)}, u32[]{:S(2)}) collective-permute-start(bf16[256,224]{1,0:T(8,128)(2,1)S(1)} %shard_map.55.refs_4_), channel_id=1, source_target_pairs={{0,16},{16,0},{1,17},{17,1},{2,18},{18,2},{3,19},{19,3},{4,20},{20... | collective-permute-start | bytes 344072 | tf_op jit(solution)/shard_map/ppermute | solution.py:313
  52.3 1.8 %collective-permute-done.8.refs_0_.refs_2_ = bf16[64,1792]{1,0:T(8,128)(2,1)S(1)} collective-permute-done((bf16[64,1792]{1,0:T(8,128)(2,1)S(1)}, bf16[64,1792]{1,0:T(8,128)(2,1)S(1)}, u32[]{:S(2)}, u32[]{:S(2)}) %collective-permute-start.8) | collective-permute-done | bytes 229408 | tf_op jit(solution)/shard_map/ppermute | solution.py:65
  54.2 0.8 collective-permute-done.9.refs_1_.refs_3_
  55.5 1.6 %collective-permute-start.11 = (bf16[128,224]{1,0:T(8,128)(2,1)S(1)}, bf16[128,224]{1,0:T(8,128)(2,1)S(1)}, u32[]{:S(2)}, u32[]{:S(2)}) collective-permute-start(bf16[128,224]{1,0:T(8,128)(2,1)S(1)} %shard_map.56.refs_6_), channel_id=1, source_target_pairs={{0,16},{16,0},{1,17},{17,1},{2,18},{18,2},{3,19},{19,3},{4,20},{20... | collective-permute-start | bytes 172040 | tf_op jit(solution)/shard_map/ppermute | solution.py:313
  57.0 0.9 shard_map.53
  58.0 1.9 %collective-permute-done.11.refs_7_ = bf16[128,224]{1,0:T(8,128)(2,1)S(1)} collective-permute-done((bf16[128,224]{1,0:T(8,128)(2,1)S(1)}, bf16[128,224]{1,0:T(8,128)(2,1)S(1)}, u32[]{:S(2)}, u32[]{:S(2)}) %collective-permute-start.11) | collective-permute-done | bytes 57376 | tf_op jit(solution)/shard_map/ppermute | solution.py:313
  59.8 0.7 shard_map.57
  60.6 1.7 %collective-permute-done.12.come_ref = bf16[112,1792]{1,0:T(8,128)(2,1)S(1)} collective-permute-done((bf16[112,1792]{1,0:T(8,128)(2,1)S(1)}, bf16[112,1792]{1,0:T(8,128)(2,1)S(1)}, u32[]{:S(2)}, u32[]{:S(2)}) %collective-permute-start.12) | collective-permute-done | bytes 401440 | tf_op jit(solution)/shard_map/ppermute | solution.py:338
  62.6 1.8 %collective-permute-start.13 = (bf16[176,896]{1,0:T(8,128)(2,1)S(1)}, bf16[176,896]{1,0:T(8,128)(2,1)S(1)}, u32[]{:S(2)}, u32[]{:S(2)}) collective-permute-start(bf16[176,896]{1,0:T(8,128)(2,1)S(1)} %get-tuple-element.56), channel_id=1, source_target_pairs={{0,4},{1,5},{4,8},{5,9},{8,12},{9,13},{12,14},{13,15},{14,10},{15,... | collective-permute-start | bytes 946184 | tf_op jit(solution)/shard_map/ppermute | solution.py:65
  64.7 1.7 %collective-permute-start.14 = (bf16[160,896]{1,0:T(8,128)(2,1)S(1)}, bf16[160,896]{1,0:T(8,128)(2,1)S(1)}, u32[]{:S(2)}, u32[]{:S(2)}) collective-permute-start(bf16[160,896]{1,0:T(8,128)(2,1)S(1)} %get-tuple-element.58), channel_id=1, source_target_pairs={{0,4},{1,5},{4,8},{5,9},{8,12},{9,13},{12,14},{13,15},{14,10},{15,... | collective-permute-start | bytes 860168 | tf_op jit(solution)/shard_map/ppermute | solution.py:65
  66.7 6.2 %collective-permute-done.13.message_ref = bf16[176,896]{1,0:T(8,128)(2,1)S(1)} collective-permute-done((bf16[176,896]{1,0:T(8,128)(2,1)S(1)}, bf16[176,896]{1,0:T(8,128)(2,1)S(1)}, u32[]{:S(2)}, u32[]{:S(2)}) %collective-permute-start.13) | collective-permute-done | bytes 315424 | tf_op jit(solution)/shard_map/ppermute | solution.py:65
  73.0 1.8 %collective-permute-start.17 = (bf16[160,896]{1,0:T(8,128)(2,1)S(1)}, bf16[160,896]{1,0:T(8,128)(2,1)S(1)}, u32[]{:S(2)}, u32[]{:S(2)}) collective-permute-start(bf16[160,896]{1,0:T(8,128)(2,1)S(1)} %get-tuple-element.64), channel_id=1, source_target_pairs={{0,4},{1,5},{4,8},{5,9},{8,12},{9,13},{12,14},{13,15},{14,10},{15,... | collective-permute-start | bytes 860168 | tf_op jit(solution)/shard_map/ppermute | solution.py:65
  75.2 3.9 %collective-permute-done.14.message_ref = bf16[160,896]{1,0:T(8,128)(2,1)S(1)} collective-permute-done((bf16[160,896]{1,0:T(8,128)(2,1)S(1)}, bf16[160,896]{1,0:T(8,128)(2,1)S(1)}, u32[]{:S(2)}, u32[]{:S(2)}) %collective-permute-start.14) | collective-permute-done | bytes 286752 | tf_op jit(solution)/shard_map/ppermute | solution.py:65
  79.1 1.8 %collective-permute-start.18 = (bf16[144,896]{1,0:T(8,128)(2,1)S(1)}, bf16[144,896]{1,0:T(8,128)(2,1)S(1)}, u32[]{:S(2)}, u32[]{:S(2)}) collective-permute-start(bf16[144,896]{1,0:T(8,128)(2,1)S(1)} %get-tuple-element.66), channel_id=1, source_target_pairs={{0,4},{1,5},{4,8},{5,9},{8,12},{9,13},{12,14},{13,15},{14,10},{15,... | collective-permute-start | bytes 774152 | tf_op jit(solution)/shard_map/ppermute | solution.py:65
  81.5 3.7 %collective-permute-done.17.message_ref = bf16[160,896]{1,0:T(8,128)(2,1)S(1)} collective-permute-done((bf16[160,896]{1,0:T(8,128)(2,1)S(1)}, bf16[160,896]{1,0:T(8,128)(2,1)S(1)}, u32[]{:S(2)}, u32[]{:S(2)}) %collective-permute-start.17) | collective-permute-done | bytes 286752 | tf_op jit(solution)/shard_map/ppermute | solution.py:65
  85.3 1.3 %collective-permute-start.19 = (bf16[144,896]{1,0:T(8,128)(2,1)S(1)}, bf16[144,896]{1,0:T(8,128)(2,1)S(1)}, u32[]{:S(2)}, u32[]{:S(2)}) collective-permute-start(bf16[144,896]{1,0:T(8,128)(2,1)S(1)} %get-tuple-element.68), channel_id=1, source_target_pairs={{0,2},{1,3},{4,0},{5,1},{8,4},{9,5},{12,8},{13,9},{14,12},{15,13},... | collective-permute-start | bytes 774152 | tf_op jit(solution)/shard_map/ppermute | solution.py:65
  86.6 0.8 collective-permute-start.21
  87.4 1.3 %collective-permute-start.24 = (bf16[144,896]{1,0:T(8,128)(2,1)S(1)}, bf16[144,896]{1,0:T(8,128)(2,1)S(1)}, u32[]{:S(2)}, u32[]{:S(2)}) collective-permute-start(bf16[144,896]{1,0:T(8,128)(2,1)S(1)} %get-tuple-element.78), channel_id=1, source_target_pairs={{0,2},{1,3},{4,0},{5,1},{8,4},{9,5},{12,8},{13,9},{14,12},{15,13},... | collective-permute-start | bytes 774152 | tf_op jit(solution)/shard_map/ppermute | solution.py:65
  88.7 1.3 %collective-permute-done.18.message_ref = bf16[144,896]{1,0:T(8,128)(2,1)S(1)} collective-permute-done((bf16[144,896]{1,0:T(8,128)(2,1)S(1)}, bf16[144,896]{1,0:T(8,128)(2,1)S(1)}, u32[]{:S(2)}, u32[]{:S(2)}) %collective-permute-start.18) | collective-permute-done | bytes 258080 | tf_op jit(solution)/shard_map/ppermute | solution.py:65
  90.1 2.5 %collective-permute-start.22 = (bf16[128,896]{1,0:T(8,128)(2,1)S(1)}, bf16[128,896]{1,0:T(8,128)(2,1)S(1)}, u32[]{:S(2)}, u32[]{:S(2)}) collective-permute-start(bf16[128,896]{1,0:T(8,128)(2,1)S(1)} %get-tuple-element.74), channel_id=1, source_target_pairs={{0,4},{1,5},{4,8},{5,9},{8,12},{9,13},{12,14},{13,15},{14,10},{15,... | collective-permute-start | bytes 688136 | tf_op jit(solution)/shard_map/ppermute | solution.py:65
  92.6 0.8 collective-permute-done.19.message_ref
  93.5 2.0 %collective-permute-start.23 = (bf16[128,896]{1,0:T(8,128)(2,1)S(1)}, bf16[128,896]{1,0:T(8,128)(2,1)S(1)}, u32[]{:S(2)}, u32[]{:S(2)}) collective-permute-start(bf16[128,896]{1,0:T(8,128)(2,1)S(1)} %get-tuple-element.76), channel_id=1, source_target_pairs={{0,2},{1,3},{4,0},{5,1},{8,4},{9,5},{12,8},{13,9},{14,12},{15,13},... | collective-permute-start | bytes 688136 | tf_op jit(solution)/shard_map/ppermute | solution.py:65
  95.8 2.3 %collective-permute-done.24.message_ref = bf16[144,896]{1,0:T(8,128)(2,1)S(1)} collective-permute-done((bf16[144,896]{1,0:T(8,128)(2,1)S(1)}, bf16[144,896]{1,0:T(8,128)(2,1)S(1)}, u32[]{:S(2)}, u32[]{:S(2)}) %collective-permute-start.24) | collective-permute-done | bytes 258080 | tf_op jit(solution)/shard_map/ppermute | solution.py:65
  98.2 1.8 %collective-permute-start.25 = (bf16[128,896]{1,0:T(8,128)(2,1)S(1)}, bf16[128,896]{1,0:T(8,128)(2,1)S(1)}, u32[]{:S(2)}, u32[]{:S(2)}) collective-permute-start(bf16[128,896]{1,0:T(8,128)(2,1)S(1)} %get-tuple-element.80), channel_id=1, source_target_pairs={{0,4},{1,5},{4,8},{5,9},{8,12},{9,13},{12,14},{13,15},{14,10},{15,... | collective-permute-start | bytes 688136 | tf_op jit(solution)/shard_map/ppermute | solution.py:65
  100.5 1.7 %collective-permute-start.26 = (bf16[128,896]{1,0:T(8,128)(2,1)S(1)}, bf16[128,896]{1,0:T(8,128)(2,1)S(1)}, u32[]{:S(2)}, u32[]{:S(2)}) collective-permute-start(bf16[128,896]{1,0:T(8,128)(2,1)S(1)} %get-tuple-element.81), channel_id=1, source_target_pairs={{0,2},{1,3},{4,0},{5,1},{8,4},{9,5},{12,8},{13,9},{14,12},{15,13},... | collective-permute-start | bytes 688136 | tf_op jit(solution)/shard_map/ppermute | solution.py:65
  102.9 3.4 %collective-permute-done.25.refs_12_.refs_14_ = bf16[128,896]{1,0:T(8,128)(2,1)S(1)} collective-permute-done((bf16[128,896]{1,0:T(8,128)(2,1)S(1)}, bf16[128,896]{1,0:T(8,128)(2,1)S(1)}, u32[]{:S(2)}, u32[]{:S(2)}) %collective-permute-start.25) | collective-permute-done | bytes 229408 | tf_op jit(solution)/shard_map/ppermute | solution.py:65
  106.3 1.6 %collective-permute-done.26.refs_13_.refs_15_ = bf16[128,896]{1,0:T(8,128)(2,1)S(1)} collective-permute-done((bf16[128,896]{1,0:T(8,128)(2,1)S(1)}, bf16[128,896]{1,0:T(8,128)(2,1)S(1)}, u32[]{:S(2)}, u32[]{:S(2)}) %collective-permute-start.26) | collective-permute-done | bytes 229408 | tf_op jit(solution)/shard_map/ppermute | solution.py:65
  107.9 0.6 collective-permute-start.39
  109.0 1.2 shard_map.71
  110.2 9.3 %shard_map.72 = bf16[112,1792]{1,0:T(8,128)(2,1)} custom-call(bf16[112,896]{1,0:T(8,128)(2,1)S(1)} %get-tuple-element.82.refs_0_, bf16[112,896]{1,0:T(8,128)(2,1)S(1)} %get-tuple-element.83.refs_1_, bf16[112,896]{1,0:T(8,128)(2,1)S(1)} %get-tuple-element.84.refs_2_, bf16[112,896]{1,0:T(8,128)(2,1)S(1)} %get-tuple-element.85.refs_3_, ...), custom_call_target="tpu_custom_call" | custom-call | flops 6576668672 | bytes 20701184 | tf_op jit(solution)/shard_map/pallas_call | solution.py:34
  (70 shorter events, 6.2 us)
Async XLA Ops:
  0.6 1.0 copy-start
  1.6 0.7 copy-start.2
  2.6 14.0 %collective-permute-start.1 = (bf16[128,1792]{1,0:T(8,128)(2,1)S(1)}, bf16[128,1792]{1,0:T(8,128)(2,1)S(1)}, u32[]{:S(2)}, u32[]{:S(2)}) collective-permute-start(bf16[128,1792]{1,0:T(8,128)(2,1)S(1)} %shard_map.50.refs_0_), channel_id=1, source_target_pairs={{0,2},{1,3},{4,0},{5,1},{8,4},{9,5},{12,8},{13,9},{14,12},{15,13},... | collective-permute-start | bytes 1376264 | tf_op jit(solution)/shard_map/ppermute | solution.py:65
  5.7 13.5 %collective-permute-start = (bf16[128,1792]{1,0:T(8,128)(2,1)S(1)}, bf16[128,1792]{1,0:T(8,128)(2,1)S(1)}, u32[]{:S(2)}, u32[]{:S(2)}) collective-permute-start(bf16[128,1792]{1,0:T(8,128)(2,1)S(1)} %shard_map.50.refs_0_), channel_id=1, source_target_pairs={{0,4},{1,5},{4,8},{5,9},{8,12},{9,13},{12,14},{13,15},{14,10},{15,... | collective-permute-start | bytes 1376264 | tf_op jit(solution)/shard_map/ppermute | solution.py:65
  5.8 1.0 copy-start.1
  7.8 20.8 %all-to-all-start = ((bf16[8,112,224]{2,1,0:T(8,128)(2,1)}), bf16[8,112,224]{2,1,0:T(8,128)(2,1)S(1)}, u32[]{:S(2)}, u32[]{:S(2)}) async-start(bf16[8,112,224]{2,1,0:T(8,128)(2,1)} %shard_map.51), calls=%async_computation | async-start | bytes 917504 | tf_op jit(solution)/shard_map/all_to_all | solution.py:291
  16.7 17.1 %collective-permute-start.3 = (bf16[128,1792]{1,0:T(8,128)(2,1)S(1)}, bf16[128,1792]{1,0:T(8,128)(2,1)S(1)}, u32[]{:S(2)}, u32[]{:S(2)}) collective-permute-start(bf16[128,1792]{1,0:T(8,128)(2,1)S(1)} %collective-permute-done.1.refs_2_), channel_id=1, source_target_pairs={{0,2},{1,3},{4,0},{5,1},{8,4},{9,5},{12,8},{13,9},{14,12},{15,13},... | collective-permute-start | bytes 1376264 | tf_op jit(solution)/shard_map/ppermute | solution.py:65
  19.1 15.1 %collective-permute-start.2 = (bf16[128,1792]{1,0:T(8,128)(2,1)S(1)}, bf16[128,1792]{1,0:T(8,128)(2,1)S(1)}, u32[]{:S(2)}, u32[]{:S(2)}) collective-permute-start(bf16[128,1792]{1,0:T(8,128)(2,1)S(1)} %collective-permute-done.refs_1_), channel_id=1, source_target_pairs={{0,4},{1,5},{4,8},{5,9},{8,12},{9,13},{12,14},{13,15},{14,10},{15,... | collective-permute-start | bytes 1376264 | tf_op jit(solution)/shard_map/ppermute | solution.py:65
  28.5 9.1 %collective-permute-start.4 = (bf16[896,224]{1,0:T(8,128)(2,1)S(1)}, bf16[896,224]{1,0:T(8,128)(2,1)S(1)}, u32[]{:S(2)}, u32[]{:S(2)}) collective-permute-start(bf16[896,224]{1,0:T(8,128)(2,1)S(1)} %bitcast.5), channel_id=1, source_target_pairs={{0,1},{1,0},{2,3},{3,2},{4,5},{5,4},{6,7},{7,6},{8,9},{9,8},{10,11... | collective-permute-start | bytes 1204232 | tf_op jit(solution)/shard_map/ppermute | solution.py:296
  33.7 13.4 %collective-permute-start.7 = (bf16[128,1792]{1,0:T(8,128)(2,1)S(1)}, bf16[128,1792]{1,0:T(8,128)(2,1)S(1)}, u32[]{:S(2)}, u32[]{:S(2)}) collective-permute-start(bf16[128,1792]{1,0:T(8,128)(2,1)S(1)} %collective-permute-done.3.refs_4_), channel_id=1, source_target_pairs={{0,2},{1,3},{4,0},{5,1},{8,4},{9,5},{12,8},{13,9},{14,12},{15,13},... | collective-permute-start | bytes 1376264 | tf_op jit(solution)/shard_map/ppermute | solution.py:65
  34.3 13.4 %collective-permute-start.6 = (bf16[128,1792]{1,0:T(8,128)(2,1)S(1)}, bf16[128,1792]{1,0:T(8,128)(2,1)S(1)}, u32[]{:S(2)}, u32[]{:S(2)}) collective-permute-start(bf16[128,1792]{1,0:T(8,128)(2,1)S(1)} %collective-permute-done.2.refs_3_), channel_id=1, source_target_pairs={{0,4},{1,5},{4,8},{5,9},{8,12},{9,13},{12,14},{13,15},{14,10},{15,... | collective-permute-start | bytes 1376264 | tf_op jit(solution)/shard_map/ppermute | solution.py:65
  38.5 18.5 %collective-permute-start.5 = (bf16[640,224]{1,0:T(8,128)(2,1)S(1)}, bf16[640,224]{1,0:T(8,128)(2,1)S(1)}, u32[]{:S(2)}, u32[]{:S(2)}) collective-permute-start(bf16[640,224]{1,0:T(8,128)(2,1)S(1)} %shard_map.52.refs_5_), channel_id=1, source_target_pairs={{0,16},{16,0},{1,17},{17,1},{2,18},{18,2},{3,19},{19,3},{4,20},{20... | collective-permute-start | bytes 860168 | tf_op jit(solution)/shard_map/ppermute | solution.py:313
  47.6 6.5 %collective-permute-start.8 = (bf16[64,1792]{1,0:T(8,128)(2,1)S(1)}, bf16[64,1792]{1,0:T(8,128)(2,1)S(1)}, u32[]{:S(2)}, u32[]{:S(2)}) collective-permute-start(bf16[64,1792]{1,0:T(8,128)(2,1)S(1)} %get-tuple-element.50), channel_id=1, source_target_pairs={{0,4},{1,5},{4,8},{5,9},{8,12},{9,13},{12,14},{13,15},{14,10},{15,... | collective-permute-start | bytes 688136 | tf_op jit(solution)/shard_map/ppermute | solution.py:65
  49.0 6.0 %collective-permute-start.9 = (bf16[64,1792]{1,0:T(8,128)(2,1)S(1)}, bf16[64,1792]{1,0:T(8,128)(2,1)S(1)}, u32[]{:S(2)}, u32[]{:S(2)}) collective-permute-start(bf16[64,1792]{1,0:T(8,128)(2,1)S(1)} %get-tuple-element.51), channel_id=1, source_target_pairs={{0,2},{1,3},{4,0},{5,1},{8,4},{9,5},{12,8},{13,9},{14,12},{15,13},... | collective-permute-start | bytes 688136 | tf_op jit(solution)/shard_map/ppermute | solution.py:65
  50.8 7.1 %collective-permute-start.10 = (bf16[256,224]{1,0:T(8,128)(2,1)S(1)}, bf16[256,224]{1,0:T(8,128)(2,1)S(1)}, u32[]{:S(2)}, u32[]{:S(2)}) collective-permute-start(bf16[256,224]{1,0:T(8,128)(2,1)S(1)} %shard_map.55.refs_4_), channel_id=1, source_target_pairs={{0,16},{16,0},{1,17},{17,1},{2,18},{18,2},{3,19},{19,3},{4,20},{20... | collective-permute-start | bytes 344072 | tf_op jit(solution)/shard_map/ppermute | solution.py:313
  55.5 4.3 %collective-permute-start.11 = (bf16[128,224]{1,0:T(8,128)(2,1)S(1)}, bf16[128,224]{1,0:T(8,128)(2,1)S(1)}, u32[]{:S(2)}, u32[]{:S(2)}) collective-permute-start(bf16[128,224]{1,0:T(8,128)(2,1)S(1)} %shard_map.56.refs_6_), channel_id=1, source_target_pairs={{0,16},{16,0},{1,17},{17,1},{2,18},{18,2},{3,19},{19,3},{4,20},{20... | collective-permute-start | bytes 172040 | tf_op jit(solution)/shard_map/ppermute | solution.py:313
  60.5 1.8 %collective-permute-start.12 = (bf16[112,1792]{1,0:T(8,128)(2,1)S(1)}, bf16[112,1792]{1,0:T(8,128)(2,1)S(1)}, u32[]{:S(2)}, u32[]{:S(2)}) collective-permute-start(bf16[112,1792]{1,0:T(8,128)(2,1)S(1)} %get-tuple-element.54), channel_id=1, source_target_pairs={{0,1},{1,0},{2,3},{3,2},{4,5},{5,4},{6,7},{7,6},{8,9},{9,8},{10,11... | collective-permute-start | bytes 1204232 | tf_op jit(solution)/shard_map/ppermute | solution.py:338
  62.6 10.3 %collective-permute-start.13 = (bf16[176,896]{1,0:T(8,128)(2,1)S(1)}, bf16[176,896]{1,0:T(8,128)(2,1)S(1)}, u32[]{:S(2)}, u32[]{:S(2)}) collective-permute-start(bf16[176,896]{1,0:T(8,128)(2,1)S(1)} %get-tuple-element.56), channel_id=1, source_target_pairs={{0,4},{1,5},{4,8},{5,9},{8,12},{9,13},{12,14},{13,15},{14,10},{15,... | collective-permute-start | bytes 946184 | tf_op jit(solution)/shard_map/ppermute | solution.py:65
  64.4 10.4 %collective-permute-start.16 = (bf16[176,896]{1,0:T(8,128)(2,1)S(1)}, bf16[176,896]{1,0:T(8,128)(2,1)S(1)}, u32[]{:S(2)}, u32[]{:S(2)}) collective-permute-start(bf16[176,896]{1,0:T(8,128)(2,1)S(1)} %get-tuple-element.62), channel_id=1, source_target_pairs={{0,2},{1,3},{4,0},{5,1},{8,4},{9,5},{12,8},{13,9},{14,12},{15,13},... | collective-permute-start | bytes 946184 | tf_op jit(solution)/shard_map/ppermute | solution.py:65
  64.7 14.4 %collective-permute-start.14 = (bf16[160,896]{1,0:T(8,128)(2,1)S(1)}, bf16[160,896]{1,0:T(8,128)(2,1)S(1)}, u32[]{:S(2)}, u32[]{:S(2)}) collective-permute-start(bf16[160,896]{1,0:T(8,128)(2,1)S(1)} %get-tuple-element.58), channel_id=1, source_target_pairs={{0,4},{1,5},{4,8},{5,9},{8,12},{9,13},{12,14},{13,15},{14,10},{15,... | collective-permute-start | bytes 860168 | tf_op jit(solution)/shard_map/ppermute | solution.py:65
  66.4 14.5 %collective-permute-start.15 = (bf16[160,896]{1,0:T(8,128)(2,1)S(1)}, bf16[160,896]{1,0:T(8,128)(2,1)S(1)}, u32[]{:S(2)}, u32[]{:S(2)}) collective-permute-start(bf16[160,896]{1,0:T(8,128)(2,1)S(1)} %get-tuple-element.60), channel_id=1, source_target_pairs={{0,2},{1,3},{4,0},{5,1},{8,4},{9,5},{12,8},{13,9},{14,12},{15,13},... | collective-permute-start | bytes 860168 | tf_op jit(solution)/shard_map/ppermute | solution.py:65
  66.7 14.2 %collective-permute-start.27 = (bf16[112,896]{1,0:T(8,128)(2,1)S(1)}, bf16[112,896]{1,0:T(8,128)(2,1)S(1)}, u32[]{:S(2)}, u32[]{:S(2)}) collective-permute-start(bf16[112,896]{1,0:T(8,128)(2,1)S(1)} %get-tuple-element.82.refs_0_), channel_id=1, source_target_pairs={{0,1},{1,0},{2,3},{3,2},{4,5},{5,4},{6,7},{7,6},{8,9},{9,8},{10,11... | collective-permute-start | bytes 602120 | tf_op jit(solution)/shard_map/ppermute | solution.py:368
  73.0 12.2 %collective-permute-start.17 = (bf16[160,896]{1,0:T(8,128)(2,1)S(1)}, bf16[160,896]{1,0:T(8,128)(2,1)S(1)}, u32[]{:S(2)}, u32[]{:S(2)}) collective-permute-start(bf16[160,896]{1,0:T(8,128)(2,1)S(1)} %get-tuple-element.64), channel_id=1, source_target_pairs={{0,4},{1,5},{4,8},{5,9},{8,12},{9,13},{12,14},{13,15},{14,10},{15,... | collective-permute-start | bytes 860168 | tf_op jit(solution)/shard_map/ppermute | solution.py:65
  74.8 11.7 %collective-permute-start.20 = (bf16[160,896]{1,0:T(8,128)(2,1)S(1)}, bf16[160,896]{1,0:T(8,128)(2,1)S(1)}, u32[]{:S(2)}, u32[]{:S(2)}) collective-permute-start(bf16[160,896]{1,0:T(8,128)(2,1)S(1)} %get-tuple-element.70), channel_id=1, source_target_pairs={{0,2},{1,3},{4,0},{5,1},{8,4},{9,5},{12,8},{13,9},{14,12},{15,13},... | collective-permute-start | bytes 860168 | tf_op jit(solution)/shard_map/ppermute | solution.py:65
  79.1 10.9 %collective-permute-start.18 = (bf16[144,896]{1,0:T(8,128)(2,1)S(1)}, bf16[144,896]{1,0:T(8,128)(2,1)S(1)}, u32[]{:S(2)}, u32[]{:S(2)}) collective-permute-start(bf16[144,896]{1,0:T(8,128)(2,1)S(1)} %get-tuple-element.66), channel_id=1, source_target_pairs={{0,4},{1,5},{4,8},{5,9},{8,12},{9,13},{12,14},{13,15},{14,10},{15,... | collective-permute-start | bytes 774152 | tf_op jit(solution)/shard_map/ppermute | solution.py:65
  80.9 5.7 %collective-permute-start.28 = (bf16[112,896]{1,0:T(8,128)(2,1)S(1)}, bf16[112,896]{1,0:T(8,128)(2,1)S(1)}, u32[]{:S(2)}, u32[]{:S(2)}) collective-permute-start(bf16[112,896]{1,0:T(8,128)(2,1)S(1)} %get-tuple-element.83.refs_1_), channel_id=1, source_target_pairs={{0,1},{1,0},{2,3},{3,2},{4,5},{5,4},{6,7},{7,6},{8,9},{9,8},{10,11... | collective-permute-start | bytes 602120 | tf_op jit(solution)/shard_map/ppermute | solution.py:368
  81.0 6.5 %collective-permute-start.30 = (bf16[112,896]{1,0:T(8,128)(2,1)S(1)}, bf16[112,896]{1,0:T(8,128)(2,1)S(1)}, u32[]{:S(2)}, u32[]{:S(2)}) collective-permute-start(bf16[112,896]{1,0:T(8,128)(2,1)S(1)} %get-tuple-element.85.refs_3_), channel_id=1, source_target_pairs={{0,1},{1,0},{2,3},{3,2},{4,5},{5,4},{6,7},{7,6},{8,9},{9,8},{10,11... | collective-permute-start | bytes 602120 | tf_op jit(solution)/shard_map/ppermute | solution.py:368
  85.3 8.2 %collective-permute-start.19 = (bf16[144,896]{1,0:T(8,128)(2,1)S(1)}, bf16[144,896]{1,0:T(8,128)(2,1)S(1)}, u32[]{:S(2)}, u32[]{:S(2)}) collective-permute-start(bf16[144,896]{1,0:T(8,128)(2,1)S(1)} %get-tuple-element.68), channel_id=1, source_target_pairs={{0,2},{1,3},{4,0},{5,1},{8,4},{9,5},{12,8},{13,9},{14,12},{15,13},... | collective-permute-start | bytes 774152 | tf_op jit(solution)/shard_map/ppermute | solution.py:65
  86.5 3.6 %collective-permute-start.31 = (bf16[112,896]{1,0:T(8,128)(2,1)S(1)}, bf16[112,896]{1,0:T(8,128)(2,1)S(1)}, u32[]{:S(2)}, u32[]{:S(2)}) collective-permute-start(bf16[112,896]{1,0:T(8,128)(2,1)S(1)} %get-tuple-element.86.refs_4_), channel_id=1, source_target_pairs={{0,1},{1,0},{2,3},{3,2},{4,5},{5,4},{6,7},{7,6},{8,9},{9,8},{10,11... | collective-permute-start | bytes 602120 | tf_op jit(solution)/shard_map/ppermute | solution.py:368
  86.6 9.1 %collective-permute-start.21 = (bf16[144,896]{1,0:T(8,128)(2,1)S(1)}, bf16[144,896]{1,0:T(8,128)(2,1)S(1)}, u32[]{:S(2)}, u32[]{:S(2)}) collective-permute-start(bf16[144,896]{1,0:T(8,128)(2,1)S(1)} %get-tuple-element.72), channel_id=1, source_target_pairs={{0,4},{1,5},{4,8},{5,9},{8,12},{9,13},{12,14},{13,15},{14,10},{15,... | collective-permute-start | bytes 774152 | tf_op jit(solution)/shard_map/ppermute | solution.py:65
  87.4 10.7 %collective-permute-start.24 = (bf16[144,896]{1,0:T(8,128)(2,1)S(1)}, bf16[144,896]{1,0:T(8,128)(2,1)S(1)}, u32[]{:S(2)}, u32[]{:S(2)}) collective-permute-start(bf16[144,896]{1,0:T(8,128)(2,1)S(1)} %get-tuple-element.78), channel_id=1, source_target_pairs={{0,2},{1,3},{4,0},{5,1},{8,4},{9,5},{12,8},{13,9},{14,12},{15,13},... | collective-permute-start | bytes 774152 | tf_op jit(solution)/shard_map/ppermute | solution.py:65
  90.0 3.4 %collective-permute-start.29 = (bf16[112,896]{1,0:T(8,128)(2,1)S(1)}, bf16[112,896]{1,0:T(8,128)(2,1)S(1)}, u32[]{:S(2)}, u32[]{:S(2)}) collective-permute-start(bf16[112,896]{1,0:T(8,128)(2,1)S(1)} %get-tuple-element.84.refs_2_), channel_id=1, source_target_pairs={{0,1},{1,0},{2,3},{3,2},{4,5},{5,4},{6,7},{7,6},{8,9},{9,8},{10,11... | collective-permute-start | bytes 602120 | tf_op jit(solution)/shard_map/ppermute | solution.py:368
  90.1 10.4 %collective-permute-start.22 = (bf16[128,896]{1,0:T(8,128)(2,1)S(1)}, bf16[128,896]{1,0:T(8,128)(2,1)S(1)}, u32[]{:S(2)}, u32[]{:S(2)}) collective-permute-start(bf16[128,896]{1,0:T(8,128)(2,1)S(1)} %get-tuple-element.74), channel_id=1, source_target_pairs={{0,4},{1,5},{4,8},{5,9},{8,12},{9,13},{12,14},{13,15},{14,10},{15,... | collective-permute-start | bytes 688136 | tf_op jit(solution)/shard_map/ppermute | solution.py:65
  93.4 4.8 %collective-permute-start.32 = (bf16[112,896]{1,0:T(8,128)(2,1)S(1)}, bf16[112,896]{1,0:T(8,128)(2,1)S(1)}, u32[]{:S(2)}, u32[]{:S(2)}) collective-permute-start(bf16[112,896]{1,0:T(8,128)(2,1)S(1)} %get-tuple-element.87.refs_5_), channel_id=1, source_target_pairs={{0,1},{1,0},{2,3},{3,2},{4,5},{5,4},{6,7},{7,6},{8,9},{9,8},{10,11... | collective-permute-start | bytes 602120 | tf_op jit(solution)/shard_map/ppermute | solution.py:368
  93.5 9.3 %collective-permute-start.23 = (bf16[128,896]{1,0:T(8,128)(2,1)S(1)}, bf16[128,896]{1,0:T(8,128)(2,1)S(1)}, u32[]{:S(2)}, u32[]{:S(2)}) collective-permute-start(bf16[128,896]{1,0:T(8,128)(2,1)S(1)} %get-tuple-element.76), channel_id=1, source_target_pairs={{0,2},{1,3},{4,0},{5,1},{8,4},{9,5},{12,8},{13,9},{14,12},{15,13},... | collective-permute-start | bytes 688136 | tf_op jit(solution)/shard_map/ppermute | solution.py:65
  95.8 6.5 %collective-permute-start.34 = (bf16[112,896]{1,0:T(8,128)(2,1)S(1)}, bf16[112,896]{1,0:T(8,128)(2,1)S(1)}, u32[]{:S(2)}, u32[]{:S(2)}) collective-permute-start(bf16[112,896]{1,0:T(8,128)(2,1)S(1)} %get-tuple-element.89.refs_7_), channel_id=1, source_target_pairs={{0,1},{1,0},{2,3},{3,2},{4,5},{5,4},{6,7},{7,6},{8,9},{9,8},{10,11... | collective-permute-start | bytes 602120 | tf_op jit(solution)/shard_map/ppermute | solution.py:368
  98.1 4.2 %collective-permute-start.35 = (bf16[112,896]{1,0:T(8,128)(2,1)S(1)}, bf16[112,896]{1,0:T(8,128)(2,1)S(1)}, u32[]{:S(2)}, u32[]{:S(2)}) collective-permute-start(bf16[112,896]{1,0:T(8,128)(2,1)S(1)} %get-tuple-element.90.refs_8_), channel_id=1, source_target_pairs={{0,1},{1,0},{2,3},{3,2},{4,5},{5,4},{6,7},{7,6},{8,9},{9,8},{10,11... | collective-permute-start | bytes 602120 | tf_op jit(solution)/shard_map/ppermute | solution.py:368
  98.2 8.1 %collective-permute-start.25 = (bf16[128,896]{1,0:T(8,128)(2,1)S(1)}, bf16[128,896]{1,0:T(8,128)(2,1)S(1)}, u32[]{:S(2)}, u32[]{:S(2)}) collective-permute-start(bf16[128,896]{1,0:T(8,128)(2,1)S(1)} %get-tuple-element.80), channel_id=1, source_target_pairs={{0,4},{1,5},{4,8},{5,9},{8,12},{9,13},{12,14},{13,15},{14,10},{15,... | collective-permute-start | bytes 688136 | tf_op jit(solution)/shard_map/ppermute | solution.py:65
  100.5 7.4 %collective-permute-start.26 = (bf16[128,896]{1,0:T(8,128)(2,1)S(1)}, bf16[128,896]{1,0:T(8,128)(2,1)S(1)}, u32[]{:S(2)}, u32[]{:S(2)}) collective-permute-start(bf16[128,896]{1,0:T(8,128)(2,1)S(1)} %get-tuple-element.81), channel_id=1, source_target_pairs={{0,2},{1,3},{4,0},{5,1},{8,4},{9,5},{12,8},{13,9},{14,12},{15,13},... | collective-permute-start | bytes 688136 | tf_op jit(solution)/shard_map/ppermute | solution.py:65
  102.2 5.7 %collective-permute-start.33 = (bf16[112,896]{1,0:T(8,128)(2,1)S(1)}, bf16[112,896]{1,0:T(8,128)(2,1)S(1)}, u32[]{:S(2)}, u32[]{:S(2)}) collective-permute-start(bf16[112,896]{1,0:T(8,128)(2,1)S(1)} %get-tuple-element.88.refs_6_), channel_id=1, source_target_pairs={{0,1},{1,0},{2,3},{3,2},{4,5},{5,4},{6,7},{7,6},{8,9},{9,8},{10,11... | collective-permute-start | bytes 602120 | tf_op jit(solution)/shard_map/ppermute | solution.py:368
  102.3 6.2 %collective-permute-start.36 = (bf16[112,896]{1,0:T(8,128)(2,1)S(1)}, bf16[112,896]{1,0:T(8,128)(2,1)S(1)}, u32[]{:S(2)}, u32[]{:S(2)}) collective-permute-start(bf16[112,896]{1,0:T(8,128)(2,1)S(1)} %get-tuple-element.91.refs_9_), channel_id=1, source_target_pairs={{0,1},{1,0},{2,3},{3,2},{4,5},{5,4},{6,7},{7,6},{8,9},{9,8},{10,11... | collective-permute-start | bytes 602120 | tf_op jit(solution)/shard_map/ppermute | solution.py:368
  102.8 5.8 %collective-permute-start.38 = (bf16[112,896]{1,0:T(8,128)(2,1)S(1)}, bf16[112,896]{1,0:T(8,128)(2,1)S(1)}, u32[]{:S(2)}, u32[]{:S(2)}) collective-permute-start(bf16[112,896]{1,0:T(8,128)(2,1)S(1)} %get-tuple-element.93.refs_11_), channel_id=1, source_target_pairs={{0,1},{1,0},{2,3},{3,2},{4,5},{5,4},{6,7},{7,6},{8,9},{9,8},{10,11... | collective-permute-start | bytes 602120 | tf_op jit(solution)/shard_map/ppermute | solution.py:368
  106.3 4.0 %collective-permute-start.41 = (bf16[128,896]{1,0:T(8,128)(2,1)S(1)}, bf16[128,896]{1,0:T(8,128)(2,1)S(1)}, u32[]{:S(2)}, u32[]{:S(2)}) collective-permute-start(bf16[128,896]{1,0:T(8,128)(2,1)S(1)} %collective-permute-done.25.refs_12_.refs_14_), channel_id=1, source_target_pairs={{0,1},{1,0},{2,3},{3,2},{4,5},{5,4},{6,7},{7,6},{8,9},{9,8},{10,11... | collective-permute-start | bytes 688136 | tf_op jit(solution)/shard_map/ppermute | solution.py:368
  107.9 2.4 %collective-permute-start.42 = (bf16[128,896]{1,0:T(8,128)(2,1)S(1)}, bf16[128,896]{1,0:T(8,128)(2,1)S(1)}, u32[]{:S(2)}, u32[]{:S(2)}) collective-permute-start(bf16[128,896]{1,0:T(8,128)(2,1)S(1)} %collective-permute-done.26.refs_13_.refs_15_), channel_id=1, source_target_pairs={{0,1},{1,0},{2,3},{3,2},{4,5},{5,4},{6,7},{7,6},{8,9},{9,8},{10,11... | collective-permute-start | bytes 688136 | tf_op jit(solution)/shard_map/ppermute | solution.py:368
  107.9 2.3 %collective-permute-start.39 = (bf16[112,896]{1,0:T(8,128)(2,1)S(1)}, bf16[112,896]{1,0:T(8,128)(2,1)S(1)}, u32[]{:S(2)}, u32[]{:S(2)}) collective-permute-start(bf16[112,896]{1,0:T(8,128)(2,1)S(1)} %get-tuple-element.94.refs_12_), channel_id=1, source_target_pairs={{0,1},{1,0},{2,3},{3,2},{4,5},{5,4},{6,7},{7,6},{8,9},{9,8},{10,11... | collective-permute-start | bytes 602120 | tf_op jit(solution)/shard_map/ppermute | solution.py:368
  108.5 1.7 %collective-permute-start.37 = (bf16[112,896]{1,0:T(8,128)(2,1)S(1)}, bf16[112,896]{1,0:T(8,128)(2,1)S(1)}, u32[]{:S(2)}, u32[]{:S(2)}) collective-permute-start(bf16[112,896]{1,0:T(8,128)(2,1)S(1)} %get-tuple-element.92.refs_10_), channel_id=1, source_target_pairs={{0,1},{1,0},{2,3},{3,2},{4,5},{5,4},{6,7},{7,6},{8,9},{9,8},{10,11... | collective-permute-start | bytes 602120 | tf_op jit(solution)/shard_map/ppermute | solution.py:368
  108.6 1.6 %collective-permute-start.40 = (bf16[112,896]{1,0:T(8,128)(2,1)S(1)}, bf16[112,896]{1,0:T(8,128)(2,1)S(1)}, u32[]{:S(2)}, u32[]{:S(2)}) collective-permute-start(bf16[112,896]{1,0:T(8,128)(2,1)S(1)} %get-tuple-element.95.refs_13_), channel_id=1, source_target_pairs={{0,1},{1,0},{2,3},{3,2},{4,5},{5,4},{6,7},{7,6},{8,9},{9,8},{10,11... | collective-permute-start | bytes 602120 | tf_op jit(solution)/shard_map/ppermute | solution.py:368

commit v5 on v4

--- a/solution.py
+++ b/solution.py
@@ -203,17 +203,17 @@
 
 
 def early_kernel(count, members, *refs):
-    halves, parts = refs[:count], refs[count : count + members]
-    cons_ref, cov_ref, rows_ref = refs[count + members :]
-    cov_ref[...] = cov_sum(halves, [parts], cons_ref, rows_ref)
+    halves, near = refs[:count], refs[count : count + members]
+    middle = refs[count + members : count + 2 * members]
+    cons_ref, cov_ref, rows_ref = refs[count + 2 * members :]
+    cov_ref[...] = cov_sum(halves, [near, middle], cons_ref, rows_ref)
 
 
 def late_kernel(count, members, *refs):
     core = lax.axis_index("tok") % 2
-    halves, middle = refs[:count], refs[count : count + members]
-    far = refs[count + members : count + 2 * members]
-    early_ref, cons_ref, keep_ref, give_ref, rows_ref = refs[count + 2 * members :]
-    cov = early_ref[...] + cov_sum(halves, [middle, far], cons_ref, rows_ref)
+    halves, far = refs[:count], refs[count : count + members]
+    early_ref, cons_ref, keep_ref, give_ref, rows_ref = refs[count + members :]
+    cov = early_ref[...] + cov_sum(halves, [far], cons_ref, rows_ref)
     slab = cov.shape[0] // 2
     low, high = cov[:slab], cov[slab:]
     keep_ref[...] = jnp.where(core == 0, low, high)
@@ -317,23 +317,24 @@
     early_rows, early_parts = rotate(blocks[:-3])
     middle_rows, middle_parts = rotate(blocks[-3:-1])
     far_rows, far_parts = rotate(blocks[-1:])
-    near = (chips - 3) * count
+    near = (chips - 1) * count
+    early_rows = early_rows + middle_rows
     early_cons, early_cov = call(
         functools.partial(early_kernel, len(early_rows), members),
         (shape((near, cols), BF16), shape((cols, width), F32)),
         [],
-        early_rows + early_parts,
+        early_rows + early_parts + middle_parts,
         [shape((near, width), BF16)],
         flops=2 * near * cols * width,
     )
-    late_rows = middle_rows + far_rows
+    late_rows = far_rows
     late_cons, keep, give = call(
         functools.partial(late_kernel, len(late_rows), members),
-        (shape((3 * count, cols), BF16), shape((slab, width), F32), shape((slab, width), BF16)),
+        (shape((count, cols), BF16), shape((slab, width), F32), shape((slab, width), BF16)),
         [],
-        late_rows + middle_parts + far_parts + [early_cov],
-        [shape((3 * count, width), BF16)],
-        flops=2 * 3 * count * cols * width,
+        late_rows + far_parts + [early_cov],
+        [shape((count, width), BF16)],
+        flops=2 * count * cols * width,
     )
     come = lax.ppermute(give, "tok", siblings)
 

time: 120 us -> 120 us (level)
  no operation moved by 1% of the time
where the time goes in v5:
time: 120 us; the launch traced here: 119 us
  waiting for transfers between devices  53.5 us (45%)
  starting transfers between devices  46.2 us (38%)
  Pallas kernels  16 us (13%)
  local copies, waits for them, and re-layouts  2.67 us (2%)
    ppermute x22, waiting for transfers between devices, shift(): lax.ppermute(block, 'tok', [(2 * a + c, 2 * b + c) for a, b in pairs for...  42.1 us
    ppermute x22, starting transfers between devices, shift(): lax.ppermute(block, 'tok', [(2 * a + c, 2 * b + c) for a, b in pairs for...  33 us
    pallas_call x23, Pallas kernels, call(): pl.pallas_call(kernel, out_shape=outs, in_specs=[SMEM] * len(smem) + [VME...  16 us
    all_to_all x1, waiting for transfers between devices, shards(): lax.all_to_all(pieces, 'tok', split_axis=0, concat_axis=0, tiled=True, ax...  8 us
    all_to_all x1, starting transfers between devices, shards(): lax.all_to_all(pieces, 'tok', split_axis=0, concat_axis=0, tiled=True, ax...  6.22 us
    ppermute x3, starting transfers between devices, rotate(): return (halves, [rotated, lax.ppermute(rotated, 'ckpt', [(0, 1), (1, 0)])])  4.65 us
    unnamed x6, local copies, waits for them, and re-layouts  2.66 us
  transfers between devices with their start and end apart: 44, of which 19 were waited for; matrix products, arithmetic and copies ran while one was open for 0% of the time, Pallas kernels for 5%

profile of v5, /device:TPU:0, one launch (start us, length us, event | category | flops | bytes accessed | tf_op | source)
XLA Modules:
  0.0 119.3 jit_solution(15729369575535045170)
XLA Ops:
  0.6 1.0 copy-done
  1.7 0.7 copy-done.2
  2.6 3.0 %collective-permute-start.1 = (bf16[128,1792]{1,0:T(8,128)(2,1)S(1)}, bf16[128,1792]{1,0:T(8,128)(2,1)S(1)}, u32[]{:S(2)}, u32[]{:S(2)}) collective-permute-start(bf16[128,1792]{1,0:T(8,128)(2,1)S(1)} %shard_map.50.refs_0_), channel_id=1, source_target_pairs={{0,2},{1,3},{4,0},{5,1},{8,4},{9,5},{12,8},{13,9},{14,12},{15,13},... | collective-permute-start | bytes 1376264 | tf_op jit(solution)/shard_map/ppermute | solution.py:65
  5.8 1.0 copy-done.1
  6.8 1.0 shard_map.51
  7.8 6.2 %all-to-all-start = ((bf16[8,112,224]{2,1,0:T(8,128)(2,1)}), bf16[8,112,224]{2,1,0:T(8,128)(2,1)S(1)}, u32[]{:S(2)}, u32[]{:S(2)}) async-start(bf16[8,112,224]{2,1,0:T(8,128)(2,1)} %shard_map.51), calls=%async_computation | async-start | bytes 917504 | tf_op jit(solution)/shard_map/all_to_all | solution.py:291
  14.0 2.7 %collective-permute-done.1.refs_2_ = bf16[128,1792]{1,0:T(8,128)(2,1)S(1)} collective-permute-done((bf16[128,1792]{1,0:T(8,128)(2,1)S(1)}, bf16[128,1792]{1,0:T(8,128)(2,1)S(1)}, u32[]{:S(2)}, u32[]{:S(2)}) %collective-permute-start.1) | collective-permute-done | bytes 458784 | tf_op jit(solution)/shard_map/ppermute | solution.py:65
  16.7 2.5 %collective-permute-start.3 = (bf16[128,1792]{1,0:T(8,128)(2,1)S(1)}, bf16[128,1792]{1,0:T(8,128)(2,1)S(1)}, u32[]{:S(2)}, u32[]{:S(2)}) collective-permute-start(bf16[128,1792]{1,0:T(8,128)(2,1)S(1)} %collective-permute-done.1.refs_2_), channel_id=1, source_target_pairs={{0,2},{1,3},{4,0},{5,1},{8,4},{9,5},{12,8},{13,9},{14,12},{15,13},... | collective-permute-start | bytes 1376264 | tf_op jit(solution)/shard_map/ppermute | solution.py:65
  19.1 1.4 %collective-permute-start.2 = (bf16[128,1792]{1,0:T(8,128)(2,1)S(1)}, bf16[128,1792]{1,0:T(8,128)(2,1)S(1)}, u32[]{:S(2)}, u32[]{:S(2)}) collective-permute-start(bf16[128,1792]{1,0:T(8,128)(2,1)S(1)} %collective-permute-done.refs_1_), channel_id=1, source_target_pairs={{0,4},{1,5},{4,8},{5,9},{8,12},{9,13},{12,14},{13,15},{14,10},{15,... | collective-permute-start | bytes 1376264 | tf_op jit(solution)/shard_map/ppermute | solution.py:65
  20.5 8.0 %all-to-all-done = bf16[8,112,224]{2,1,0:T(8,128)(2,1)S(1)} async-done(((bf16[8,112,224]{2,1,0:T(8,128)(2,1)}), bf16[8,112,224]{2,1,0:T(8,128)(2,1)S(1)}, u32[]{:S(2)}, u32[]{:S(2)}) %all-to-all-start) | async-done | bytes 401440 | tf_op jit(solution)/shard_map/all_to_all | solution.py:291
  28.5 5.2 %collective-permute-done.3.refs_4_ = bf16[128,1792]{1,0:T(8,128)(2,1)S(1)} collective-permute-done((bf16[128,1792]{1,0:T(8,128)(2,1)S(1)}, bf16[128,1792]{1,0:T(8,128)(2,1)S(1)}, u32[]{:S(2)}, u32[]{:S(2)}) %collective-permute-start.3) | collective-permute-done | bytes 458784 | tf_op jit(solution)/shard_map/ppermute | solution.py:65
  33.7 0.5 collective-permute-start.5
  34.3 3.4 %collective-permute-start.4 = (bf16[128,1792]{1,0:T(8,128)(2,1)S(1)}, bf16[128,1792]{1,0:T(8,128)(2,1)S(1)}, u32[]{:S(2)}, u32[]{:S(2)}) collective-permute-start(bf16[128,1792]{1,0:T(8,128)(2,1)S(1)} %collective-permute-done.2.refs_3_), channel_id=1, source_target_pairs={{0,4},{1,5},{4,8},{5,9},{8,12},{9,13},{12,14},{13,15},{14,10},{15,... | collective-permute-start | bytes 1376264 | tf_op jit(solution)/shard_map/ppermute | solution.py:65
  37.6 0.9 shard_map.52.refs_7_
  38.5 1.6 %collective-permute-start.7 = (bf16[640,224]{1,0:T(8,128)(2,1)S(1)}, bf16[640,224]{1,0:T(8,128)(2,1)S(1)}, u32[]{:S(2)}, u32[]{:S(2)}) collective-permute-start(bf16[640,224]{1,0:T(8,128)(2,1)S(1)} %shard_map.52.refs_7_), channel_id=1, source_target_pairs={{0,16},{16,0},{1,17},{17,1},{2,18},{18,2},{3,19},{19,3},{4,20},{20... | collective-permute-start | bytes 860168 | tf_op jit(solution)/shard_map/ppermute | solution.py:313
  40.1 7.0 %collective-permute-done.5.refs_1_.refs_6_.behind_ref = bf16[128,1792]{1,0:T(8,128)(2,1)S(1)} collective-permute-done((bf16[128,1792]{1,0:T(8,128)(2,1)S(1)}, bf16[128,1792]{1,0:T(8,128)(2,1)S(1)}, u32[]{:S(2)}, u32[]{:S(2)}) %collective-permute-start.5) | collective-permute-done | bytes 458784 | tf_op jit(solution)/shard_map/ppermute | solution.py:65
  47.6 1.3 %collective-permute-start.9 = (bf16[64,1792]{1,0:T(8,128)(2,1)S(1)}, bf16[64,1792]{1,0:T(8,128)(2,1)S(1)}, u32[]{:S(2)}, u32[]{:S(2)}) collective-permute-start(bf16[64,1792]{1,0:T(8,128)(2,1)S(1)} %get-tuple-element.50), channel_id=1, source_target_pairs={{0,4},{1,5},{4,8},{5,9},{8,12},{9,13},{12,14},{13,15},{14,10},{15,... | collective-permute-start | bytes 688136 | tf_op jit(solution)/shard_map/ppermute | solution.py:65
  49.0 1.3 %collective-permute-start.10 = (bf16[64,1792]{1,0:T(8,128)(2,1)S(1)}, bf16[64,1792]{1,0:T(8,128)(2,1)S(1)}, u32[]{:S(2)}, u32[]{:S(2)}) collective-permute-start(bf16[64,1792]{1,0:T(8,128)(2,1)S(1)} %get-tuple-element.51), channel_id=1, source_target_pairs={{0,2},{1,3},{4,0},{5,1},{8,4},{9,5},{12,8},{13,9},{14,12},{15,13},... | collective-permute-start | bytes 688136 | tf_op jit(solution)/shard_map/ppermute | solution.py:65
  50.2 0.5 shard_map.53.refs_9_
  50.8 1.5 %collective-permute-start.8 = (bf16[256,224]{1,0:T(8,128)(2,1)S(1)}, bf16[256,224]{1,0:T(8,128)(2,1)S(1)}, u32[]{:S(2)}, u32[]{:S(2)}) collective-permute-start(bf16[256,224]{1,0:T(8,128)(2,1)S(1)} %shard_map.53.refs_9_), channel_id=1, source_target_pairs={{0,16},{16,0},{1,17},{17,1},{2,18},{18,2},{3,19},{19,3},{4,20},{20... | collective-permute-start | bytes 344072 | tf_op jit(solution)/shard_map/ppermute | solution.py:313
  52.3 1.8 %collective-permute-done.9.refs_0_ = bf16[64,1792]{1,0:T(8,128)(2,1)S(1)} collective-permute-done((bf16[64,1792]{1,0:T(8,128)(2,1)S(1)}, bf16[64,1792]{1,0:T(8,128)(2,1)S(1)}, u32[]{:S(2)}, u32[]{:S(2)}) %collective-permute-start.9) | collective-permute-done | bytes 229408 | tf_op jit(solution)/shard_map/ppermute | solution.py:65
  54.2 0.8 collective-permute-done.10.refs_1_
  55.5 1.6 %collective-permute-start.11 = (bf16[128,224]{1,0:T(8,128)(2,1)S(1)}, bf16[128,224]{1,0:T(8,128)(2,1)S(1)}, u32[]{:S(2)}, u32[]{:S(2)}) collective-permute-start(bf16[128,224]{1,0:T(8,128)(2,1)S(1)} %shard_map.56.refs_2_), channel_id=1, source_target_pairs={{0,16},{16,0},{1,17},{17,1},{2,18},{18,2},{3,19},{19,3},{4,20},{20... | collective-permute-start | bytes 172040 | tf_op jit(solution)/shard_map/ppermute | solution.py:313
  57.0 1.1 shard_map.54
  58.2 1.6 %collective-permute-done.11.refs_3_ = bf16[128,224]{1,0:T(8,128)(2,1)S(1)} collective-permute-done((bf16[128,224]{1,0:T(8,128)(2,1)S(1)}, bf16[128,224]{1,0:T(8,128)(2,1)S(1)}, u32[]{:S(2)}, u32[]{:S(2)}) %collective-permute-start.11) | collective-permute-done | bytes 57376 | tf_op jit(solution)/shard_map/ppermute | solution.py:313
  60.3 1.7 %collective-permute-done.12.come_ref = bf16[112,1792]{1,0:T(8,128)(2,1)S(1)} collective-permute-done((bf16[112,1792]{1,0:T(8,128)(2,1)S(1)}, bf16[112,1792]{1,0:T(8,128)(2,1)S(1)}, u32[]{:S(2)}, u32[]{:S(2)}) %collective-permute-start.12) | collective-permute-done | bytes 401440 | tf_op jit(solution)/shard_map/ppermute | solution.py:339
  62.4 1.8 %collective-permute-start.13 = (bf16[176,896]{1,0:T(8,128)(2,1)S(1)}, bf16[176,896]{1,0:T(8,128)(2,1)S(1)}, u32[]{:S(2)}, u32[]{:S(2)}) collective-permute-start(bf16[176,896]{1,0:T(8,128)(2,1)S(1)} %get-tuple-element.56), channel_id=1, source_target_pairs={{0,4},{1,5},{4,8},{5,9},{8,12},{9,13},{12,14},{13,15},{14,10},{15,... | collective-permute-start | bytes 946184 | tf_op jit(solution)/shard_map/ppermute | solution.py:65
  64.4 1.7 %collective-permute-start.14 = (bf16[160,896]{1,0:T(8,128)(2,1)S(1)}, bf16[160,896]{1,0:T(8,128)(2,1)S(1)}, u32[]{:S(2)}, u32[]{:S(2)}) collective-permute-start(bf16[160,896]{1,0:T(8,128)(2,1)S(1)} %get-tuple-element.58), channel_id=1, source_target_pairs={{0,4},{1,5},{4,8},{5,9},{8,12},{9,13},{12,14},{13,15},{14,10},{15,... | collective-permute-start | bytes 860168 | tf_op jit(solution)/shard_map/ppermute | solution.py:65
  66.5 6.2 %collective-permute-done.13.message_ref = bf16[176,896]{1,0:T(8,128)(2,1)S(1)} collective-permute-done((bf16[176,896]{1,0:T(8,128)(2,1)S(1)}, bf16[176,896]{1,0:T(8,128)(2,1)S(1)}, u32[]{:S(2)}, u32[]{:S(2)}) %collective-permute-start.13) | collective-permute-done | bytes 315424 | tf_op jit(solution)/shard_map/ppermute | solution.py:65
  72.8 1.8 %collective-permute-start.17 = (bf16[160,896]{1,0:T(8,128)(2,1)S(1)}, bf16[160,896]{1,0:T(8,128)(2,1)S(1)}, u32[]{:S(2)}, u32[]{:S(2)}) collective-permute-start(bf16[160,896]{1,0:T(8,128)(2,1)S(1)} %get-tuple-element.64), channel_id=1, source_target_pairs={{0,4},{1,5},{4,8},{5,9},{8,12},{9,13},{12,14},{13,15},{14,10},{15,... | collective-permute-start | bytes 860168 | tf_op jit(solution)/shard_map/ppermute | solution.py:65
  74.9 3.9 %collective-permute-done.14.message_ref = bf16[160,896]{1,0:T(8,128)(2,1)S(1)} collective-permute-done((bf16[160,896]{1,0:T(8,128)(2,1)S(1)}, bf16[160,896]{1,0:T(8,128)(2,1)S(1)}, u32[]{:S(2)}, u32[]{:S(2)}) %collective-permute-start.14) | collective-permute-done | bytes 286752 | tf_op jit(solution)/shard_map/ppermute | solution.py:65
  78.9 1.8 %collective-permute-start.18 = (bf16[144,896]{1,0:T(8,128)(2,1)S(1)}, bf16[144,896]{1,0:T(8,128)(2,1)S(1)}, u32[]{:S(2)}, u32[]{:S(2)}) collective-permute-start(bf16[144,896]{1,0:T(8,128)(2,1)S(1)} %get-tuple-element.66), channel_id=1, source_target_pairs={{0,4},{1,5},{4,8},{5,9},{8,12},{9,13},{12,14},{13,15},{14,10},{15,... | collective-permute-start | bytes 774152 | tf_op jit(solution)/shard_map/ppermute | solution.py:65
  81.2 3.8 %collective-permute-done.17.message_ref = bf16[160,896]{1,0:T(8,128)(2,1)S(1)} collective-permute-done((bf16[160,896]{1,0:T(8,128)(2,1)S(1)}, bf16[160,896]{1,0:T(8,128)(2,1)S(1)}, u32[]{:S(2)}, u32[]{:S(2)}) %collective-permute-start.17) | collective-permute-done | bytes 286752 | tf_op jit(solution)/shard_map/ppermute | solution.py:65
  85.0 1.3 %collective-permute-start.19 = (bf16[144,896]{1,0:T(8,128)(2,1)S(1)}, bf16[144,896]{1,0:T(8,128)(2,1)S(1)}, u32[]{:S(2)}, u32[]{:S(2)}) collective-permute-start(bf16[144,896]{1,0:T(8,128)(2,1)S(1)} %get-tuple-element.68), channel_id=1, source_target_pairs={{0,2},{1,3},{4,0},{5,1},{8,4},{9,5},{12,8},{13,9},{14,12},{15,13},... | collective-permute-start | bytes 774152 | tf_op jit(solution)/shard_map/ppermute | solution.py:65
  86.4 0.8 collective-permute-start.21
  87.2 1.3 %collective-permute-start.24 = (bf16[144,896]{1,0:T(8,128)(2,1)S(1)}, bf16[144,896]{1,0:T(8,128)(2,1)S(1)}, u32[]{:S(2)}, u32[]{:S(2)}) collective-permute-start(bf16[144,896]{1,0:T(8,128)(2,1)S(1)} %get-tuple-element.78), channel_id=1, source_target_pairs={{0,2},{1,3},{4,0},{5,1},{8,4},{9,5},{12,8},{13,9},{14,12},{15,13},... | collective-permute-start | bytes 774152 | tf_op jit(solution)/shard_map/ppermute | solution.py:65
  88.5 1.3 %collective-permute-done.18.message_ref = bf16[144,896]{1,0:T(8,128)(2,1)S(1)} collective-permute-done((bf16[144,896]{1,0:T(8,128)(2,1)S(1)}, bf16[144,896]{1,0:T(8,128)(2,1)S(1)}, u32[]{:S(2)}, u32[]{:S(2)}) %collective-permute-start.18) | collective-permute-done | bytes 258080 | tf_op jit(solution)/shard_map/ppermute | solution.py:65
  89.8 2.5 %collective-permute-start.22 = (bf16[128,896]{1,0:T(8,128)(2,1)S(1)}, bf16[128,896]{1,0:T(8,128)(2,1)S(1)}, u32[]{:S(2)}, u32[]{:S(2)}) collective-permute-start(bf16[128,896]{1,0:T(8,128)(2,1)S(1)} %get-tuple-element.74), channel_id=1, source_target_pairs={{0,4},{1,5},{4,8},{5,9},{8,12},{9,13},{12,14},{13,15},{14,10},{15,... | collective-permute-start | bytes 688136 | tf_op jit(solution)/shard_map/ppermute | solution.py:65
  92.4 0.8 collective-permute-done.19.message_ref
  93.2 2.0 %collective-permute-start.23 = (bf16[128,896]{1,0:T(8,128)(2,1)S(1)}, bf16[128,896]{1,0:T(8,128)(2,1)S(1)}, u32[]{:S(2)}, u32[]{:S(2)}) collective-permute-start(bf16[128,896]{1,0:T(8,128)(2,1)S(1)} %get-tuple-element.76), channel_id=1, source_target_pairs={{0,2},{1,3},{4,0},{5,1},{8,4},{9,5},{12,8},{13,9},{14,12},{15,13},... | collective-permute-start | bytes 688136 | tf_op jit(solution)/shard_map/ppermute | solution.py:65
  95.5 2.3 %collective-permute-done.24.message_ref = bf16[144,896]{1,0:T(8,128)(2,1)S(1)} collective-permute-done((bf16[144,896]{1,0:T(8,128)(2,1)S(1)}, bf16[144,896]{1,0:T(8,128)(2,1)S(1)}, u32[]{:S(2)}, u32[]{:S(2)}) %collective-permute-start.24) | collective-permute-done | bytes 258080 | tf_op jit(solution)/shard_map/ppermute | solution.py:65
  98.0 1.8 %collective-permute-start.25 = (bf16[128,896]{1,0:T(8,128)(2,1)S(1)}, bf16[128,896]{1,0:T(8,128)(2,1)S(1)}, u32[]{:S(2)}, u32[]{:S(2)}) collective-permute-start(bf16[128,896]{1,0:T(8,128)(2,1)S(1)} %get-tuple-element.80), channel_id=1, source_target_pairs={{0,4},{1,5},{4,8},{5,9},{8,12},{9,13},{12,14},{13,15},{14,10},{15,... | collective-permute-start | bytes 688136 | tf_op jit(solution)/shard_map/ppermute | solution.py:65
  100.2 1.7 %collective-permute-start.26 = (bf16[128,896]{1,0:T(8,128)(2,1)S(1)}, bf16[128,896]{1,0:T(8,128)(2,1)S(1)}, u32[]{:S(2)}, u32[]{:S(2)}) collective-permute-start(bf16[128,896]{1,0:T(8,128)(2,1)S(1)} %get-tuple-element.81), channel_id=1, source_target_pairs={{0,2},{1,3},{4,0},{5,1},{8,4},{9,5},{12,8},{13,9},{14,12},{15,13},... | collective-permute-start | bytes 688136 | tf_op jit(solution)/shard_map/ppermute | solution.py:65
  102.7 3.4 %collective-permute-done.25.refs_12_.refs_14_ = bf16[128,896]{1,0:T(8,128)(2,1)S(1)} collective-permute-done((bf16[128,896]{1,0:T(8,128)(2,1)S(1)}, bf16[128,896]{1,0:T(8,128)(2,1)S(1)}, u32[]{:S(2)}, u32[]{:S(2)}) %collective-permute-start.25) | collective-permute-done | bytes 229408 | tf_op jit(solution)/shard_map/ppermute | solution.py:65
  106.0 1.6 %collective-permute-done.26.refs_13_.refs_15_ = bf16[128,896]{1,0:T(8,128)(2,1)S(1)} collective-permute-done((bf16[128,896]{1,0:T(8,128)(2,1)S(1)}, bf16[128,896]{1,0:T(8,128)(2,1)S(1)}, u32[]{:S(2)}, u32[]{:S(2)}) %collective-permute-start.26) | collective-permute-done | bytes 229408 | tf_op jit(solution)/shard_map/ppermute | solution.py:65
  107.7 0.6 collective-permute-start.39
  108.8 1.2 shard_map.71
  110.0 9.3 %shard_map.72 = bf16[112,1792]{1,0:T(8,128)(2,1)} custom-call(bf16[112,896]{1,0:T(8,128)(2,1)S(1)} %get-tuple-element.82.refs_0_, bf16[112,896]{1,0:T(8,128)(2,1)S(1)} %get-tuple-element.83.refs_1_, bf16[112,896]{1,0:T(8,128)(2,1)S(1)} %get-tuple-element.84.refs_2_, bf16[112,896]{1,0:T(8,128)(2,1)S(1)} %get-tuple-element.85.refs_3_, ...), custom_call_target="tpu_custom_call" | custom-call | flops 6576668672 | bytes 20701184 | tf_op jit(solution)/shard_map/pallas_call | solution.py:34
  (70 shorter events, 6.1 us)
Async XLA Ops:
  0.6 1.0 copy-start
  1.6 0.7 copy-start.2
  2.6 14.0 %collective-permute-start.1 = (bf16[128,1792]{1,0:T(8,128)(2,1)S(1)}, bf16[128,1792]{1,0:T(8,128)(2,1)S(1)}, u32[]{:S(2)}, u32[]{:S(2)}) collective-permute-start(bf16[128,1792]{1,0:T(8,128)(2,1)S(1)} %shard_map.50.refs_0_), channel_id=1, source_target_pairs={{0,2},{1,3},{4,0},{5,1},{8,4},{9,5},{12,8},{13,9},{14,12},{15,13},... | collective-permute-start | bytes 1376264 | tf_op jit(solution)/shard_map/ppermute | solution.py:65
  5.7 13.5 %collective-permute-start = (bf16[128,1792]{1,0:T(8,128)(2,1)S(1)}, bf16[128,1792]{1,0:T(8,128)(2,1)S(1)}, u32[]{:S(2)}, u32[]{:S(2)}) collective-permute-start(bf16[128,1792]{1,0:T(8,128)(2,1)S(1)} %shard_map.50.refs_0_), channel_id=1, source_target_pairs={{0,4},{1,5},{4,8},{5,9},{8,12},{9,13},{12,14},{13,15},{14,10},{15,... | collective-permute-start | bytes 1376264 | tf_op jit(solution)/shard_map/ppermute | solution.py:65
  5.8 1.0 copy-start.1
  7.8 20.8 %all-to-all-start = ((bf16[8,112,224]{2,1,0:T(8,128)(2,1)}), bf16[8,112,224]{2,1,0:T(8,128)(2,1)S(1)}, u32[]{:S(2)}, u32[]{:S(2)}) async-start(bf16[8,112,224]{2,1,0:T(8,128)(2,1)} %shard_map.51), calls=%async_computation | async-start | bytes 917504 | tf_op jit(solution)/shard_map/all_to_all | solution.py:291
  16.7 17.1 %collective-permute-start.3 = (bf16[128,1792]{1,0:T(8,128)(2,1)S(1)}, bf16[128,1792]{1,0:T(8,128)(2,1)S(1)}, u32[]{:S(2)}, u32[]{:S(2)}) collective-permute-start(bf16[128,1792]{1,0:T(8,128)(2,1)S(1)} %collective-permute-done.1.refs_2_), channel_id=1, source_target_pairs={{0,2},{1,3},{4,0},{5,1},{8,4},{9,5},{12,8},{13,9},{14,12},{15,13},... | collective-permute-start | bytes 1376264 | tf_op jit(solution)/shard_map/ppermute | solution.py:65
  19.1 15.1 %collective-permute-start.2 = (bf16[128,1792]{1,0:T(8,128)(2,1)S(1)}, bf16[128,1792]{1,0:T(8,128)(2,1)S(1)}, u32[]{:S(2)}, u32[]{:S(2)}) collective-permute-start(bf16[128,1792]{1,0:T(8,128)(2,1)S(1)} %collective-permute-done.refs_1_), channel_id=1, source_target_pairs={{0,4},{1,5},{4,8},{5,9},{8,12},{9,13},{12,14},{13,15},{14,10},{15,... | collective-permute-start | bytes 1376264 | tf_op jit(solution)/shard_map/ppermute | solution.py:65
  28.5 9.1 %collective-permute-start.6 = (bf16[896,224]{1,0:T(8,128)(2,1)S(1)}, bf16[896,224]{1,0:T(8,128)(2,1)S(1)}, u32[]{:S(2)}, u32[]{:S(2)}) collective-permute-start(bf16[896,224]{1,0:T(8,128)(2,1)S(1)} %bitcast.5), channel_id=1, source_target_pairs={{0,1},{1,0},{2,3},{3,2},{4,5},{5,4},{6,7},{7,6},{8,9},{9,8},{10,11... | collective-permute-start | bytes 1204232 | tf_op jit(solution)/shard_map/ppermute | solution.py:296
  33.7 13.4 %collective-permute-start.5 = (bf16[128,1792]{1,0:T(8,128)(2,1)S(1)}, bf16[128,1792]{1,0:T(8,128)(2,1)S(1)}, u32[]{:S(2)}, u32[]{:S(2)}) collective-permute-start(bf16[128,1792]{1,0:T(8,128)(2,1)S(1)} %collective-permute-done.3.refs_4_), channel_id=1, source_target_pairs={{0,2},{1,3},{4,0},{5,1},{8,4},{9,5},{12,8},{13,9},{14,12},{15,13},... | collective-permute-start | bytes 1376264 | tf_op jit(solution)/shard_map/ppermute | solution.py:65
  34.3 13.4 %collective-permute-start.4 = (bf16[128,1792]{1,0:T(8,128)(2,1)S(1)}, bf16[128,1792]{1,0:T(8,128)(2,1)S(1)}, u32[]{:S(2)}, u32[]{:S(2)}) collective-permute-start(bf16[128,1792]{1,0:T(8,128)(2,1)S(1)} %collective-permute-done.2.refs_3_), channel_id=1, source_target_pairs={{0,4},{1,5},{4,8},{5,9},{8,12},{9,13},{12,14},{13,15},{14,10},{15,... | collective-permute-start | bytes 1376264 | tf_op jit(solution)/shard_map/ppermute | solution.py:65
  38.5 18.5 %collective-permute-start.7 = (bf16[640,224]{1,0:T(8,128)(2,1)S(1)}, bf16[640,224]{1,0:T(8,128)(2,1)S(1)}, u32[]{:S(2)}, u32[]{:S(2)}) collective-permute-start(bf16[640,224]{1,0:T(8,128)(2,1)S(1)} %shard_map.52.refs_7_), channel_id=1, source_target_pairs={{0,16},{16,0},{1,17},{17,1},{2,18},{18,2},{3,19},{19,3},{4,20},{20... | collective-permute-start | bytes 860168 | tf_op jit(solution)/shard_map/ppermute | solution.py:313
  47.6 6.5 %collective-permute-start.9 = (bf16[64,1792]{1,0:T(8,128)(2,1)S(1)}, bf16[64,1792]{1,0:T(8,128)(2,1)S(1)}, u32[]{:S(2)}, u32[]{:S(2)}) collective-permute-start(bf16[64,1792]{1,0:T(8,128)(2,1)S(1)} %get-tuple-element.50), channel_id=1, source_target_pairs={{0,4},{1,5},{4,8},{5,9},{8,12},{9,13},{12,14},{13,15},{14,10},{15,... | collective-permute-start | bytes 688136 | tf_op jit(solution)/shard_map/ppermute | solution.py:65
  49.0 6.0 %collective-permute-start.10 = (bf16[64,1792]{1,0:T(8,128)(2,1)S(1)}, bf16[64,1792]{1,0:T(8,128)(2,1)S(1)}, u32[]{:S(2)}, u32[]{:S(2)}) collective-permute-start(bf16[64,1792]{1,0:T(8,128)(2,1)S(1)} %get-tuple-element.51), channel_id=1, source_target_pairs={{0,2},{1,3},{4,0},{5,1},{8,4},{9,5},{12,8},{13,9},{14,12},{15,13},... | collective-permute-start | bytes 688136 | tf_op jit(solution)/shard_map/ppermute | solution.py:65
  50.8 6.2 %collective-permute-start.8 = (bf16[256,224]{1,0:T(8,128)(2,1)S(1)}, bf16[256,224]{1,0:T(8,128)(2,1)S(1)}, u32[]{:S(2)}, u32[]{:S(2)}) collective-permute-start(bf16[256,224]{1,0:T(8,128)(2,1)S(1)} %shard_map.53.refs_9_), channel_id=1, source_target_pairs={{0,16},{16,0},{1,17},{17,1},{2,18},{18,2},{3,19},{19,3},{4,20},{20... | collective-permute-start | bytes 344072 | tf_op jit(solution)/shard_map/ppermute | solution.py:313
  55.5 4.3 %collective-permute-start.11 = (bf16[128,224]{1,0:T(8,128)(2,1)S(1)}, bf16[128,224]{1,0:T(8,128)(2,1)S(1)}, u32[]{:S(2)}, u32[]{:S(2)}) collective-permute-start(bf16[128,224]{1,0:T(8,128)(2,1)S(1)} %shard_map.56.refs_2_), channel_id=1, source_target_pairs={{0,16},{16,0},{1,17},{17,1},{2,18},{18,2},{3,19},{19,3},{4,20},{20... | collective-permute-start | bytes 172040 | tf_op jit(solution)/shard_map/ppermute | solution.py:313
  60.2 1.8 %collective-permute-start.12 = (bf16[112,1792]{1,0:T(8,128)(2,1)S(1)}, bf16[112,1792]{1,0:T(8,128)(2,1)S(1)}, u32[]{:S(2)}, u32[]{:S(2)}) collective-permute-start(bf16[112,1792]{1,0:T(8,128)(2,1)S(1)} %get-tuple-element.54), channel_id=1, source_target_pairs={{0,1},{1,0},{2,3},{3,2},{4,5},{5,4},{6,7},{7,6},{8,9},{9,8},{10,11... | collective-permute-start | bytes 1204232 | tf_op jit(solution)/shard_map/ppermute | solution.py:339
  62.4 10.3 %collective-permute-start.13 = (bf16[176,896]{1,0:T(8,128)(2,1)S(1)}, bf16[176,896]{1,0:T(8,128)(2,1)S(1)}, u32[]{:S(2)}, u32[]{:S(2)}) collective-permute-start(bf16[176,896]{1,0:T(8,128)(2,1)S(1)} %get-tuple-element.56), channel_id=1, source_target_pairs={{0,4},{1,5},{4,8},{5,9},{8,12},{9,13},{12,14},{13,15},{14,10},{15,... | collective-permute-start | bytes 946184 | tf_op jit(solution)/shard_map/ppermute | solution.py:65
  64.2 10.4 %collective-permute-start.16 = (bf16[176,896]{1,0:T(8,128)(2,1)S(1)}, bf16[176,896]{1,0:T(8,128)(2,1)S(1)}, u32[]{:S(2)}, u32[]{:S(2)}) collective-permute-start(bf16[176,896]{1,0:T(8,128)(2,1)S(1)} %get-tuple-element.62), channel_id=1, source_target_pairs={{0,2},{1,3},{4,0},{5,1},{8,4},{9,5},{12,8},{13,9},{14,12},{15,13},... | collective-permute-start | bytes 946184 | tf_op jit(solution)/shard_map/ppermute | solution.py:65
  64.4 14.4 %collective-permute-start.14 = (bf16[160,896]{1,0:T(8,128)(2,1)S(1)}, bf16[160,896]{1,0:T(8,128)(2,1)S(1)}, u32[]{:S(2)}, u32[]{:S(2)}) collective-permute-start(bf16[160,896]{1,0:T(8,128)(2,1)S(1)} %get-tuple-element.58), channel_id=1, source_target_pairs={{0,4},{1,5},{4,8},{5,9},{8,12},{9,13},{12,14},{13,15},{14,10},{15,... | collective-permute-start | bytes 860168 | tf_op jit(solution)/shard_map/ppermute | solution.py:65
  66.2 14.5 %collective-permute-start.15 = (bf16[160,896]{1,0:T(8,128)(2,1)S(1)}, bf16[160,896]{1,0:T(8,128)(2,1)S(1)}, u32[]{:S(2)}, u32[]{:S(2)}) collective-permute-start(bf16[160,896]{1,0:T(8,128)(2,1)S(1)} %get-tuple-element.60), channel_id=1, source_target_pairs={{0,2},{1,3},{4,0},{5,1},{8,4},{9,5},{12,8},{13,9},{14,12},{15,13},... | collective-permute-start | bytes 860168 | tf_op jit(solution)/shard_map/ppermute | solution.py:65
  66.5 14.2 %collective-permute-start.27 = (bf16[112,896]{1,0:T(8,128)(2,1)S(1)}, bf16[112,896]{1,0:T(8,128)(2,1)S(1)}, u32[]{:S(2)}, u32[]{:S(2)}) collective-permute-start(bf16[112,896]{1,0:T(8,128)(2,1)S(1)} %get-tuple-element.82.refs_0_), channel_id=1, source_target_pairs={{0,1},{1,0},{2,3},{3,2},{4,5},{5,4},{6,7},{7,6},{8,9},{9,8},{10,11... | collective-permute-start | bytes 602120 | tf_op jit(solution)/shard_map/ppermute | solution.py:369
  72.8 12.2 %collective-permute-start.17 = (bf16[160,896]{1,0:T(8,128)(2,1)S(1)}, bf16[160,896]{1,0:T(8,128)(2,1)S(1)}, u32[]{:S(2)}, u32[]{:S(2)}) collective-permute-start(bf16[160,896]{1,0:T(8,128)(2,1)S(1)} %get-tuple-element.64), channel_id=1, source_target_pairs={{0,4},{1,5},{4,8},{5,9},{8,12},{9,13},{12,14},{13,15},{14,10},{15,... | collective-permute-start | bytes 860168 | tf_op jit(solution)/shard_map/ppermute | solution.py:65
  74.6 11.7 %collective-permute-start.20 = (bf16[160,896]{1,0:T(8,128)(2,1)S(1)}, bf16[160,896]{1,0:T(8,128)(2,1)S(1)}, u32[]{:S(2)}, u32[]{:S(2)}) collective-permute-start(bf16[160,896]{1,0:T(8,128)(2,1)S(1)} %get-tuple-element.70), channel_id=1, source_target_pairs={{0,2},{1,3},{4,0},{5,1},{8,4},{9,5},{12,8},{13,9},{14,12},{15,13},... | collective-permute-start | bytes 860168 | tf_op jit(solution)/shard_map/ppermute | solution.py:65
  78.9 10.9 %collective-permute-start.18 = (bf16[144,896]{1,0:T(8,128)(2,1)S(1)}, bf16[144,896]{1,0:T(8,128)(2,1)S(1)}, u32[]{:S(2)}, u32[]{:S(2)}) collective-permute-start(bf16[144,896]{1,0:T(8,128)(2,1)S(1)} %get-tuple-element.66), channel_id=1, source_target_pairs={{0,4},{1,5},{4,8},{5,9},{8,12},{9,13},{12,14},{13,15},{14,10},{15,... | collective-permute-start | bytes 774152 | tf_op jit(solution)/shard_map/ppermute | solution.py:65
  80.7 5.7 %collective-permute-start.28 = (bf16[112,896]{1,0:T(8,128)(2,1)S(1)}, bf16[112,896]{1,0:T(8,128)(2,1)S(1)}, u32[]{:S(2)}, u32[]{:S(2)}) collective-permute-start(bf16[112,896]{1,0:T(8,128)(2,1)S(1)} %get-tuple-element.83.refs_1_), channel_id=1, source_target_pairs={{0,1},{1,0},{2,3},{3,2},{4,5},{5,4},{6,7},{7,6},{8,9},{9,8},{10,11... | collective-permute-start | bytes 602120 | tf_op jit(solution)/shard_map/ppermute | solution.py:369
  80.7 6.5 %collective-permute-start.30 = (bf16[112,896]{1,0:T(8,128)(2,1)S(1)}, bf16[112,896]{1,0:T(8,128)(2,1)S(1)}, u32[]{:S(2)}, u32[]{:S(2)}) collective-permute-start(bf16[112,896]{1,0:T(8,128)(2,1)S(1)} %get-tuple-element.85.refs_3_), channel_id=1, source_target_pairs={{0,1},{1,0},{2,3},{3,2},{4,5},{5,4},{6,7},{7,6},{8,9},{9,8},{10,11... | collective-permute-start | bytes 602120 | tf_op jit(solution)/shard_map/ppermute | solution.py:369
  85.0 8.2 %collective-permute-start.19 = (bf16[144,896]{1,0:T(8,128)(2,1)S(1)}, bf16[144,896]{1,0:T(8,128)(2,1)S(1)}, u32[]{:S(2)}, u32[]{:S(2)}) collective-permute-start(bf16[144,896]{1,0:T(8,128)(2,1)S(1)} %get-tuple-element.68), channel_id=1, source_target_pairs={{0,2},{1,3},{4,0},{5,1},{8,4},{9,5},{12,8},{13,9},{14,12},{15,13},... | collective-permute-start | bytes 774152 | tf_op jit(solution)/shard_map/ppermute | solution.py:65
  86.3 3.6 %collective-permute-start.31 = (bf16[112,896]{1,0:T(8,128)(2,1)S(1)}, bf16[112,896]{1,0:T(8,128)(2,1)S(1)}, u32[]{:S(2)}, u32[]{:S(2)}) collective-permute-start(bf16[112,896]{1,0:T(8,128)(2,1)S(1)} %get-tuple-element.86.refs_4_), channel_id=1, source_target_pairs={{0,1},{1,0},{2,3},{3,2},{4,5},{5,4},{6,7},{7,6},{8,9},{9,8},{10,11... | collective-permute-start | bytes 602120 | tf_op jit(solution)/shard_map/ppermute | solution.py:369
  86.4 9.1 %collective-permute-start.21 = (bf16[144,896]{1,0:T(8,128)(2,1)S(1)}, bf16[144,896]{1,0:T(8,128)(2,1)S(1)}, u32[]{:S(2)}, u32[]{:S(2)}) collective-permute-start(bf16[144,896]{1,0:T(8,128)(2,1)S(1)} %get-tuple-element.72), channel_id=1, source_target_pairs={{0,4},{1,5},{4,8},{5,9},{8,12},{9,13},{12,14},{13,15},{14,10},{15,... | collective-permute-start | bytes 774152 | tf_op jit(solution)/shard_map/ppermute | solution.py:65
  87.2 10.7 %collective-permute-start.24 = (bf16[144,896]{1,0:T(8,128)(2,1)S(1)}, bf16[144,896]{1,0:T(8,128)(2,1)S(1)}, u32[]{:S(2)}, u32[]{:S(2)}) collective-permute-start(bf16[144,896]{1,0:T(8,128)(2,1)S(1)} %get-tuple-element.78), channel_id=1, source_target_pairs={{0,2},{1,3},{4,0},{5,1},{8,4},{9,5},{12,8},{13,9},{14,12},{15,13},... | collective-permute-start | bytes 774152 | tf_op jit(solution)/shard_map/ppermute | solution.py:65
  89.8 3.4 %collective-permute-start.29 = (bf16[112,896]{1,0:T(8,128)(2,1)S(1)}, bf16[112,896]{1,0:T(8,128)(2,1)S(1)}, u32[]{:S(2)}, u32[]{:S(2)}) collective-permute-start(bf16[112,896]{1,0:T(8,128)(2,1)S(1)} %get-tuple-element.84.refs_2_), channel_id=1, source_target_pairs={{0,1},{1,0},{2,3},{3,2},{4,5},{5,4},{6,7},{7,6},{8,9},{9,8},{10,11... | collective-permute-start | bytes 602120 | tf_op jit(solution)/shard_map/ppermute | solution.py:369
  89.8 10.4 %collective-permute-start.22 = (bf16[128,896]{1,0:T(8,128)(2,1)S(1)}, bf16[128,896]{1,0:T(8,128)(2,1)S(1)}, u32[]{:S(2)}, u32[]{:S(2)}) collective-permute-start(bf16[128,896]{1,0:T(8,128)(2,1)S(1)} %get-tuple-element.74), channel_id=1, source_target_pairs={{0,4},{1,5},{4,8},{5,9},{8,12},{9,13},{12,14},{13,15},{14,10},{15,... | collective-permute-start | bytes 688136 | tf_op jit(solution)/shard_map/ppermute | solution.py:65
  93.2 4.8 %collective-permute-start.32 = (bf16[112,896]{1,0:T(8,128)(2,1)S(1)}, bf16[112,896]{1,0:T(8,128)(2,1)S(1)}, u32[]{:S(2)}, u32[]{:S(2)}) collective-permute-start(bf16[112,896]{1,0:T(8,128)(2,1)S(1)} %get-tuple-element.87.refs_5_), channel_id=1, source_target_pairs={{0,1},{1,0},{2,3},{3,2},{4,5},{5,4},{6,7},{7,6},{8,9},{9,8},{10,11... | collective-permute-start | bytes 602120 | tf_op jit(solution)/shard_map/ppermute | solution.py:369
  93.2 9.3 %collective-permute-start.23 = (bf16[128,896]{1,0:T(8,128)(2,1)S(1)}, bf16[128,896]{1,0:T(8,128)(2,1)S(1)}, u32[]{:S(2)}, u32[]{:S(2)}) collective-permute-start(bf16[128,896]{1,0:T(8,128)(2,1)S(1)} %get-tuple-element.76), channel_id=1, source_target_pairs={{0,2},{1,3},{4,0},{5,1},{8,4},{9,5},{12,8},{13,9},{14,12},{15,13},... | collective-permute-start | bytes 688136 | tf_op jit(solution)/shard_map/ppermute | solution.py:65
  95.5 6.5 %collective-permute-start.34 = (bf16[112,896]{1,0:T(8,128)(2,1)S(1)}, bf16[112,896]{1,0:T(8,128)(2,1)S(1)}, u32[]{:S(2)}, u32[]{:S(2)}) collective-permute-start(bf16[112,896]{1,0:T(8,128)(2,1)S(1)} %get-tuple-element.89.refs_7_), channel_id=1, source_target_pairs={{0,1},{1,0},{2,3},{3,2},{4,5},{5,4},{6,7},{7,6},{8,9},{9,8},{10,11... | collective-permute-start | bytes 602120 | tf_op jit(solution)/shard_map/ppermute | solution.py:369
  97.9 4.2 %collective-permute-start.35 = (bf16[112,896]{1,0:T(8,128)(2,1)S(1)}, bf16[112,896]{1,0:T(8,128)(2,1)S(1)}, u32[]{:S(2)}, u32[]{:S(2)}) collective-permute-start(bf16[112,896]{1,0:T(8,128)(2,1)S(1)} %get-tuple-element.90.refs_8_), channel_id=1, source_target_pairs={{0,1},{1,0},{2,3},{3,2},{4,5},{5,4},{6,7},{7,6},{8,9},{9,8},{10,11... | collective-permute-start | bytes 602120 | tf_op jit(solution)/shard_map/ppermute | solution.py:369
  98.0 8.1 %collective-permute-start.25 = (bf16[128,896]{1,0:T(8,128)(2,1)S(1)}, bf16[128,896]{1,0:T(8,128)(2,1)S(1)}, u32[]{:S(2)}, u32[]{:S(2)}) collective-permute-start(bf16[128,896]{1,0:T(8,128)(2,1)S(1)} %get-tuple-element.80), channel_id=1, source_target_pairs={{0,4},{1,5},{4,8},{5,9},{8,12},{9,13},{12,14},{13,15},{14,10},{15,... | collective-permute-start | bytes 688136 | tf_op jit(solution)/shard_map/ppermute | solution.py:65
  100.2 7.4 %collective-permute-start.26 = (bf16[128,896]{1,0:T(8,128)(2,1)S(1)}, bf16[128,896]{1,0:T(8,128)(2,1)S(1)}, u32[]{:S(2)}, u32[]{:S(2)}) collective-permute-start(bf16[128,896]{1,0:T(8,128)(2,1)S(1)} %get-tuple-element.81), channel_id=1, source_target_pairs={{0,2},{1,3},{4,0},{5,1},{8,4},{9,5},{12,8},{13,9},{14,12},{15,13},... | collective-permute-start | bytes 688136 | tf_op jit(solution)/shard_map/ppermute | solution.py:65
  102.0 5.7 %collective-permute-start.33 = (bf16[112,896]{1,0:T(8,128)(2,1)S(1)}, bf16[112,896]{1,0:T(8,128)(2,1)S(1)}, u32[]{:S(2)}, u32[]{:S(2)}) collective-permute-start(bf16[112,896]{1,0:T(8,128)(2,1)S(1)} %get-tuple-element.88.refs_6_), channel_id=1, source_target_pairs={{0,1},{1,0},{2,3},{3,2},{4,5},{5,4},{6,7},{7,6},{8,9},{9,8},{10,11... | collective-permute-start | bytes 602120 | tf_op jit(solution)/shard_map/ppermute | solution.py:369
  102.1 6.2 %collective-permute-start.36 = (bf16[112,896]{1,0:T(8,128)(2,1)S(1)}, bf16[112,896]{1,0:T(8,128)(2,1)S(1)}, u32[]{:S(2)}, u32[]{:S(2)}) collective-permute-start(bf16[112,896]{1,0:T(8,128)(2,1)S(1)} %get-tuple-element.91.refs_9_), channel_id=1, source_target_pairs={{0,1},{1,0},{2,3},{3,2},{4,5},{5,4},{6,7},{7,6},{8,9},{9,8},{10,11... | collective-permute-start | bytes 602120 | tf_op jit(solution)/shard_map/ppermute | solution.py:369
  102.6 5.8 %collective-permute-start.38 = (bf16[112,896]{1,0:T(8,128)(2,1)S(1)}, bf16[112,896]{1,0:T(8,128)(2,1)S(1)}, u32[]{:S(2)}, u32[]{:S(2)}) collective-permute-start(bf16[112,896]{1,0:T(8,128)(2,1)S(1)} %get-tuple-element.93.refs_11_), channel_id=1, source_target_pairs={{0,1},{1,0},{2,3},{3,2},{4,5},{5,4},{6,7},{7,6},{8,9},{9,8},{10,11... | collective-permute-start | bytes 602120 | tf_op jit(solution)/shard_map/ppermute | solution.py:369
  106.0 4.0 %collective-permute-start.41 = (bf16[128,896]{1,0:T(8,128)(2,1)S(1)}, bf16[128,896]{1,0:T(8,128)(2,1)S(1)}, u32[]{:S(2)}, u32[]{:S(2)}) collective-permute-start(bf16[128,896]{1,0:T(8,128)(2,1)S(1)} %collective-permute-done.25.refs_12_.refs_14_), channel_id=1, source_target_pairs={{0,1},{1,0},{2,3},{3,2},{4,5},{5,4},{6,7},{7,6},{8,9},{9,8},{10,11... | collective-permute-start | bytes 688136 | tf_op jit(solution)/shard_map/ppermute | solution.py:369
  107.6 2.4 %collective-permute-start.42 = (bf16[128,896]{1,0:T(8,128)(2,1)S(1)}, bf16[128,896]{1,0:T(8,128)(2,1)S(1)}, u32[]{:S(2)}, u32[]{:S(2)}) collective-permute-start(bf16[128,896]{1,0:T(8,128)(2,1)S(1)} %collective-permute-done.26.refs_13_.refs_15_), channel_id=1, source_target_pairs={{0,1},{1,0},{2,3},{3,2},{4,5},{5,4},{6,7},{7,6},{8,9},{9,8},{10,11... | collective-permute-start | bytes 688136 | tf_op jit(solution)/shard_map/ppermute | solution.py:369
  107.7 2.3 %collective-permute-start.39 = (bf16[112,896]{1,0:T(8,128)(2,1)S(1)}, bf16[112,896]{1,0:T(8,128)(2,1)S(1)}, u32[]{:S(2)}, u32[]{:S(2)}) collective-permute-start(bf16[112,896]{1,0:T(8,128)(2,1)S(1)} %get-tuple-element.94.refs_12_), channel_id=1, source_target_pairs={{0,1},{1,0},{2,3},{3,2},{4,5},{5,4},{6,7},{7,6},{8,9},{9,8},{10,11... | collective-permute-start | bytes 602120 | tf_op jit(solution)/shard_map/ppermute | solution.py:369
  108.2 1.7 %collective-permute-start.37 = (bf16[112,896]{1,0:T(8,128)(2,1)S(1)}, bf16[112,896]{1,0:T(8,128)(2,1)S(1)}, u32[]{:S(2)}, u32[]{:S(2)}) collective-permute-start(bf16[112,896]{1,0:T(8,128)(2,1)S(1)} %get-tuple-element.92.refs_10_), channel_id=1, source_target_pairs={{0,1},{1,0},{2,3},{3,2},{4,5},{5,4},{6,7},{7,6},{8,9},{9,8},{10,11... | collective-permute-start | bytes 602120 | tf_op jit(solution)/shard_map/ppermute | solution.py:369
  108.3 1.6 %collective-permute-start.40 = (bf16[112,896]{1,0:T(8,128)(2,1)S(1)}, bf16[112,896]{1,0:T(8,128)(2,1)S(1)}, u32[]{:S(2)}, u32[]{:S(2)}) collective-permute-start(bf16[112,896]{1,0:T(8,128)(2,1)S(1)} %get-tuple-element.95.refs_13_), channel_id=1, source_target_pairs={{0,1},{1,0},{2,3},{3,2},{4,5},{5,4},{6,7},{7,6},{8,9},{9,8},{10,11... | collective-permute-start | bytes 602120 | tf_op jit(solution)/shard_map/ppermute | solution.py:369

commit v6 on v5

--- a/solution.py
+++ b/solution.py
@@ -247,13 +247,14 @@
     own = contract(picks.astype(BF16), columns, 1, 1)
     start = (own * inverse).astype(BF16)
 
-    flipped[...] = whole[...].T
-
     def apply_once(vector):
         inner = jnp.dot(vector.astype(BF16), whole[...], preferred_element_type=F32) * inverse
         return jnp.dot(inner.astype(BF16), flipped[...], preferred_element_type=F32) * inverse
 
-    first = 1.5 * start.astype(F32) - 0.5 * apply_once(start)
+    inner = jnp.dot(start, whole[...], preferred_element_type=F32) * inverse
+    flipped[...] = whole[...].T
+    applied = jnp.dot(inner.astype(BF16), flipped[...], preferred_element_type=F32) * inverse
+    first = 1.5 * start.astype(F32) - 0.5 * applied
     upper = 1.5 * first - 0.5 * apply_once(first)
     middle = apply_once(upper)
     cubic = 1.5 * middle - 0.5 * apply_once(middle)

time: 120 us -> 120 us (level)
  no operation moved by 1% of the time
where the time goes in v6:
time: 120 us; the launch traced here: 119 us
  waiting for transfers between devices  53.5 us (45%)
  starting transfers between devices  46.2 us (38%)
  Pallas kernels  16 us (13%)
  local copies, waits for them, and re-layouts  2.67 us (2%)
    ppermute x22, waiting for transfers between devices, shift(): lax.ppermute(block, 'tok', [(2 * a + c, 2 * b + c) for a, b in pairs for...  42.1 us
    ppermute x22, starting transfers between devices, shift(): lax.ppermute(block, 'tok', [(2 * a + c, 2 * b + c) for a, b in pairs for...  33 us
    pallas_call x23, Pallas kernels, call(): pl.pallas_call(kernel, out_shape=outs, in_specs=[SMEM] * len(smem) + [VME...  16 us
    all_to_all x1, waiting for transfers between devices, shards(): lax.all_to_all(pieces, 'tok', split_axis=0, concat_axis=0, tiled=True, ax...  8 us
    all_to_all x1, starting transfers between devices, shards(): lax.all_to_all(pieces, 'tok', split_axis=0, concat_axis=0, tiled=True, ax...  6.22 us
    ppermute x3, starting transfers between devices, rotate(): return (halves, [rotated, lax.ppermute(rotated, 'ckpt', [(0, 1), (1, 0)])])  4.65 us
    unnamed x6, local copies, waits for them, and re-layouts  2.66 us
  transfers between devices with their start and end apart: 44, of which 19 were waited for; matrix products, arithmetic and copies ran while one was open for 0% of the time, Pallas kernels for 5%

profile of v6, /device:TPU:0, one launch (start us, length us, event | category | flops | bytes accessed | tf_op | source)
XLA Modules:
  0.0 119.3 jit_solution(2671363777149487187)
XLA Ops:
  0.6 1.0 copy-done
  1.7 0.7 copy-done.2
  2.6 3.0 %collective-permute-start.1 = (bf16[128,1792]{1,0:T(8,128)(2,1)S(1)}, bf16[128,1792]{1,0:T(8,128)(2,1)S(1)}, u32[]{:S(2)}, u32[]{:S(2)}) collective-permute-start(bf16[128,1792]{1,0:T(8,128)(2,1)S(1)} %shard_map.50.refs_0_), channel_id=1, source_target_pairs={{0,2},{1,3},{4,0},{5,1},{8,4},{9,5},{12,8},{13,9},{14,12},{15,13},... | collective-permute-start | bytes 1376264 | tf_op jit(solution)/shard_map/ppermute | solution.py:65
  5.8 1.0 copy-done.1
  6.8 1.0 shard_map.51
  7.8 6.2 %all-to-all-start = ((bf16[8,112,224]{2,1,0:T(8,128)(2,1)}), bf16[8,112,224]{2,1,0:T(8,128)(2,1)S(1)}, u32[]{:S(2)}, u32[]{:S(2)}) async-start(bf16[8,112,224]{2,1,0:T(8,128)(2,1)} %shard_map.51), calls=%async_computation | async-start | bytes 917504 | tf_op jit(solution)/shard_map/all_to_all | solution.py:292
  14.0 2.7 %collective-permute-done.1.refs_2_ = bf16[128,1792]{1,0:T(8,128)(2,1)S(1)} collective-permute-done((bf16[128,1792]{1,0:T(8,128)(2,1)S(1)}, bf16[128,1792]{1,0:T(8,128)(2,1)S(1)}, u32[]{:S(2)}, u32[]{:S(2)}) %collective-permute-start.1) | collective-permute-done | bytes 458784 | tf_op jit(solution)/shard_map/ppermute | solution.py:65
  16.7 2.5 %collective-permute-start.3 = (bf16[128,1792]{1,0:T(8,128)(2,1)S(1)}, bf16[128,1792]{1,0:T(8,128)(2,1)S(1)}, u32[]{:S(2)}, u32[]{:S(2)}) collective-permute-start(bf16[128,1792]{1,0:T(8,128)(2,1)S(1)} %collective-permute-done.1.refs_2_), channel_id=1, source_target_pairs={{0,2},{1,3},{4,0},{5,1},{8,4},{9,5},{12,8},{13,9},{14,12},{15,13},... | collective-permute-start | bytes 1376264 | tf_op jit(solution)/shard_map/ppermute | solution.py:65
  19.1 1.4 %collective-permute-start.2 = (bf16[128,1792]{1,0:T(8,128)(2,1)S(1)}, bf16[128,1792]{1,0:T(8,128)(2,1)S(1)}, u32[]{:S(2)}, u32[]{:S(2)}) collective-permute-start(bf16[128,1792]{1,0:T(8,128)(2,1)S(1)} %collective-permute-done.refs_1_), channel_id=1, source_target_pairs={{0,4},{1,5},{4,8},{5,9},{8,12},{9,13},{12,14},{13,15},{14,10},{15,... | collective-permute-start | bytes 1376264 | tf_op jit(solution)/shard_map/ppermute | solution.py:65
  20.5 8.0 %all-to-all-done = bf16[8,112,224]{2,1,0:T(8,128)(2,1)S(1)} async-done(((bf16[8,112,224]{2,1,0:T(8,128)(2,1)}), bf16[8,112,224]{2,1,0:T(8,128)(2,1)S(1)}, u32[]{:S(2)}, u32[]{:S(2)}) %all-to-all-start) | async-done | bytes 401440 | tf_op jit(solution)/shard_map/all_to_all | solution.py:292
  28.5 5.2 %collective-permute-done.3.refs_4_ = bf16[128,1792]{1,0:T(8,128)(2,1)S(1)} collective-permute-done((bf16[128,1792]{1,0:T(8,128)(2,1)S(1)}, bf16[128,1792]{1,0:T(8,128)(2,1)S(1)}, u32[]{:S(2)}, u32[]{:S(2)}) %collective-permute-start.3) | collective-permute-done | bytes 458784 | tf_op jit(solution)/shard_map/ppermute | solution.py:65
  33.7 0.5 collective-permute-start.5
  34.3 3.4 %collective-permute-start.4 = (bf16[128,1792]{1,0:T(8,128)(2,1)S(1)}, bf16[128,1792]{1,0:T(8,128)(2,1)S(1)}, u32[]{:S(2)}, u32[]{:S(2)}) collective-permute-start(bf16[128,1792]{1,0:T(8,128)(2,1)S(1)} %collective-permute-done.2.refs_3_), channel_id=1, source_target_pairs={{0,4},{1,5},{4,8},{5,9},{8,12},{9,13},{12,14},{13,15},{14,10},{15,... | collective-permute-start | bytes 1376264 | tf_op jit(solution)/shard_map/ppermute | solution.py:65
  37.6 0.9 shard_map.52.refs_7_
  38.5 1.6 %collective-permute-start.7 = (bf16[640,224]{1,0:T(8,128)(2,1)S(1)}, bf16[640,224]{1,0:T(8,128)(2,1)S(1)}, u32[]{:S(2)}, u32[]{:S(2)}) collective-permute-start(bf16[640,224]{1,0:T(8,128)(2,1)S(1)} %shard_map.52.refs_7_), channel_id=1, source_target_pairs={{0,16},{16,0},{1,17},{17,1},{2,18},{18,2},{3,19},{19,3},{4,20},{20... | collective-permute-start | bytes 860168 | tf_op jit(solution)/shard_map/ppermute | solution.py:314
  40.1 7.0 %collective-permute-done.5.refs_1_.refs_6_.behind_ref = bf16[128,1792]{1,0:T(8,128)(2,1)S(1)} collective-permute-done((bf16[128,1792]{1,0:T(8,128)(2,1)S(1)}, bf16[128,1792]{1,0:T(8,128)(2,1)S(1)}, u32[]{:S(2)}, u32[]{:S(2)}) %collective-permute-start.5) | collective-permute-done | bytes 458784 | tf_op jit(solution)/shard_map/ppermute | solution.py:65
  47.6 1.3 %collective-permute-start.9 = (bf16[64,1792]{1,0:T(8,128)(2,1)S(1)}, bf16[64,1792]{1,0:T(8,128)(2,1)S(1)}, u32[]{:S(2)}, u32[]{:S(2)}) collective-permute-start(bf16[64,1792]{1,0:T(8,128)(2,1)S(1)} %get-tuple-element.50), channel_id=1, source_target_pairs={{0,4},{1,5},{4,8},{5,9},{8,12},{9,13},{12,14},{13,15},{14,10},{15,... | collective-permute-start | bytes 688136 | tf_op jit(solution)/shard_map/ppermute | solution.py:65
  49.0 1.3 %collective-permute-start.10 = (bf16[64,1792]{1,0:T(8,128)(2,1)S(1)}, bf16[64,1792]{1,0:T(8,128)(2,1)S(1)}, u32[]{:S(2)}, u32[]{:S(2)}) collective-permute-start(bf16[64,1792]{1,0:T(8,128)(2,1)S(1)} %get-tuple-element.51), channel_id=1, source_target_pairs={{0,2},{1,3},{4,0},{5,1},{8,4},{9,5},{12,8},{13,9},{14,12},{15,13},... | collective-permute-start | bytes 688136 | tf_op jit(solution)/shard_map/ppermute | solution.py:65
  50.2 0.5 shard_map.53.refs_9_
  50.8 1.5 %collective-permute-start.8 = (bf16[256,224]{1,0:T(8,128)(2,1)S(1)}, bf16[256,224]{1,0:T(8,128)(2,1)S(1)}, u32[]{:S(2)}, u32[]{:S(2)}) collective-permute-start(bf16[256,224]{1,0:T(8,128)(2,1)S(1)} %shard_map.53.refs_9_), channel_id=1, source_target_pairs={{0,16},{16,0},{1,17},{17,1},{2,18},{18,2},{3,19},{19,3},{4,20},{20... | collective-permute-start | bytes 344072 | tf_op jit(solution)/shard_map/ppermute | solution.py:314
  52.3 1.8 %collective-permute-done.9.refs_0_ = bf16[64,1792]{1,0:T(8,128)(2,1)S(1)} collective-permute-done((bf16[64,1792]{1,0:T(8,128)(2,1)S(1)}, bf16[64,1792]{1,0:T(8,128)(2,1)S(1)}, u32[]{:S(2)}, u32[]{:S(2)}) %collective-permute-start.9) | collective-permute-done | bytes 229408 | tf_op jit(solution)/shard_map/ppermute | solution.py:65
  54.2 0.8 collective-permute-done.10.refs_1_
  55.5 1.6 %collective-permute-start.11 = (bf16[128,224]{1,0:T(8,128)(2,1)S(1)}, bf16[128,224]{1,0:T(8,128)(2,1)S(1)}, u32[]{:S(2)}, u32[]{:S(2)}) collective-permute-start(bf16[128,224]{1,0:T(8,128)(2,1)S(1)} %shard_map.56.refs_2_), channel_id=1, source_target_pairs={{0,16},{16,0},{1,17},{17,1},{2,18},{18,2},{3,19},{19,3},{4,20},{20... | collective-permute-start | bytes 172040 | tf_op jit(solution)/shard_map/ppermute | solution.py:314
  57.0 1.1 shard_map.54
  58.2 1.6 %collective-permute-done.11.refs_3_ = bf16[128,224]{1,0:T(8,128)(2,1)S(1)} collective-permute-done((bf16[128,224]{1,0:T(8,128)(2,1)S(1)}, bf16[128,224]{1,0:T(8,128)(2,1)S(1)}, u32[]{:S(2)}, u32[]{:S(2)}) %collective-permute-start.11) | collective-permute-done | bytes 57376 | tf_op jit(solution)/shard_map/ppermute | solution.py:314
  60.3 1.7 %collective-permute-done.12.come_ref = bf16[112,1792]{1,0:T(8,128)(2,1)S(1)} collective-permute-done((bf16[112,1792]{1,0:T(8,128)(2,1)S(1)}, bf16[112,1792]{1,0:T(8,128)(2,1)S(1)}, u32[]{:S(2)}, u32[]{:S(2)}) %collective-permute-start.12) | collective-permute-done | bytes 401440 | tf_op jit(solution)/shard_map/ppermute | solution.py:340
  62.4 1.8 %collective-permute-start.13 = (bf16[176,896]{1,0:T(8,128)(2,1)S(1)}, bf16[176,896]{1,0:T(8,128)(2,1)S(1)}, u32[]{:S(2)}, u32[]{:S(2)}) collective-permute-start(bf16[176,896]{1,0:T(8,128)(2,1)S(1)} %get-tuple-element.56), channel_id=1, source_target_pairs={{0,4},{1,5},{4,8},{5,9},{8,12},{9,13},{12,14},{13,15},{14,10},{15,... | collective-permute-start | bytes 946184 | tf_op jit(solution)/shard_map/ppermute | solution.py:65
  64.4 1.7 %collective-permute-start.14 = (bf16[160,896]{1,0:T(8,128)(2,1)S(1)}, bf16[160,896]{1,0:T(8,128)(2,1)S(1)}, u32[]{:S(2)}, u32[]{:S(2)}) collective-permute-start(bf16[160,896]{1,0:T(8,128)(2,1)S(1)} %get-tuple-element.58), channel_id=1, source_target_pairs={{0,4},{1,5},{4,8},{5,9},{8,12},{9,13},{12,14},{13,15},{14,10},{15,... | collective-permute-start | bytes 860168 | tf_op jit(solution)/shard_map/ppermute | solution.py:65
  66.5 6.2 %collective-permute-done.13.message_ref = bf16[176,896]{1,0:T(8,128)(2,1)S(1)} collective-permute-done((bf16[176,896]{1,0:T(8,128)(2,1)S(1)}, bf16[176,896]{1,0:T(8,128)(2,1)S(1)}, u32[]{:S(2)}, u32[]{:S(2)}) %collective-permute-start.13) | collective-permute-done | bytes 315424 | tf_op jit(solution)/shard_map/ppermute | solution.py:65
  72.8 1.8 %collective-permute-start.17 = (bf16[160,896]{1,0:T(8,128)(2,1)S(1)}, bf16[160,896]{1,0:T(8,128)(2,1)S(1)}, u32[]{:S(2)}, u32[]{:S(2)}) collective-permute-start(bf16[160,896]{1,0:T(8,128)(2,1)S(1)} %get-tuple-element.64), channel_id=1, source_target_pairs={{0,4},{1,5},{4,8},{5,9},{8,12},{9,13},{12,14},{13,15},{14,10},{15,... | collective-permute-start | bytes 860168 | tf_op jit(solution)/shard_map/ppermute | solution.py:65
  74.9 3.9 %collective-permute-done.14.message_ref = bf16[160,896]{1,0:T(8,128)(2,1)S(1)} collective-permute-done((bf16[160,896]{1,0:T(8,128)(2,1)S(1)}, bf16[160,896]{1,0:T(8,128)(2,1)S(1)}, u32[]{:S(2)}, u32[]{:S(2)}) %collective-permute-start.14) | collective-permute-done | bytes 286752 | tf_op jit(solution)/shard_map/ppermute | solution.py:65
  78.9 1.8 %collective-permute-start.18 = (bf16[144,896]{1,0:T(8,128)(2,1)S(1)}, bf16[144,896]{1,0:T(8,128)(2,1)S(1)}, u32[]{:S(2)}, u32[]{:S(2)}) collective-permute-start(bf16[144,896]{1,0:T(8,128)(2,1)S(1)} %get-tuple-element.66), channel_id=1, source_target_pairs={{0,4},{1,5},{4,8},{5,9},{8,12},{9,13},{12,14},{13,15},{14,10},{15,... | collective-permute-start | bytes 774152 | tf_op jit(solution)/shard_map/ppermute | solution.py:65
  81.2 3.8 %collective-permute-done.17.message_ref = bf16[160,896]{1,0:T(8,128)(2,1)S(1)} collective-permute-done((bf16[160,896]{1,0:T(8,128)(2,1)S(1)}, bf16[160,896]{1,0:T(8,128)(2,1)S(1)}, u32[]{:S(2)}, u32[]{:S(2)}) %collective-permute-start.17) | collective-permute-done | bytes 286752 | tf_op jit(solution)/shard_map/ppermute | solution.py:65
  85.0 1.3 %collective-permute-start.19 = (bf16[144,896]{1,0:T(8,128)(2,1)S(1)}, bf16[144,896]{1,0:T(8,128)(2,1)S(1)}, u32[]{:S(2)}, u32[]{:S(2)}) collective-permute-start(bf16[144,896]{1,0:T(8,128)(2,1)S(1)} %get-tuple-element.68), channel_id=1, source_target_pairs={{0,2},{1,3},{4,0},{5,1},{8,4},{9,5},{12,8},{13,9},{14,12},{15,13},... | collective-permute-start | bytes 774152 | tf_op jit(solution)/shard_map/ppermute | solution.py:65
  86.4 0.8 collective-permute-start.21
  87.2 1.3 %collective-permute-start.24 = (bf16[144,896]{1,0:T(8,128)(2,1)S(1)}, bf16[144,896]{1,0:T(8,128)(2,1)S(1)}, u32[]{:S(2)}, u32[]{:S(2)}) collective-permute-start(bf16[144,896]{1,0:T(8,128)(2,1)S(1)} %get-tuple-element.78), channel_id=1, source_target_pairs={{0,2},{1,3},{4,0},{5,1},{8,4},{9,5},{12,8},{13,9},{14,12},{15,13},... | collective-permute-start | bytes 774152 | tf_op jit(solution)/shard_map/ppermute | solution.py:65
  88.5 1.3 %collective-permute-done.18.message_ref = bf16[144,896]{1,0:T(8,128)(2,1)S(1)} collective-permute-done((bf16[144,896]{1,0:T(8,128)(2,1)S(1)}, bf16[144,896]{1,0:T(8,128)(2,1)S(1)}, u32[]{:S(2)}, u32[]{:S(2)}) %collective-permute-start.18) | collective-permute-done | bytes 258080 | tf_op jit(solution)/shard_map/ppermute | solution.py:65
  89.8 2.5 %collective-permute-start.22 = (bf16[128,896]{1,0:T(8,128)(2,1)S(1)}, bf16[128,896]{1,0:T(8,128)(2,1)S(1)}, u32[]{:S(2)}, u32[]{:S(2)}) collective-permute-start(bf16[128,896]{1,0:T(8,128)(2,1)S(1)} %get-tuple-element.74), channel_id=1, source_target_pairs={{0,4},{1,5},{4,8},{5,9},{8,12},{9,13},{12,14},{13,15},{14,10},{15,... | collective-permute-start | bytes 688136 | tf_op jit(solution)/shard_map/ppermute | solution.py:65
  92.4 0.8 collective-permute-done.19.message_ref
  93.2 2.0 %collective-permute-start.23 = (bf16[128,896]{1,0:T(8,128)(2,1)S(1)}, bf16[128,896]{1,0:T(8,128)(2,1)S(1)}, u32[]{:S(2)}, u32[]{:S(2)}) collective-permute-start(bf16[128,896]{1,0:T(8,128)(2,1)S(1)} %get-tuple-element.76), channel_id=1, source_target_pairs={{0,2},{1,3},{4,0},{5,1},{8,4},{9,5},{12,8},{13,9},{14,12},{15,13},... | collective-permute-start | bytes 688136 | tf_op jit(solution)/shard_map/ppermute | solution.py:65
  95.5 2.3 %collective-permute-done.24.message_ref = bf16[144,896]{1,0:T(8,128)(2,1)S(1)} collective-permute-done((bf16[144,896]{1,0:T(8,128)(2,1)S(1)}, bf16[144,896]{1,0:T(8,128)(2,1)S(1)}, u32[]{:S(2)}, u32[]{:S(2)}) %collective-permute-start.24) | collective-permute-done | bytes 258080 | tf_op jit(solution)/shard_map/ppermute | solution.py:65
  98.0 1.8 %collective-permute-start.25 = (bf16[128,896]{1,0:T(8,128)(2,1)S(1)}, bf16[128,896]{1,0:T(8,128)(2,1)S(1)}, u32[]{:S(2)}, u32[]{:S(2)}) collective-permute-start(bf16[128,896]{1,0:T(8,128)(2,1)S(1)} %get-tuple-element.80), channel_id=1, source_target_pairs={{0,4},{1,5},{4,8},{5,9},{8,12},{9,13},{12,14},{13,15},{14,10},{15,... | collective-permute-start | bytes 688136 | tf_op jit(solution)/shard_map/ppermute | solution.py:65
  100.2 1.7 %collective-permute-start.26 = (bf16[128,896]{1,0:T(8,128)(2,1)S(1)}, bf16[128,896]{1,0:T(8,128)(2,1)S(1)}, u32[]{:S(2)}, u32[]{:S(2)}) collective-permute-start(bf16[128,896]{1,0:T(8,128)(2,1)S(1)} %get-tuple-element.81), channel_id=1, source_target_pairs={{0,2},{1,3},{4,0},{5,1},{8,4},{9,5},{12,8},{13,9},{14,12},{15,13},... | collective-permute-start | bytes 688136 | tf_op jit(solution)/shard_map/ppermute | solution.py:65
  102.7 3.4 %collective-permute-done.25.refs_12_.refs_14_ = bf16[128,896]{1,0:T(8,128)(2,1)S(1)} collective-permute-done((bf16[128,896]{1,0:T(8,128)(2,1)S(1)}, bf16[128,896]{1,0:T(8,128)(2,1)S(1)}, u32[]{:S(2)}, u32[]{:S(2)}) %collective-permute-start.25) | collective-permute-done | bytes 229408 | tf_op jit(solution)/shard_map/ppermute | solution.py:65
  106.0 1.6 %collective-permute-done.26.refs_13_.refs_15_ = bf16[128,896]{1,0:T(8,128)(2,1)S(1)} collective-permute-done((bf16[128,896]{1,0:T(8,128)(2,1)S(1)}, bf16[128,896]{1,0:T(8,128)(2,1)S(1)}, u32[]{:S(2)}, u32[]{:S(2)}) %collective-permute-start.26) | collective-permute-done | bytes 229408 | tf_op jit(solution)/shard_map/ppermute | solution.py:65
  107.7 0.6 collective-permute-start.39
  108.8 1.2 shard_map.71
  110.0 9.3 %shard_map.72 = bf16[112,1792]{1,0:T(8,128)(2,1)} custom-call(bf16[112,896]{1,0:T(8,128)(2,1)S(1)} %get-tuple-element.82.refs_0_, bf16[112,896]{1,0:T(8,128)(2,1)S(1)} %get-tuple-element.83.refs_1_, bf16[112,896]{1,0:T(8,128)(2,1)S(1)} %get-tuple-element.84.refs_2_, bf16[112,896]{1,0:T(8,128)(2,1)S(1)} %get-tuple-element.85.refs_3_, ...), custom_call_target="tpu_custom_call" | custom-call | flops 6576668672 | bytes 20701184 | tf_op jit(solution)/shard_map/pallas_call | solution.py:34
  (70 shorter events, 6.1 us)
Async XLA Ops:
  0.6 1.0 copy-start
  1.6 0.7 copy-start.2
  2.6 14.0 %collective-permute-start.1 = (bf16[128,1792]{1,0:T(8,128)(2,1)S(1)}, bf16[128,1792]{1,0:T(8,128)(2,1)S(1)}, u32[]{:S(2)}, u32[]{:S(2)}) collective-permute-start(bf16[128,1792]{1,0:T(8,128)(2,1)S(1)} %shard_map.50.refs_0_), channel_id=1, source_target_pairs={{0,2},{1,3},{4,0},{5,1},{8,4},{9,5},{12,8},{13,9},{14,12},{15,13},... | collective-permute-start | bytes 1376264 | tf_op jit(solution)/shard_map/ppermute | solution.py:65
  5.7 13.5 %collective-permute-start = (bf16[128,1792]{1,0:T(8,128)(2,1)S(1)}, bf16[128,1792]{1,0:T(8,128)(2,1)S(1)}, u32[]{:S(2)}, u32[]{:S(2)}) collective-permute-start(bf16[128,1792]{1,0:T(8,128)(2,1)S(1)} %shard_map.50.refs_0_), channel_id=1, source_target_pairs={{0,4},{1,5},{4,8},{5,9},{8,12},{9,13},{12,14},{13,15},{14,10},{15,... | collective-permute-start | bytes 1376264 | tf_op jit(solution)/shard_map/ppermute | solution.py:65
  5.8 1.0 copy-start.1
  7.8 20.8 %all-to-all-start = ((bf16[8,112,224]{2,1,0:T(8,128)(2,1)}), bf16[8,112,224]{2,1,0:T(8,128)(2,1)S(1)}, u32[]{:S(2)}, u32[]{:S(2)}) async-start(bf16[8,112,224]{2,1,0:T(8,128)(2,1)} %shard_map.51), calls=%async_computation | async-start | bytes 917504 | tf_op jit(solution)/shard_map/all_to_all | solution.py:292
  16.7 17.1 %collective-permute-start.3 = (bf16[128,1792]{1,0:T(8,128)(2,1)S(1)}, bf16[128,1792]{1,0:T(8,128)(2,1)S(1)}, u32[]{:S(2)}, u32[]{:S(2)}) collective-permute-start(bf16[128,1792]{1,0:T(8,128)(2,1)S(1)} %collective-permute-done.1.refs_2_), channel_id=1, source_target_pairs={{0,2},{1,3},{4,0},{5,1},{8,4},{9,5},{12,8},{13,9},{14,12},{15,13},... | collective-permute-start | bytes 1376264 | tf_op jit(solution)/shard_map/ppermute | solution.py:65
  19.1 15.1 %collective-permute-start.2 = (bf16[128,1792]{1,0:T(8,128)(2,1)S(1)}, bf16[128,1792]{1,0:T(8,128)(2,1)S(1)}, u32[]{:S(2)}, u32[]{:S(2)}) collective-permute-start(bf16[128,1792]{1,0:T(8,128)(2,1)S(1)} %collective-permute-done.refs_1_), channel_id=1, source_target_pairs={{0,4},{1,5},{4,8},{5,9},{8,12},{9,13},{12,14},{13,15},{14,10},{15,... | collective-permute-start | bytes 1376264 | tf_op jit(solution)/shard_map/ppermute | solution.py:65
  28.5 9.1 %collective-permute-start.6 = (bf16[896,224]{1,0:T(8,128)(2,1)S(1)}, bf16[896,224]{1,0:T(8,128)(2,1)S(1)}, u32[]{:S(2)}, u32[]{:S(2)}) collective-permute-start(bf16[896,224]{1,0:T(8,128)(2,1)S(1)} %bitcast.5), channel_id=1, source_target_pairs={{0,1},{1,0},{2,3},{3,2},{4,5},{5,4},{6,7},{7,6},{8,9},{9,8},{10,11... | collective-permute-start | bytes 1204232 | tf_op jit(solution)/shard_map/ppermute | solution.py:297
  33.7 13.4 %collective-permute-start.5 = (bf16[128,1792]{1,0:T(8,128)(2,1)S(1)}, bf16[128,1792]{1,0:T(8,128)(2,1)S(1)}, u32[]{:S(2)}, u32[]{:S(2)}) collective-permute-start(bf16[128,1792]{1,0:T(8,128)(2,1)S(1)} %collective-permute-done.3.refs_4_), channel_id=1, source_target_pairs={{0,2},{1,3},{4,0},{5,1},{8,4},{9,5},{12,8},{13,9},{14,12},{15,13},... | collective-permute-start | bytes 1376264 | tf_op jit(solution)/shard_map/ppermute | solution.py:65
  34.3 13.4 %collective-permute-start.4 = (bf16[128,1792]{1,0:T(8,128)(2,1)S(1)}, bf16[128,1792]{1,0:T(8,128)(2,1)S(1)}, u32[]{:S(2)}, u32[]{:S(2)}) collective-permute-start(bf16[128,1792]{1,0:T(8,128)(2,1)S(1)} %collective-permute-done.2.refs_3_), channel_id=1, source_target_pairs={{0,4},{1,5},{4,8},{5,9},{8,12},{9,13},{12,14},{13,15},{14,10},{15,... | collective-permute-start | bytes 1376264 | tf_op jit(solution)/shard_map/ppermute | solution.py:65
  38.5 18.5 %collective-permute-start.7 = (bf16[640,224]{1,0:T(8,128)(2,1)S(1)}, bf16[640,224]{1,0:T(8,128)(2,1)S(1)}, u32[]{:S(2)}, u32[]{:S(2)}) collective-permute-start(bf16[640,224]{1,0:T(8,128)(2,1)S(1)} %shard_map.52.refs_7_), channel_id=1, source_target_pairs={{0,16},{16,0},{1,17},{17,1},{2,18},{18,2},{3,19},{19,3},{4,20},{20... | collective-permute-start | bytes 860168 | tf_op jit(solution)/shard_map/ppermute | solution.py:314
  47.6 6.5 %collective-permute-start.9 = (bf16[64,1792]{1,0:T(8,128)(2,1)S(1)}, bf16[64,1792]{1,0:T(8,128)(2,1)S(1)}, u32[]{:S(2)}, u32[]{:S(2)}) collective-permute-start(bf16[64,1792]{1,0:T(8,128)(2,1)S(1)} %get-tuple-element.50), channel_id=1, source_target_pairs={{0,4},{1,5},{4,8},{5,9},{8,12},{9,13},{12,14},{13,15},{14,10},{15,... | collective-permute-start | bytes 688136 | tf_op jit(solution)/shard_map/ppermute | solution.py:65
  49.0 6.0 %collective-permute-start.10 = (bf16[64,1792]{1,0:T(8,128)(2,1)S(1)}, bf16[64,1792]{1,0:T(8,128)(2,1)S(1)}, u32[]{:S(2)}, u32[]{:S(2)}) collective-permute-start(bf16[64,1792]{1,0:T(8,128)(2,1)S(1)} %get-tuple-element.51), channel_id=1, source_target_pairs={{0,2},{1,3},{4,0},{5,1},{8,4},{9,5},{12,8},{13,9},{14,12},{15,13},... | collective-permute-start | bytes 688136 | tf_op jit(solution)/shard_map/ppermute | solution.py:65
  50.8 6.2 %collective-permute-start.8 = (bf16[256,224]{1,0:T(8,128)(2,1)S(1)}, bf16[256,224]{1,0:T(8,128)(2,1)S(1)}, u32[]{:S(2)}, u32[]{:S(2)}) collective-permute-start(bf16[256,224]{1,0:T(8,128)(2,1)S(1)} %shard_map.53.refs_9_), channel_id=1, source_target_pairs={{0,16},{16,0},{1,17},{17,1},{2,18},{18,2},{3,19},{19,3},{4,20},{20... | collective-permute-start | bytes 344072 | tf_op jit(solution)/shard_map/ppermute | solution.py:314
  55.5 4.3 %collective-permute-start.11 = (bf16[128,224]{1,0:T(8,128)(2,1)S(1)}, bf16[128,224]{1,0:T(8,128)(2,1)S(1)}, u32[]{:S(2)}, u32[]{:S(2)}) collective-permute-start(bf16[128,224]{1,0:T(8,128)(2,1)S(1)} %shard_map.56.refs_2_), channel_id=1, source_target_pairs={{0,16},{16,0},{1,17},{17,1},{2,18},{18,2},{3,19},{19,3},{4,20},{20... | collective-permute-start | bytes 172040 | tf_op jit(solution)/shard_map/ppermute | solution.py:314
  60.2 1.8 %collective-permute-start.12 = (bf16[112,1792]{1,0:T(8,128)(2,1)S(1)}, bf16[112,1792]{1,0:T(8,128)(2,1)S(1)}, u32[]{:S(2)}, u32[]{:S(2)}) collective-permute-start(bf16[112,1792]{1,0:T(8,128)(2,1)S(1)} %get-tuple-element.54), channel_id=1, source_target_pairs={{0,1},{1,0},{2,3},{3,2},{4,5},{5,4},{6,7},{7,6},{8,9},{9,8},{10,11... | collective-permute-start | bytes 1204232 | tf_op jit(solution)/shard_map/ppermute | solution.py:340
  62.4 10.3 %collective-permute-start.13 = (bf16[176,896]{1,0:T(8,128)(2,1)S(1)}, bf16[176,896]{1,0:T(8,128)(2,1)S(1)}, u32[]{:S(2)}, u32[]{:S(2)}) collective-permute-start(bf16[176,896]{1,0:T(8,128)(2,1)S(1)} %get-tuple-element.56), channel_id=1, source_target_pairs={{0,4},{1,5},{4,8},{5,9},{8,12},{9,13},{12,14},{13,15},{14,10},{15,... | collective-permute-start | bytes 946184 | tf_op jit(solution)/shard_map/ppermute | solution.py:65
  64.2 10.4 %collective-permute-start.16 = (bf16[176,896]{1,0:T(8,128)(2,1)S(1)}, bf16[176,896]{1,0:T(8,128)(2,1)S(1)}, u32[]{:S(2)}, u32[]{:S(2)}) collective-permute-start(bf16[176,896]{1,0:T(8,128)(2,1)S(1)} %get-tuple-element.62), channel_id=1, source_target_pairs={{0,2},{1,3},{4,0},{5,1},{8,4},{9,5},{12,8},{13,9},{14,12},{15,13},... | collective-permute-start | bytes 946184 | tf_op jit(solution)/shard_map/ppermute | solution.py:65
  64.4 14.4 %collective-permute-start.14 = (bf16[160,896]{1,0:T(8,128)(2,1)S(1)}, bf16[160,896]{1,0:T(8,128)(2,1)S(1)}, u32[]{:S(2)}, u32[]{:S(2)}) collective-permute-start(bf16[160,896]{1,0:T(8,128)(2,1)S(1)} %get-tuple-element.58), channel_id=1, source_target_pairs={{0,4},{1,5},{4,8},{5,9},{8,12},{9,13},{12,14},{13,15},{14,10},{15,... | collective-permute-start | bytes 860168 | tf_op jit(solution)/shard_map/ppermute | solution.py:65
  66.2 14.5 %collective-permute-start.15 = (bf16[160,896]{1,0:T(8,128)(2,1)S(1)}, bf16[160,896]{1,0:T(8,128)(2,1)S(1)}, u32[]{:S(2)}, u32[]{:S(2)}) collective-permute-start(bf16[160,896]{1,0:T(8,128)(2,1)S(1)} %get-tuple-element.60), channel_id=1, source_target_pairs={{0,2},{1,3},{4,0},{5,1},{8,4},{9,5},{12,8},{13,9},{14,12},{15,13},... | collective-permute-start | bytes 860168 | tf_op jit(solution)/shard_map/ppermute | solution.py:65
  66.5 14.2 %collective-permute-start.27 = (bf16[112,896]{1,0:T(8,128)(2,1)S(1)}, bf16[112,896]{1,0:T(8,128)(2,1)S(1)}, u32[]{:S(2)}, u32[]{:S(2)}) collective-permute-start(bf16[112,896]{1,0:T(8,128)(2,1)S(1)} %get-tuple-element.82.refs_0_), channel_id=1, source_target_pairs={{0,1},{1,0},{2,3},{3,2},{4,5},{5,4},{6,7},{7,6},{8,9},{9,8},{10,11... | collective-permute-start | bytes 602120 | tf_op jit(solution)/shard_map/ppermute | solution.py:370
  72.8 12.2 %collective-permute-start.17 = (bf16[160,896]{1,0:T(8,128)(2,1)S(1)}, bf16[160,896]{1,0:T(8,128)(2,1)S(1)}, u32[]{:S(2)}, u32[]{:S(2)}) collective-permute-start(bf16[160,896]{1,0:T(8,128)(2,1)S(1)} %get-tuple-element.64), channel_id=1, source_target_pairs={{0,4},{1,5},{4,8},{5,9},{8,12},{9,13},{12,14},{13,15},{14,10},{15,... | collective-permute-start | bytes 860168 | tf_op jit(solution)/shard_map/ppermute | solution.py:65
  74.6 11.7 %collective-permute-start.20 = (bf16[160,896]{1,0:T(8,128)(2,1)S(1)}, bf16[160,896]{1,0:T(8,128)(2,1)S(1)}, u32[]{:S(2)}, u32[]{:S(2)}) collective-permute-start(bf16[160,896]{1,0:T(8,128)(2,1)S(1)} %get-tuple-element.70), channel_id=1, source_target_pairs={{0,2},{1,3},{4,0},{5,1},{8,4},{9,5},{12,8},{13,9},{14,12},{15,13},... | collective-permute-start | bytes 860168 | tf_op jit(solution)/shard_map/ppermute | solution.py:65
  78.9 10.9 %collective-permute-start.18 = (bf16[144,896]{1,0:T(8,128)(2,1)S(1)}, bf16[144,896]{1,0:T(8,128)(2,1)S(1)}, u32[]{:S(2)}, u32[]{:S(2)}) collective-permute-start(bf16[144,896]{1,0:T(8,128)(2,1)S(1)} %get-tuple-element.66), channel_id=1, source_target_pairs={{0,4},{1,5},{4,8},{5,9},{8,12},{9,13},{12,14},{13,15},{14,10},{15,... | collective-permute-start | bytes 774152 | tf_op jit(solution)/shard_map/ppermute | solution.py:65
  80.7 5.7 %collective-permute-start.28 = (bf16[112,896]{1,0:T(8,128)(2,1)S(1)}, bf16[112,896]{1,0:T(8,128)(2,1)S(1)}, u32[]{:S(2)}, u32[]{:S(2)}) collective-permute-start(bf16[112,896]{1,0:T(8,128)(2,1)S(1)} %get-tuple-element.83.refs_1_), channel_id=1, source_target_pairs={{0,1},{1,0},{2,3},{3,2},{4,5},{5,4},{6,7},{7,6},{8,9},{9,8},{10,11... | collective-permute-start | bytes 602120 | tf_op jit(solution)/shard_map/ppermute | solution.py:370
  80.7 6.5 %collective-permute-start.30 = (bf16[112,896]{1,0:T(8,128)(2,1)S(1)}, bf16[112,896]{1,0:T(8,128)(2,1)S(1)}, u32[]{:S(2)}, u32[]{:S(2)}) collective-permute-start(bf16[112,896]{1,0:T(8,128)(2,1)S(1)} %get-tuple-element.85.refs_3_), channel_id=1, source_target_pairs={{0,1},{1,0},{2,3},{3,2},{4,5},{5,4},{6,7},{7,6},{8,9},{9,8},{10,11... | collective-permute-start | bytes 602120 | tf_op jit(solution)/shard_map/ppermute | solution.py:370
  85.0 8.2 %collective-permute-start.19 = (bf16[144,896]{1,0:T(8,128)(2,1)S(1)}, bf16[144,896]{1,0:T(8,128)(2,1)S(1)}, u32[]{:S(2)}, u32[]{:S(2)}) collective-permute-start(bf16[144,896]{1,0:T(8,128)(2,1)S(1)} %get-tuple-element.68), channel_id=1, source_target_pairs={{0,2},{1,3},{4,0},{5,1},{8,4},{9,5},{12,8},{13,9},{14,12},{15,13},... | collective-permute-start | bytes 774152 | tf_op jit(solution)/shard_map/ppermute | solution.py:65
  86.3 3.6 %collective-permute-start.31 = (bf16[112,896]{1,0:T(8,128)(2,1)S(1)}, bf16[112,896]{1,0:T(8,128)(2,1)S(1)}, u32[]{:S(2)}, u32[]{:S(2)}) collective-permute-start(bf16[112,896]{1,0:T(8,128)(2,1)S(1)} %get-tuple-element.86.refs_4_), channel_id=1, source_target_pairs={{0,1},{1,0},{2,3},{3,2},{4,5},{5,4},{6,7},{7,6},{8,9},{9,8},{10,11... | collective-permute-start | bytes 602120 | tf_op jit(solution)/shard_map/ppermute | solution.py:370
  86.4 9.1 %collective-permute-start.21 = (bf16[144,896]{1,0:T(8,128)(2,1)S(1)}, bf16[144,896]{1,0:T(8,128)(2,1)S(1)}, u32[]{:S(2)}, u32[]{:S(2)}) collective-permute-start(bf16[144,896]{1,0:T(8,128)(2,1)S(1)} %get-tuple-element.72), channel_id=1, source_target_pairs={{0,4},{1,5},{4,8},{5,9},{8,12},{9,13},{12,14},{13,15},{14,10},{15,... | collective-permute-start | bytes 774152 | tf_op jit(solution)/shard_map/ppermute | solution.py:65
  87.2 10.7 %collective-permute-start.24 = (bf16[144,896]{1,0:T(8,128)(2,1)S(1)}, bf16[144,896]{1,0:T(8,128)(2,1)S(1)}, u32[]{:S(2)}, u32[]{:S(2)}) collective-permute-start(bf16[144,896]{1,0:T(8,128)(2,1)S(1)} %get-tuple-element.78), channel_id=1, source_target_pairs={{0,2},{1,3},{4,0},{5,1},{8,4},{9,5},{12,8},{13,9},{14,12},{15,13},... | collective-permute-start | bytes 774152 | tf_op jit(solution)/shard_map/ppermute | solution.py:65
  89.8 3.4 %collective-permute-start.29 = (bf16[112,896]{1,0:T(8,128)(2,1)S(1)}, bf16[112,896]{1,0:T(8,128)(2,1)S(1)}, u32[]{:S(2)}, u32[]{:S(2)}) collective-permute-start(bf16[112,896]{1,0:T(8,128)(2,1)S(1)} %get-tuple-element.84.refs_2_), channel_id=1, source_target_pairs={{0,1},{1,0},{2,3},{3,2},{4,5},{5,4},{6,7},{7,6},{8,9},{9,8},{10,11... | collective-permute-start | bytes 602120 | tf_op jit(solution)/shard_map/ppermute | solution.py:370
  89.8 10.4 %collective-permute-start.22 = (bf16[128,896]{1,0:T(8,128)(2,1)S(1)}, bf16[128,896]{1,0:T(8,128)(2,1)S(1)}, u32[]{:S(2)}, u32[]{:S(2)}) collective-permute-start(bf16[128,896]{1,0:T(8,128)(2,1)S(1)} %get-tuple-element.74), channel_id=1, source_target_pairs={{0,4},{1,5},{4,8},{5,9},{8,12},{9,13},{12,14},{13,15},{14,10},{15,... | collective-permute-start | bytes 688136 | tf_op jit(solution)/shard_map/ppermute | solution.py:65
  93.2 4.8 %collective-permute-start.32 = (bf16[112,896]{1,0:T(8,128)(2,1)S(1)}, bf16[112,896]{1,0:T(8,128)(2,1)S(1)}, u32[]{:S(2)}, u32[]{:S(2)}) collective-permute-start(bf16[112,896]{1,0:T(8,128)(2,1)S(1)} %get-tuple-element.87.refs_5_), channel_id=1, source_target_pairs={{0,1},{1,0},{2,3},{3,2},{4,5},{5,4},{6,7},{7,6},{8,9},{9,8},{10,11... | collective-permute-start | bytes 602120 | tf_op jit(solution)/shard_map/ppermute | solution.py:370
  93.2 9.3 %collective-permute-start.23 = (bf16[128,896]{1,0:T(8,128)(2,1)S(1)}, bf16[128,896]{1,0:T(8,128)(2,1)S(1)}, u32[]{:S(2)}, u32[]{:S(2)}) collective-permute-start(bf16[128,896]{1,0:T(8,128)(2,1)S(1)} %get-tuple-element.76), channel_id=1, source_target_pairs={{0,2},{1,3},{4,0},{5,1},{8,4},{9,5},{12,8},{13,9},{14,12},{15,13},... | collective-permute-start | bytes 688136 | tf_op jit(solution)/shard_map/ppermute | solution.py:65
  95.5 6.5 %collective-permute-start.34 = (bf16[112,896]{1,0:T(8,128)(2,1)S(1)}, bf16[112,896]{1,0:T(8,128)(2,1)S(1)}, u32[]{:S(2)}, u32[]{:S(2)}) collective-permute-start(bf16[112,896]{1,0:T(8,128)(2,1)S(1)} %get-tuple-element.89.refs_7_), channel_id=1, source_target_pairs={{0,1},{1,0},{2,3},{3,2},{4,5},{5,4},{6,7},{7,6},{8,9},{9,8},{10,11... | collective-permute-start | bytes 602120 | tf_op jit(solution)/shard_map/ppermute | solution.py:370
  97.9 4.2 %collective-permute-start.35 = (bf16[112,896]{1,0:T(8,128)(2,1)S(1)}, bf16[112,896]{1,0:T(8,128)(2,1)S(1)}, u32[]{:S(2)}, u32[]{:S(2)}) collective-permute-start(bf16[112,896]{1,0:T(8,128)(2,1)S(1)} %get-tuple-element.90.refs_8_), channel_id=1, source_target_pairs={{0,1},{1,0},{2,3},{3,2},{4,5},{5,4},{6,7},{7,6},{8,9},{9,8},{10,11... | collective-permute-start | bytes 602120 | tf_op jit(solution)/shard_map/ppermute | solution.py:370
  98.0 8.1 %collective-permute-start.25 = (bf16[128,896]{1,0:T(8,128)(2,1)S(1)}, bf16[128,896]{1,0:T(8,128)(2,1)S(1)}, u32[]{:S(2)}, u32[]{:S(2)}) collective-permute-start(bf16[128,896]{1,0:T(8,128)(2,1)S(1)} %get-tuple-element.80), channel_id=1, source_target_pairs={{0,4},{1,5},{4,8},{5,9},{8,12},{9,13},{12,14},{13,15},{14,10},{15,... | collective-permute-start | bytes 688136 | tf_op jit(solution)/shard_map/ppermute | solution.py:65
  100.2 7.4 %collective-permute-start.26 = (bf16[128,896]{1,0:T(8,128)(2,1)S(1)}, bf16[128,896]{1,0:T(8,128)(2,1)S(1)}, u32[]{:S(2)}, u32[]{:S(2)}) collective-permute-start(bf16[128,896]{1,0:T(8,128)(2,1)S(1)} %get-tuple-element.81), channel_id=1, source_target_pairs={{0,2},{1,3},{4,0},{5,1},{8,4},{9,5},{12,8},{13,9},{14,12},{15,13},... | collective-permute-start | bytes 688136 | tf_op jit(solution)/shard_map/ppermute | solution.py:65
  102.0 5.7 %collective-permute-start.33 = (bf16[112,896]{1,0:T(8,128)(2,1)S(1)}, bf16[112,896]{1,0:T(8,128)(2,1)S(1)}, u32[]{:S(2)}, u32[]{:S(2)}) collective-permute-start(bf16[112,896]{1,0:T(8,128)(2,1)S(1)} %get-tuple-element.88.refs_6_), channel_id=1, source_target_pairs={{0,1},{1,0},{2,3},{3,2},{4,5},{5,4},{6,7},{7,6},{8,9},{9,8},{10,11... | collective-permute-start | bytes 602120 | tf_op jit(solution)/shard_map/ppermute | solution.py:370
  102.1 6.2 %collective-permute-start.36 = (bf16[112,896]{1,0:T(8,128)(2,1)S(1)}, bf16[112,896]{1,0:T(8,128)(2,1)S(1)}, u32[]{:S(2)}, u32[]{:S(2)}) collective-permute-start(bf16[112,896]{1,0:T(8,128)(2,1)S(1)} %get-tuple-element.91.refs_9_), channel_id=1, source_target_pairs={{0,1},{1,0},{2,3},{3,2},{4,5},{5,4},{6,7},{7,6},{8,9},{9,8},{10,11... | collective-permute-start | bytes 602120 | tf_op jit(solution)/shard_map/ppermute | solution.py:370
  102.6 5.8 %collective-permute-start.38 = (bf16[112,896]{1,0:T(8,128)(2,1)S(1)}, bf16[112,896]{1,0:T(8,128)(2,1)S(1)}, u32[]{:S(2)}, u32[]{:S(2)}) collective-permute-start(bf16[112,896]{1,0:T(8,128)(2,1)S(1)} %get-tuple-element.93.refs_11_), channel_id=1, source_target_pairs={{0,1},{1,0},{2,3},{3,2},{4,5},{5,4},{6,7},{7,6},{8,9},{9,8},{10,11... | collective-permute-start | bytes 602120 | tf_op jit(solution)/shard_map/ppermute | solution.py:370
  106.0 4.0 %collective-permute-start.41 = (bf16[128,896]{1,0:T(8,128)(2,1)S(1)}, bf16[128,896]{1,0:T(8,128)(2,1)S(1)}, u32[]{:S(2)}, u32[]{:S(2)}) collective-permute-start(bf16[128,896]{1,0:T(8,128)(2,1)S(1)} %collective-permute-done.25.refs_12_.refs_14_), channel_id=1, source_target_pairs={{0,1},{1,0},{2,3},{3,2},{4,5},{5,4},{6,7},{7,6},{8,9},{9,8},{10,11... | collective-permute-start | bytes 688136 | tf_op jit(solution)/shard_map/ppermute | solution.py:370
  107.6 2.4 %collective-permute-start.42 = (bf16[128,896]{1,0:T(8,128)(2,1)S(1)}, bf16[128,896]{1,0:T(8,128)(2,1)S(1)}, u32[]{:S(2)}, u32[]{:S(2)}) collective-permute-start(bf16[128,896]{1,0:T(8,128)(2,1)S(1)} %collective-permute-done.26.refs_13_.refs_15_), channel_id=1, source_target_pairs={{0,1},{1,0},{2,3},{3,2},{4,5},{5,4},{6,7},{7,6},{8,9},{9,8},{10,11... | collective-permute-start | bytes 688136 | tf_op jit(solution)/shard_map/ppermute | solution.py:370
  107.7 2.3 %collective-permute-start.39 = (bf16[112,896]{1,0:T(8,128)(2,1)S(1)}, bf16[112,896]{1,0:T(8,128)(2,1)S(1)}, u32[]{:S(2)}, u32[]{:S(2)}) collective-permute-start(bf16[112,896]{1,0:T(8,128)(2,1)S(1)} %get-tuple-element.94.refs_12_), channel_id=1, source_target_pairs={{0,1},{1,0},{2,3},{3,2},{4,5},{5,4},{6,7},{7,6},{8,9},{9,8},{10,11... | collective-permute-start | bytes 602120 | tf_op jit(solution)/shard_map/ppermute | solution.py:370
  108.2 1.7 %collective-permute-start.37 = (bf16[112,896]{1,0:T(8,128)(2,1)S(1)}, bf16[112,896]{1,0:T(8,128)(2,1)S(1)}, u32[]{:S(2)}, u32[]{:S(2)}) collective-permute-start(bf16[112,896]{1,0:T(8,128)(2,1)S(1)} %get-tuple-element.92.refs_10_), channel_id=1, source_target_pairs={{0,1},{1,0},{2,3},{3,2},{4,5},{5,4},{6,7},{7,6},{8,9},{9,8},{10,11... | collective-permute-start | bytes 602120 | tf_op jit(solution)/shard_map/ppermute | solution.py:370
  108.3 1.6 %collective-permute-start.40 = (bf16[112,896]{1,0:T(8,128)(2,1)S(1)}, bf16[112,896]{1,0:T(8,128)(2,1)S(1)}, u32[]{:S(2)}, u32[]{:S(2)}) collective-permute-start(bf16[112,896]{1,0:T(8,128)(2,1)S(1)} %get-tuple-element.95.refs_13_), channel_id=1, source_target_pairs={{0,1},{1,0},{2,3},{3,2},{4,5},{5,4},{6,7},{7,6},{8,9},{9,8},{10,11... | collective-permute-start | bytes 602120 | tf_op jit(solution)/shard_map/ppermute | solution.py:370
